TPU v7x, 32 devices: a whole 2x2x4 slice. The times are simulated.
32 devices in a mesh: ctx: 4 (over z), head: 2 (over y), seq: 4 (over x, core).
Axes of the slice: x: 2, y: 2, z: 4, core: 2. Of those that a mesh axis runs over, the one named last changes fastest.
Arguments:
- x_heads: bfloat16 [4, 16, 1024, 128], P('seq', 'head', 'ctx'), may hold values from -6 to 6
- target: bfloat16 [4, 16, 1024, 128], P('seq', 'head', 'ctx'), may hold values from -6 to 6
- b_proj: bfloat16 [4, 1024, 128], P('seq', 'ctx'), may hold values from -6 to 6
- c_proj: bfloat16 [4, 1024, 128], P('seq', 'ctx'), may hold values from -0.5 to 0.5
- dt_raw: float32 [4, 16, 1024], P('seq', 'head', 'ctx'), may hold values from -1.2 to 1.2
- a_log: float32 [16], P('head'), as said below
- skip_gain: float32 [16], P('head'), may hold values from 0.5 to 1.5
- dt_bias: float32 [16], P('head'), may hold values from -4.5 to -3.5
Outputs:
- grad_x: bfloat16 [4, 16, 1024, 128], P('seq', 'head', 'ctx')
- grad_b: float32 [4, 1024, 128], P('seq', ('ctx', 'head'))
- grad_c: float32 [4, 1024, 128], P('seq', ('ctx', 'head'))
- grad_dt_raw: float32 [4, 16, 1024], P('seq', 'head', 'ctx')
- grad_a_log: float32 [16], P('head')
- grad_skip: float32 [16], P('head')
- grad_dt_bias: float32 [16], P('head')
Inputs may be any that keep to these rules, and one draw needn't show every extreme that they name: exp(a_log) lies between 16 / 1024 and 3.
All inputs are finite; a program needn't handle non-finite values.
Results may differ from a plain program's by a relative error of at most 0.0054.
Values sent between devices are 32-bit elements; how exact they have to be, the bound alone decides.
No kernel may reach another device: no remote copies, remote signals or barrier semaphores. Data moves between devices by JAX's collectives and lax.ppermute only.
A program may use at most 64 MiB of HBM per device.

v0:
```python
import jax
import jax.numpy as jnp
from jax import lax
from jax.sharding import PartitionSpec as P

GROUP = 256


highest = lax.Precision.HIGHEST


def carried_in(part, axis, combine, identity, reverse):
    count = lax.axis_size(axis)
    place = lax.axis_index(axis)
    ahead = count - 1 - place if reverse else place
    gathered = jax.tree.map(lambda a: lax.all_gather(a, axis), part)
    state = jax.tree.map(lambda a, e: jnp.zeros_like(a) + jnp.asarray(e, a.dtype), part, identity)

    def one(turn, state):
        source = count - 1 - turn if reverse else turn
        return combine(
            state, jax.tree.map(lambda a: lax.dynamic_index_in_dim(a, source, 0, False), gathered)
        )

    return lax.fori_loop(0, ahead, one, state)


def block_logs(dt_block, decay_rate):
    return jnp.cumsum(-decay_rate[:, None] * dt_block, axis=-1)


def state_part(x_block, b_block, dt_block, log_decay):
    weights = jnp.exp(log_decay[:, -1:] - log_decay) * dt_block
    scaled = (x_block.astype(jnp.float32) * weights[:, :, None]).astype(jnp.bfloat16)
    contrib = jnp.einsum("hjp,jn->hpn", scaled, b_block, preferred_element_type=jnp.float32)
    return (weights, scaled, contrib, jnp.exp(log_decay[:, -1]))


def intra_parts(b_block, c_block, dt_block, log_decay):
    block_size = log_decay.shape[-1]
    row_ids = lax.broadcasted_iota(jnp.int32, (block_size, block_size), 0)
    column_ids = lax.broadcasted_iota(jnp.int32, (block_size, block_size), 1)
    causal = (row_ids >= column_ids)[None]
    log_gaps = log_decay[:, :, None] - log_decay[:, None, :]
    decays = jnp.where(causal, jnp.exp(jnp.where(causal, log_gaps, 0.0)), 0.0)
    scores = jnp.einsum("in,jn->ij", c_block, b_block, preferred_element_type=jnp.float32)
    mixing = (scores[None] * decays * dt_block[:, None, :]).astype(jnp.bfloat16)
    return (decays, scores, mixing)


def forward_block(x_block, t_block, c_block, log_decay, skip_gain, start_state, mixing):
    inner = jnp.einsum("hij,hjp->hip", mixing, x_block, preferred_element_type=jnp.float32)
    state_low = start_state.astype(jnp.bfloat16)
    growth = jnp.exp(log_decay)[:, :, None]
    carried = (
        jnp.einsum("in,hpn->hip", c_block, state_low, preferred_element_type=jnp.float32) * growth
    )
    out_error = (
        inner
        + carried
        + skip_gain[:, None, None] * x_block.astype(jnp.float32)
        - t_block.astype(jnp.float32)
    )
    error_weighted = (out_error * growth).astype(jnp.bfloat16)
    pulled = jnp.einsum("hip,in->hpn", error_weighted, c_block, preferred_element_type=jnp.float32)
    return (out_error, carried, error_weighted, state_low, pulled)


def backward_local(
    x_block,
    b_block,
    c_block,
    dt_block,
    skip_gain,
    out_error,
    carried,
    error_weighted,
    state_low,
    decays,
    scores,
    mixing,
):
    error_low = out_error.astype(jnp.bfloat16)
    grad_mixing = jnp.einsum("hip,hjp->hij", error_low, x_block, preferred_element_type=jnp.float32)
    grad_in = (
        jnp.einsum("hij,hip->hjp", mixing, error_low, preferred_element_type=jnp.float32)
        + skip_gain[:, None, None] * out_error
    )
    masked = grad_mixing * decays
    grad_score = (masked * dt_block[:, None, :]).astype(jnp.bfloat16)
    grad_c = jnp.einsum("hij,jn->in", grad_score, b_block, preferred_element_type=jnp.float32)
    grad_c = grad_c + jnp.einsum(
        "hip,hpn->in", error_weighted, state_low, preferred_element_type=jnp.float32
    )
    grad_b = jnp.einsum("hij,in->jn", grad_score, c_block, preferred_element_type=jnp.float32)
    product = masked * scores[None]
    column_sum = jnp.sum(product, axis=1)
    row_sum = jnp.einsum("hij,hj->hi", product, dt_block, precision=highest)
    grad_logs = row_sum - column_sum * dt_block + jnp.sum(out_error * carried, axis=-1)
    grad_skip = jnp.sum(out_error * x_block.astype(jnp.float32), axis=(1, 2))
    return (grad_in, grad_c, grad_b, column_sum, grad_logs, grad_skip)


def backward_state(x_block, b_block, log_decay, weights, scaled, start_state, end_adjoint):
    adjoint_low = end_adjoint.astype(jnp.bfloat16)
    grad_b = jnp.einsum("hjp,hpn->jn", scaled, adjoint_low, preferred_element_type=jnp.float32)
    grad_scaled = jnp.einsum(
        "jn,hpn->hjp", b_block, adjoint_low, preferred_element_type=jnp.float32
    )
    grad_in = grad_scaled * weights[:, :, None]
    grad_weight = jnp.sum(grad_scaled * x_block.astype(jnp.float32), axis=-1)
    grad_step = grad_weight * jnp.exp(log_decay[:, -1:] - log_decay)
    grad_logs = -grad_weight * weights
    grad_final = jnp.sum(grad_weight * weights, axis=-1) + jnp.exp(log_decay[:, -1]) * jnp.sum(
        end_adjoint * start_state, axis=(1, 2)
    )
    return (grad_in, grad_b, grad_step, grad_logs, grad_final)


def finish_block(
    column_sum, grad_logs_a, grad_step_b, grad_logs_b, grad_final, dt_block, decay_rate
):
    grad_logs = grad_logs_a + grad_logs_b
    grad_logs = grad_logs.at[:, -1].add(grad_final)
    grad_log_rate = jnp.flip(jnp.cumsum(jnp.flip(grad_logs, axis=-1), axis=-1), axis=-1)
    grad_step = column_sum + grad_step_b - decay_rate[:, None] * grad_log_rate
    grad_alog = -decay_rate * jnp.sum(grad_log_rate * dt_block, axis=-1)
    return (grad_step, grad_alog)


def combine_maps(earlier, later):
    return (earlier[0] * later[0], later[0][:, None, None] * earlier[1] + later[1])


def on_device(x_heads, target, b_proj, c_proj, dt_raw, a_log, skip_gain, dt_bias):
    inputs_all = x_heads[0]
    target_all = target[0]
    b_rows = b_proj[0]
    c_rows = c_proj[0]
    decay_rate = jnp.exp(a_log)
    step_sizes = jax.nn.softplus(dt_raw[0] + dt_bias[:, None])
    head_count, positions, head_size = inputs_all.shape
    state_size = b_rows.shape[-1]
    block_count = positions // GROUP
    identity = (
        jnp.ones((head_count,), jnp.float32),
        jnp.zeros((head_count, head_size, state_size), jnp.float32),
    )
    summary = identity
    x_block = inputs_all
    t_block = target_all
    b_block = b_rows
    c_block = c_rows
    dt_block = step_sizes
    log_decay = block_logs(dt_block, decay_rate)
    weights, scaled, contrib, decay_total = state_part(x_block, b_block, dt_block, log_decay)
    pieces = [
        (
            x_block,
            t_block,
            b_block,
            c_block,
            dt_block,
            log_decay,
            weights,
            scaled,
            contrib,
            decay_total,
        )
    ]
    summary = combine_maps(summary, (decay_total, contrib))
    incoming = carried_in(summary, "ctx", combine_maps, identity, False)
    carry_state = incoming[1]
    block_index = 0
    (
        x_block,
        t_block,
        b_block,
        c_block,
        dt_block,
        log_decay,
        weights,
        scaled,
        contrib,
        decay_total,
    ) = pieces[block_index]
    decays, scores, mixing = intra_parts(b_block, c_block, dt_block, log_decay)
    out_error, carried, error_weighted, state_low, pulled = forward_block(
        x_block, t_block, c_block, log_decay, skip_gain, carry_state, mixing
    )
    local_parts = None
    forwards = [
        (
            carry_state,
            pulled,
            out_error,
            carried,
            error_weighted,
            state_low,
            decays,
            scores,
            mixing,
            local_parts,
        )
    ]
    adjoint_summary = identity
    for block_index in reversed(range(block_count)):
        adjoint_summary = combine_maps(
            adjoint_summary, (pieces[block_index][9], forwards[block_index][1])
        )
    adjoint_in = carried_in(adjoint_summary, "ctx", combine_maps, identity, True)
    end_adjoint = adjoint_in[1]
    grad_inputs = [None] * block_count
    grad_steps = [None] * block_count
    b_sums = [None] * block_count
    c_sums = [None] * block_count
    alog_sum = jnp.zeros((head_count,), jnp.float32)
    skip_sum = jnp.zeros((head_count,), jnp.float32)
    for block_index in reversed(range(block_count)):
        (
            x_block,
            t_block,
            b_block,
            c_block,
            dt_block,
            log_decay,
            weights,
            scaled,
            contrib,
            decay_total,
        ) = pieces[block_index]
        (
            start_state,
            pulled,
            out_error,
            carried,
            error_weighted,
            state_low,
            decays,
            scores,
            mixing,
            local_parts,
        ) = forwards[block_index]
        grad_in_b, grad_b_b, grad_step_b, grad_logs_b, grad_final = backward_state(
            x_block, b_block, log_decay, weights, scaled, start_state, end_adjoint
        )
        grad_in_a, grad_c_block, grad_b_a, column_sum, grad_logs_a, grad_skip_block = (
            backward_local(
                x_block,
                b_block,
                c_block,
                dt_block,
                skip_gain,
                out_error,
                carried,
                error_weighted,
                state_low,
                decays,
                scores,
                mixing,
            )
        )
        b_sums[block_index] = grad_b_a + grad_b_b
        c_sums[block_index] = grad_c_block
        grad_step, grad_alog = finish_block(
            column_sum, grad_logs_a, grad_step_b, grad_logs_b, grad_final, dt_block, decay_rate
        )
        grad_inputs[block_index] = (grad_in_a + grad_in_b).astype(jnp.bfloat16)
        grad_steps[block_index] = grad_step
        alog_sum = grad_alog
        skip_sum = grad_skip_block
        end_adjoint = decay_total[:, None, None] * end_adjoint + pulled
    grad_b, grad_c = (
        lax.psum_scatter(b_sums[0][None], "head", scatter_dimension=1, tiled=True),
        lax.psum_scatter(c_sums[0][None], "head", scatter_dimension=1, tiled=True),
    )
    grad_x = grad_inputs[0][None]
    grad_step_all = grad_steps[0]
    grad_raw = grad_step_all * jax.nn.sigmoid(dt_raw[0] + dt_bias[:, None])
    bias_sum = jnp.sum(grad_raw, axis=1)
    alog_all, skip_all, bias_all = lax.psum((alog_sum, skip_sum, bias_sum), ("ctx", "seq"))
    token_total = positions * lax.axis_size("ctx") * x_heads.shape[0] * lax.axis_size("seq")
    grad_a_log = alog_all / token_total
    grad_skip = skip_all / (token_total * head_size)
    grad_dt_bias = bias_all / token_total
    return (grad_x, grad_b, grad_c, grad_raw[None], grad_a_log, grad_skip, grad_dt_bias)


def solution(mesh):
    return jax.shard_map(
        on_device,
        mesh=mesh,
        in_specs=(
            P("seq", "head", "ctx", None),
            P("seq", "head", "ctx", None),
            P("seq", "ctx", None),
            P("seq", "ctx", None),
            P("seq", "head", "ctx"),
            P("head"),
            P("head"),
            P("head"),
        ),
        out_specs=(
            P("seq", "head", "ctx", None),
            P("seq", ("ctx", "head"), None),
            P("seq", ("ctx", "head"), None),
            P("seq", "head", "ctx"),
            P("head"),
            P("head"),
            P("head"),
        ),
        check_vma=False,
    )
```

profile of v0, /device:TPU:0, one launch (start us, length us, event | category | flops | bytes accessed | tf_op | source)
XLA Modules:
  0.0 166.1 jit_solution(14458049370681441797)
XLA Ops:
  7.3 1.3 fusion.48
  8.5 0.8 fusion.38
  9.3 0.6 reduce-window.14
  9.9 0.2 slice_reduce_fusion.1
  10.2 0.2 slice_reduce_fusion.2
  10.4 1.4 fusion.42
  11.8 2.5 %convolution_add_fusion.3 = f32[8,128,128]{2,1,0:T(8,128)} fusion(bf16[1,8,256,128]{3,2,1,0:T(8,128)(2,1)} %param.14, f32[8,256]{1,0:T(8,128)S(1)} %get-tuple-element.209, f32[8]{0:T(128)S(1)} %exponential_multiply_fusion, bf16[1,256,128]{2,1,0:T(8,128)(2,1)S(1)} %copy-done), kind=kOutput, calls=%fused_computation.27 | convolution fusion | flops 68026368 | bytes 1122336 | tf_op jit(solution)/shard_map/hjp,jn->hpn/dot_general | solution.py:35
  14.4 0.2 copy.62
  14.6 0.6 dynamic-slice.8
  15.9 0.2 dynamic-update-slice.3
  16.1 13.6 %all-reduce = f32[32]{0:T(128)S(1)} all-reduce(f32[32]{0:T(128)S(1)} %dynamic-update-slice.3), channel_id=2, replica_groups=mesh['ctx'=4,'head'=2,'seq'=4] {'ctx'}, use_global_device_ids=true, to_apply=%add | all-reduce | flops 32 | bytes 256
  29.8 0.2 copy.64
  30.0 0.7 iota_compare_fusion
  30.7 0.2 fusion.34
  30.9 32.6 %all-gather.6.cloned.1.call-done = f32[32,128,128]{2,1,0:T(8,128)} async-done(((f32[8,128,128]{2,1,0:T(8,128)}), f32[32,128,128]{2,1,0:T(8,128)}) %all-gather.6.cloned.1.call-update) | async-done | bytes 2097168 | tf_op jit(solution)/shard_map/all_gather | solution.py:16
  63.5 0.3 fusion.6
  63.8 0.3 copy-done.15
  64.1 2.0 %fusion.5 = f32[8,256,128]{1,2,0:T(8,128)S(1)} fusion(f32[8,256,128]{1,2,0:T(8,128)S(1)} %fusion.6, f32[8,256]{1,0:T(8,128)} %get-tuple-element.210, f32[8,256]{1,0:T(8,128)} %copy-done.6, f32[256,256]{1,0:T(8,128)S(1)} %fusion.34, pred[256,256]{1,0:T(8,128)(4,1)} %iota_compare_fusion, bf16[1,8,256,128]{3,2,1,0:T(8,128)(2,1)S(1)} %copy-done.2, ...), kind=kOutput, calls=%fused_computation.21 | convolution fusion | flops 138936320 | bytes 4014112 | tf_op jit(solution)/shard_map/hij,hjp->hip/dot_general | solution.py:52
  66.2 1.1 convolution_add_fusion.2
  67.3 0.3 convolution_bitcast_fusion.1
  67.7 2.3 %multiply_reduce_fusion = (f32[8,256]{1,0:T(8,128)S(1)}, bf16[256,256]{1,0:T(8,128)(2,1)S(1)}, f32[8,256,256]{2,1,0:T(8,128)}) fusion(f32[256,256]{1,0:T(8,128)S(1)} %fusion.34, f32[8,256]{1,0:T(8,128)S(1)} %copy-done.5, f32[8,256]{1,0:T(8,128)S(1)} %copy-done.7, pred[256,256]{1,0:T(8,128)(4,1)S(1)} %copy-done.9, ...), kind=kOutput, calls=%fused_computation.11 | convolution fusion | flops 139655168 | bytes 4153344 | tf_op jit(solution)/shard_map/hip,hjp->hij/dot_general | solution.py:84
  70.0 0.8 fusion.9
  70.9 3.5 %fusion.1 = f32[8,1,256]{2,1,0:T(1,128)S(1)} fusion(f32[8,256,256]{2,1,0:T(8,128)} %get-tuple-element.218, f32[256,256]{1,0:T(8,128)S(1)} %fusion.34, f32[8,256,1]{1,0,2:T(8,128)S(1)} %bitcast.109), kind=kOutput, calls=%fused_computation.9 | convolution fusion | flops 6815744 | bytes 2375680 | tf_op jit(solution)/shard_map/hij,hj->hi/dot_general | solution.py:98
  74.4 41.3 %all-gather.8.cloned.1.call-done = f32[32,128,128]{2,1,0:T(8,128)} async-done(((f32[8,128,128]{2,1,0:T(8,128)}), f32[32,128,128]{2,1,0:T(8,128)}) %all-gather.8.cloned.1.call-update) | async-done | bytes 2097168 | tf_op jit(solution)/shard_map/all_gather | solution.py:16
  115.8 5.7 %while.28 = (s32[]{:T(128)}, f32[8,128,128]{2,1,0:T(8,128)S(1)}, s32[]{:T(128)}, f32[4,8]{1,0:T(4,128)}, f32[4,8,128,128]{3,2,1,0:T(8,128)}, /*index=5*/s32[]{:T(128)}, s32[]{:T(128)}, s32[]{:T(128)}, s32[]{:T(128)}) while((s32[]{:T(128)}, f32[8,128,128]{2,1,0:T(8,128)S(1)}, s32[]{:T(128)}, f32[4,8]{1,0:T(4,128)}, ...), condition=%wide.region_5.6_spmd, body=%wide.region_4.5_spmd.sunk | while | flops 262150 | bytes 1573115 | solution.py:25
  115.8 0.7 dynamic-slice_bitcast_fusion.5
  116.5 1.2 bitcast_add_fusion.7
  117.7 0.7 dynamic-slice_bitcast_fusion.5
  118.4 1.2 bitcast_add_fusion.7
  119.6 0.7 dynamic-slice_bitcast_fusion.5
  120.3 1.2 bitcast_add_fusion.7
  121.5 1.7 fusion.13
  123.1 0.3 convolution_bitcast_fusion.2
  123.5 0.2 multiply_reduce_fusion.2
  123.6 0.2 copy-done.17
  123.8 0.9 fusion.8
  124.7 0.1 multiply_reduce_fusion.4
  125.1 0.1 scatter-add.4
  125.1 0.2 rev.7
  125.3 0.6 reduce-window.16
  125.9 0.2 slice_reduce_fusion
  126.2 0.1 rev.8
  126.3 0.8 fusion.46
  127.1 0.9 fusion.10
  128.1 29.5 %all-reduce.1 = (f32[8]{0:T(128)S(1)}, f32[8]{0:T(128)S(1)}, f32[8]{0:T(128)S(1)}) all-reduce(f32[8]{0:T(128)S(1)} %negate_multiply_fusion, f32[8]{0:T(128)S(1)} %get-tuple-element.179, f32[8]{0:T(128)S(1)} %get-tuple-element.207), channel_id=1, replica_groups=mesh['ctx'=4,'head'=2,'seq'=4] {'ctx','seq'}, use_global_device_ids=true, to_apply=%region_17.18 | all-reduce | flops 24 | bytes 192 | tf_op jit(solution)/shard_map/psum | solution.py:281
  157.5 0.5 broadcast_multiply_fusion.2
  158.1 1.0 copy.74
  159.1 0.5 broadcast_multiply_fusion
  (64 shorter events, 1.0 us)
Async XLA Ops:
  7.2 4.6 %copy-start = (bf16[1,256,128]{2,1,0:T(8,128)(2,1)S(1)}, bf16[1,256,128]{2,1,0:T(8,128)(2,1)}, u32[]{:S(2)}) copy-start(bf16[1,256,128]{2,1,0:T(8,128)(2,1)} %param.16) | copy-start | bytes 196612
  7.2 7.4 %copy-start.19 = (u32[32]{0:T(128)S(1)}, u32[32]{0:T(128)}, u32[]{:S(2)}) copy-start(u32[32]{0:T(128)} %constant.111) | copy-start | bytes 388
  7.2 7.2 %copy-start.2 = (bf16[1,8,256,128]{3,2,1,0:T(8,128)(2,1)S(1)}, bf16[1,8,256,128]{3,2,1,0:T(8,128)(2,1)}, u32[]{:S(2)}) copy-start(bf16[1,8,256,128]{3,2,1,0:T(8,128)(2,1)} %param.14) | copy-start | bytes 1572868
  7.2 22.6 %copy-start.4 = (bf16[1,8,256,128]{3,2,1,0:T(8,128)(2,1)S(1)}, bf16[1,8,256,128]{3,2,1,0:T(8,128)(2,1)}, u32[]{:S(2)}) copy-start(bf16[1,8,256,128]{3,2,1,0:T(8,128)(2,1)} %param.15) | copy-start | bytes 1572868
  7.2 23.5 %copy-start.3 = (bf16[1,256,128]{2,1,0:T(8,128)(2,1)S(1)}, bf16[1,256,128]{2,1,0:T(8,128)(2,1)}, u32[]{:S(2)}) copy-start(bf16[1,256,128]{2,1,0:T(8,128)(2,1)} %param.17) | copy-start | bytes 196612
  7.2 56.2 %all-gather.6.cloned.1.call-start = ((), (), s32[]{:S(2)}) async-start(), calls=%async_computation.4 | async-start | bytes 2621440 | tf_op jit(solution)/shard_map/all_gather | solution.py:16
  10.2 19.8 %copy-start.6 = (f32[8,256]{1,0:T(8,128)}, f32[8,256]{1,0:T(8,128)S(1)}, u32[]{:S(2)}) copy-start(f32[8,256]{1,0:T(8,128)S(1)} %get-tuple-element.212) | copy-start | bytes 24580
  10.4 19.6 %copy-start.11 = (f32[8]{0:T(128)}, f32[8]{0:T(128)S(1)}, u32[]{:S(2)}) copy-start(f32[8]{0:T(128)S(1)} %get-tuple-element.182) | copy-start | bytes 100
  11.8 18.2 %copy-start.13 = (f32[8]{0:T(128)}, f32[8]{0:T(128)S(1)}, u32[]{:S(2)}) copy-start(f32[8]{0:T(128)S(1)} %exponential_multiply_fusion) | copy-start | bytes 100
  14.3 101.4 %all-gather.8.cloned.1.call-start = ((), (), s32[]{:S(2)}) async-start(), calls=%async_computation.5 | async-start | bytes 2621440 | tf_op jit(solution)/shard_map/all_gather | solution.py:16
  63.5 0.6 copy-start.15
  64.1 2.0 %copy-start.1 = (f32[8,256,128]{1,2,0:T(8,128)}, f32[8,256,128]{1,2,0:T(8,128)S(1)}, u32[]{:S(2)}) copy-start(f32[8,256,128]{1,2,0:T(8,128)S(1)} %fusion.6) | copy-start | bytes 3145732
  64.1 2.0 %copy-start.14 = (f32[8]{0:T(128)S(1)}, f32[8]{0:T(128)}, u32[]{:S(2)}) copy-start(f32[8]{0:T(128)} %copy-done.13) | copy-start | bytes 100
  66.1 1.6 copy-start.5
  66.1 1.6 copy-start.7
  66.2 1.6 copy-start.9
  67.3 92.3 %reduce-scatter.5.cloned.1.call-start = ((), (), s32[]{:S(2)}) async-start(), calls=%async_computation.3 | async-start | bytes 196608 | tf_op jit(solution)/shard_map/reduce_scatter | solution.py:275
  70.9 88.7 %reduce-scatter.3.cloned.1.call-start = ((), (), s32[]{:S(2)}) async-start(), calls=%async_computation.2 | async-start | bytes 196608 | tf_op jit(solution)/shard_map/reduce_scatter | solution.py:274
  123.1 0.7 copy-start.17
  123.8 2.5 %copy-start.8 = (f32[1,8,256]{2,1,0:T(8,128)S(1)}, f32[1,8,256]{2,1,0:T(8,128)}, u32[]{:S(2)}) copy-start(f32[1,8,256]{2,1,0:T(8,128)} %param.18) | copy-start | bytes 24580
  123.8 2.5 %copy-start.10 = (f32[8]{0:T(128)S(1)}, f32[8]{0:T(128)}, u32[]{:S(2)}) copy-start(f32[8]{0:T(128)} %param.21) | copy-start | bytes 100
  123.8 2.5 %copy-start.12 = (f32[8]{0:T(128)S(1)}, f32[8]{0:T(128)}, u32[]{:S(2)}) copy-start(f32[8]{0:T(128)} %copy-done.11) | copy-start | bytes 100
  123.8 2.5 %copy-start.16 = (f32[8]{0:T(128)S(1)}, f32[8]{0:T(128)}, u32[]{:S(2)}) copy-start(f32[8]{0:T(128)} %get-tuple-element.216) | copy-start | bytes 100
  123.8 4.2 %copy-start.18 = (f32[8]{0:T(128)S(1)}, f32[8]{0:T(128)}, u32[]{:S(2)}) copy-start(f32[8]{0:T(128)} %param.19) | copy-start | bytes 100
Sparse Core Ops, SparseCore 0:
  14.4 48.9 all-gather.5
  67.4 48.2 all-gather.7
  118.5 9.0 reduce-scatter.4
  130.2 10.2 reduce-scatter.2
where the time goes:
time: 167 us; the launch traced here: 166 us
  waiting for transfers between devices  74 us (44%)
  blocking collectives  43.1 us (26%)
  matrix products  16.8 us (10%)
  between operations  14.7 us (9%)
  other arithmetic  11.2 us (7%)
  local copies, waits for them, and re-layouts  6.05 us (4%)
    all_gather x2, waiting for transfers between devices, carried_in(): gathered = jax.tree.map(lambda a: lax.all_gather(a, axis), part)  73.9 us
    psum x1, blocking collectives, on_device(): lax.psum((alog_sum, skip_sum, bias_sum), ('ctx', 'seq'))  29.5 us
    unnamed x1, blocking collectives  13.6 us
    add x3, other arithmetic, combine_maps(): later[0][:, None, None] * earlier[1] + later[1]  3.55 us
    dot_general x1, matrix products, backward_local(): row_sum = jnp.einsum('hij,hj->hi', product, dt_block, precision=highest)  3.5 us
  transfers between devices with their start and end apart: 4, of which 2 were waited for; matrix products, arithmetic and copies ran while one was open for 14% of the time, Pallas kernels for 0%

commit v1 on v0

v1 whole, which is shorter than its diff:
```python
import functools
import jax
import jax.numpy as jnp
from jax import lax
from jax.experimental import pallas as pl
from jax.experimental.pallas import tpu as pltpu
from jax.sharding import PartitionSpec as P

CHUNKS = 2
f32, bf16 = jnp.float32, jnp.bfloat16
highest = lax.Precision.HIGHEST
VMEM = pl.BlockSpec(memory_space=pltpu.VMEM)
SMEM = pl.BlockSpec(memory_space=pltpu.SMEM)
LIMIT = 48 * 1024 * 1024


def dot(a, b):
    return jnp.dot(a, b, preferred_element_type=f32)


def dot_nt(a, b):
    return lax.dot_general(a, b, (((1,), (1,)), ((), ())), preferred_element_type=f32)


def call(body, outs, *args, flops=0):
    return pl.pallas_call(
        body,
        out_shape=outs,
        in_specs=[SMEM if a.ndim == 1 else VMEM for a in args],
        out_specs=jax.tree.map(lambda _: VMEM, outs),
        compiler_params=pltpu.CompilerParams(vmem_limit_bytes=LIMIT),
        cost_estimate=pl.CostEstimate(flops=flops, bytes_accessed=1 << 20, transcendentals=0),
    )(*args)


def head_row(values, width):
    lanes = lax.broadcasted_iota(jnp.int32, (1, width), 1)
    row = jnp.zeros((1, width), f32)
    for h in range(values.shape[0]):
        row = jnp.where(lanes == h, values[h], row)
    return row


def steps_of(raw, bias, rate, width):
    heads, size = raw.shape
    columns = jnp.concatenate([raw, jnp.zeros((width - heads, size), f32)], axis=0).T
    shifted = columns + bias
    dt = jnp.maximum(shifted, 0.0) + jnp.log1p(jnp.exp(-jnp.abs(shifted)))
    rows = lax.broadcasted_iota(jnp.int32, (size, size), 0)
    cols = lax.broadcasted_iota(jnp.int32, (size, size), 1)
    lower = jnp.where(rows >= cols, 1.0, 0.0).astype(f32)
    logs = jnp.dot(lower, -rate * dt, precision=highest, preferred_element_type=f32)
    return shifted, dt, logs, 0.5 * logs[size - 1 : size, :]


def masked_scores(b, c):
    size = b.shape[0]
    rows = lax.broadcasted_iota(jnp.int32, (size, size), 0)
    cols = lax.broadcasted_iota(jnp.int32, (size, size), 1)
    low = jnp.where(rows >= cols, dot_nt(c, b), 0.0).astype(bf16)
    low_t = jnp.where(cols >= rows, dot_nt(b, c), 0.0).astype(bf16)
    return low, low_t


def first_body(heads, width, x, t, b, c, raw, a_log, skip, dt_bias, f_out, p_out, pay_out, a_out):
    rate = head_row(a_log, width)
    rate = jnp.where(lax.broadcasted_iota(jnp.int32, rate.shape, 1) < a_log.shape[0], jnp.exp(rate), 0.0)
    _, dt, logs, mid = steps_of(raw[...], head_row(dt_bias, width), rate, width)
    grow = jnp.exp(logs - mid)
    shrink = dt * jnp.exp(mid - logs)
    half = jnp.exp(mid)
    low, _ = masked_scores(b[...], c[...])
    b_t, c_t = b[...].T, c[...].T
    first = lax.axis_index("ctx") == 0
    for k, h in enumerate(heads):
        xs = x[h].astype(f32)
        g, scale = grow[:, h : h + 1], half[:, h : h + 1]
        xr = (xs * shrink[:, h : h + 1]).astype(bf16)
        err = g * dot(low, xr) + skip[h] * xs - t[h].astype(f32)
        ew = (err * g).astype(bf16)
        contrib = scale * dot(b_t, xr)
        pulled = scale * dot(c_t, ew)
        f_out[k] = contrib
        p_out[k] = pulled
        pay_out[k] = jnp.where(first, contrib, pulled)
        a_out[k] = jnp.broadcast_to(scale * scale, a_out.shape[1:])


def maps_body(heads, width, reach, *refs):
    c, raw, a_log, dt_bias = refs[:4]
    later, (m_out, mc_out) = refs[4 : 4 + reach], refs[4 + reach :]
    rate = head_row(a_log, width)
    rate = jnp.where(lax.broadcasted_iota(jnp.int32, rate.shape, 1) < a_log.shape[0], jnp.exp(rate), 0.0)
    bias = head_row(dt_bias, width)
    size = c.shape[0]

    def squares(c_low, raw_rows):
        _, _, logs, mid = steps_of(raw_rows, bias, rate, width)
        return c_low, c_low.T.astype(f32), jnp.exp(2.0 * logs).T, jnp.exp(2.0 * mid)

    own = squares(c[...], raw[...])
    rest = []
    for ref in later:
        rows = ref[size:, :]
        per = size // rows.shape[1]
        raw_rows = jnp.concatenate(
            [rows[per * h : per * h + per, :].reshape(1, size) if per == 1 else
             jnp.concatenate([rows[per * h + s : per * h + s + 1, :] for s in range(per)], axis=1)
             for h in range(raw.shape[0])], axis=0)
        rest.append(squares(ref[:size, :].astype(bf16), raw_rows))
    for k, h in enumerate(heads):

        def one(item):
            c_low, c_t, grow2, _ = item
            return dot((c_t * grow2[h : h + 1, :]).astype(bf16), c_low)

        m_out[k] = one(own)
        total = jnp.zeros(mc_out.shape[1:], f32)
        factor = jnp.ones((1, 1), f32)
        for item in rest:
            total = total + factor * one(item)
            factor = factor * item[3][:, h : h + 1] * item[3][:, h : h + 1]
        mc_out[k] = total


def times(m, s):
    high = m.astype(bf16)
    low = (m - high.astype(f32)).astype(bf16)
    s_low = s.astype(bf16)
    return dot(high, s_low) + dot(low, s_low)


def round_body(n, r, f, p, m, mc, a, got, s_in, d_in, pay_out, s_out, d_out):
    place = lax.axis_index("ctx")
    came_up, came_down = place == r - 1, place == n - r
    for k in range(f.shape[0]):
        s = jnp.where(came_up, got[k], s_in[k])
        d = jnp.where(came_down, got[k], d_in[k])
        s_out[k] = s
        d_out[k] = d
        after = a[k] * s + f[k]
        full = p[k] + times(m[k], s) + a[k] * (d + times(mc[k], after))
        pay_out[k] = jnp.where(place == r - 1, after, full)


def last_body(heads, width, final, scales, *refs):
    (x, t, b, c, raw, a_log, skip, dt_bias, f, mc, a, got, s_in, d_in) = refs[:14]
    refs = refs[14:]
    if not final:
        gx_out, cols_out, gb_out, gc_out, sums_out, ew_s, xr_s, s_s, a_s = refs
        before = None
    else:
        before = refs[:5]
        gx_out, raw_out, keep_out, send_out, sums_out, ew_s, xr_s, s_s, a_s = refs[5:]
    n = lax.axis_size("ctx")
    place = lax.axis_index("ctx")
    count = a_log.shape[0]
    lanes = lax.broadcasted_iota(jnp.int32, (1, width), 1)
    rate = jnp.where(lanes < count, jnp.exp(head_row(a_log, width)), 0.0)
    shifted, dt, logs, mid = steps_of(raw[...], head_row(dt_bias, width), rate, width)
    grow = jnp.exp(logs - mid)
    shrink = dt * jnp.exp(mid - logs)
    half = jnp.exp(mid)
    low, low_t = masked_scores(b[...], c[...])
    size, state = b.shape
    channels = x.shape[2]
    if final:
        v_all, w_all = before[1][0], before[1][1]
        ends, skips = before[4][0:1, :], before[4][1:2, :]
        for h in range(heads[0]):
            gx_out[h] = before[0][h]
    else:
        v_all = w_all = jnp.zeros((size, width), f32)
        ends = skips = jnp.zeros((1, width), f32)
    for k, h in enumerate(heads):
        xs = x[h].astype(f32)
        g, r, scale = grow[:, h : h + 1], shrink[:, h : h + 1], half[:, h : h + 1]
        s = jnp.where(place == n - 1, got[k], s_in[k]) if n > 1 else s_in[k]
        d = jnp.where(place == 0, got[k], d_in[k]) if n > 1 else d_in[k]
        after = a[k] * s + f[k]
        adjoint = d + times(mc[k], after)
        s_low = (scale * s).astype(bf16)
        a_low = (scale * adjoint).astype(bf16)
        xr = (xs * r).astype(bf16)
        y = dot(low, xr) + dot(c[...], s_low)
        err = g * y + skip[h] * xs - t[h].astype(f32)
        ew = (err * g).astype(bf16)
        z = dot(low_t, ew) + dot(b[...], a_low)
        gx_out[h if final else k] = (r * z + skip[h] * err).astype(bf16)
        here = lanes == h
        v_all = jnp.where(here, jnp.sum(ew.astype(f32) * y, axis=1, keepdims=True), v_all)
        w_all = jnp.where(here, jnp.sum(xr.astype(f32) * z, axis=1, keepdims=True), w_all)
        ends = jnp.where(here, jnp.sum(adjoint * after, keepdims=True).reshape(1, 1), ends)
        skips = jnp.where(here, jnp.sum(err * xs, keepdims=True).reshape(1, 1), skips)
        span = pl.ds(k * channels, channels)
        ew_s[:, span] = ew
        xr_s[:, span] = xr
        s_s[:, span] = s_low
        a_s[:, span] = a_low
    rows = lax.broadcasted_iota(jnp.int32, (size, size), 0)
    cols = lax.broadcasted_iota(jnp.int32, (size, size), 1)
    score = jnp.where(rows >= cols, dot_nt(ew_s[...], xr_s[...]), 0.0).astype(bf16)
    score_t = jnp.where(cols >= rows, dot_nt(xr_s[...], ew_s[...]), 0.0).astype(bf16)
    grad_c = dot(score, b[...]) + dot_nt(ew_s[...], s_s[...])
    grad_b = dot(score_t, c[...]) + dot_nt(xr_s[...], a_s[...])
    if not final:
        cols_out[0] = v_all
        cols_out[1] = w_all
        gb_out[...] = grad_b
        gc_out[...] = grad_c
        sums_out[...] = jnp.concatenate([ends, skips, jnp.zeros((6, width), f32)], axis=0)
        return
    grad_b = grad_b + before[2][...]
    grad_c = grad_c + before[3][...]
    parts = lax.axis_size("head")
    if parts == 1:
        keep_out[0], keep_out[1] = grad_b, grad_c
        send_out[0], send_out[1] = grad_b, grad_c
    else:
        cut = size // 2
        upper = lax.axis_index("head") >= parts // 2
        for i, grad in enumerate((grad_b, grad_c)):
            keep_out[i] = jnp.where(upper, grad[cut:, :], grad[:cut, :])
            send_out[i] = jnp.where(upper, grad[:cut, :], grad[cut:, :])
    last = lax.broadcasted_iota(jnp.int32, (size, width), 0) == size - 1
    grad_logs = v_all - w_all + jnp.where(last, ends, 0.0)
    upper_ones = jnp.where(cols >= rows, 1.0, 0.0).astype(f32)
    log_rate = jnp.dot(upper_ones, grad_logs, precision=highest, preferred_element_type=f32)
    grad_raw = (w_all / dt - rate * log_rate) / (1.0 + jnp.exp(-shifted))
    raw_out[...] = grad_raw.T[:count, :]
    alog = -rate * jnp.sum(log_rate * dt, axis=0, keepdims=True)
    bias = jnp.sum(grad_raw, axis=0, keepdims=True)
    sums_out[...] = jnp.concatenate(
        [alog * scales[0], skips * scales[1], bias * scales[0], jnp.zeros((5, width), f32)], axis=0
    )


def on_device(x_heads, target, b_proj, c_proj, dt_raw, a_log, skip_gain, dt_bias):
    x, t, b, c, raw = x_heads[0], target[0], b_proj[0], c_proj[0], dt_raw[0]
    heads, size, channels = x.shape
    state = b.shape[1]
    width = state
    n, place = lax.axis_size("ctx"), lax.axis_index("ctx")
    shape = jax.ShapeDtypeStruct

    own = jnp.concatenate([c.astype(f32), raw.reshape(-1, state)], axis=0)
    lowest = max(n // 2 - 1, 0)
    later = [
        lax.ppermute(own, "ctx", [(i + s, i) for i in range(lowest, n - s)]) for s in range(1, n - lowest)
    ]

    chunks = CHUNKS if heads % CHUNKS == 0 else 1
    per = heads // chunks
    groups = [tuple(range(i * per, (i + 1) * per)) for i in range(chunks)]
    states = shape((per, channels, state), f32)
    held = []
    for group in groups:
        f, p, pay, a = call(
            functools.partial(first_body, group, width),
            (states, states, states, shape((per, 1, state), f32)),
            x, t, b, c, raw, a_log, skip_gain, dt_bias, flops=4 * 10**8,
        )
        held.append(dict(f=f, p=p, pay=pay, a=a, s=jnp.zeros(states.shape, f32), d=jnp.zeros(states.shape, f32)))
    for group, h in zip(groups, held):
        h["m"], h["mc"] = call(
            functools.partial(maps_body, group, width, len(later)), (states, states),
            c, raw, a_log, dt_bias, *later, flops=10**8,
        )

    def swap(r):
        pairs = [(r - 1, r), (r, r - 1)]
        other = [(n - r, n - 1 - r), (n - 1 - r, n - r)]
        return pairs if r - 1 == n - 1 - r else pairs + other

    for stage in range(1, n - 1 + chunks):
        for i, h in enumerate(held):
            r = stage - i
            if not 1 <= r <= n - 1:
                continue
            if r > 1:
                h["pay"], h["s"], h["d"] = call(
                    functools.partial(round_body, n, r), (states, states, states),
                    h["f"], h["p"], h["m"], h["mc"], h["a"], h["got"], h["s"], h["d"], flops=10**8,
                )
            h["got"] = lax.ppermute(h["pay"], "ctx", swap(r))

    tokens = size * n * x_heads.shape[0] * lax.axis_size("seq")
    scales = (1.0 / tokens, 1.0 / (tokens * channels))
    sums = shape((8, width), f32)
    before = ()
    for i, (group, h) in enumerate(zip(groups, held)):
        final = i == chunks - 1
        got = h.get("got", h["s"])
        grads = shape((size, state), f32)
        cut = size if lax.axis_size("head") == 1 else size // 2
        if final:
            outs = (shape(x.shape, bf16), shape(raw.shape, f32), shape((2, cut, state), f32), shape((2, cut, state), f32), sums)
        else:
            outs = (shape((heads // chunks * (i + 1), size, channels), bf16), shape((2, size, width), f32), grads, grads, sums)
        args = (x, t, b, c, raw, a_log, skip_gain, dt_bias, h["f"], h["mc"], h["a"], got, h["s"], h["d"]) + before
        before = pl.pallas_call(
            functools.partial(last_body, group, width, final, scales),
            out_shape=outs,
            in_specs=[SMEM if v.ndim == 1 else VMEM for v in args],
            out_specs=[VMEM] * len(outs),
            scratch_shapes=[pltpu.VMEM((size, per * channels), bf16)] * 2 + [pltpu.VMEM((state, per * channels), bf16)] * 2,
            compiler_params=pltpu.CompilerParams(vmem_limit_bytes=LIMIT),
            cost_estimate=pl.CostEstimate(flops=4 * 10**8, bytes_accessed=1 << 20, transcendentals=0),
        )(*args)
    grad_x, grad_raw, keep, send, total = before

    parts = lax.axis_size("head")
    step = parts // 2
    while step >= 1:
        keep = keep + lax.ppermute(send, "head", [(i, i ^ step) for i in range(parts)])
        step //= 2
        if step >= 1:
            cut = keep.shape[1] // 2
            upper = (lax.axis_index("head") // step) % 2 == 1
            keep, send = (
                jnp.where(upper, keep[:, cut:], keep[:, :cut]),
                jnp.where(upper, keep[:, :cut], keep[:, cut:]),
            )
    for axis in ("seq", "ctx"):
        step = 1
        while step < lax.axis_size(axis):
            total = total + lax.ppermute(total, axis, [(i, i ^ step) for i in range(lax.axis_size(axis))])
            step *= 2
    return (
        grad_x[None], keep[0][None], keep[1][None], grad_raw[None],
        total[0, :heads], total[1, :heads], total[2, :heads],
    )


def solution(mesh):
    return jax.shard_map(
        on_device,
        mesh=mesh,
        in_specs=(
            P("seq", "head", "ctx", None),
            P("seq", "head", "ctx", None),
            P("seq", "ctx", None),
            P("seq", "ctx", None),
            P("seq", "head", "ctx"),
            P("head"),
            P("head"),
            P("head"),
        ),
        out_specs=(
            P("seq", "head", "ctx", None),
            P("seq", ("ctx", "head"), None),
            P("seq", ("ctx", "head"), None),
            P("seq", "head", "ctx"),
            P("head"),
            P("head"),
            P("head"),
        ),
        check_vma=False,
    )
```

time: 167 us -> 75.6 us (0.45)
  waiting for transfers between devices: 74 us -> 11.3 us
  blocking collectives: 43.1 us -> 0 us
  starting transfers between devices: 0.16 us -> 39 us
  Pallas kernels: 0 us -> 17.7 us
  matrix products: 16.8 us -> 0 us
  between operations: 14.7 us -> 0.85 us
  other arithmetic: 11.2 us -> 0.06 us
    all_gather x2 -> x0, waiting for transfers between devices: 73.9 us -> none  [carried_in(): gathered = jax.tree.map(lambda a: lax.all_gather(a, axis), part)]
    ppermute x0 -> x13, starting transfers between devices: none -> 39 us  [the longest x6 29 us: on_device(): h['got'] = lax.ppermute(h['pay'], 'ctx', swap(r))]
    psum x1 -> x0, blocking collectives: 29.5 us -> none  [on_device(): lax.psum((alog_sum, skip_sum, bias_sum), ('ctx', 'seq'))]
    pallas_call x0 -> x10, Pallas kernels: none -> 17.7 us  [the longest x8 10.3 us: call(): pl.pallas_call(body, out_shape=outs, in_specs=[SMEM if a.ndim == 1 else V...]
    dot_general x13 -> x0, matrix products: 16.8 us -> none  [the longest x1 3.5 us: backward_local(): row_sum = jnp.einsum('hij,hj->hi', product, dt_block, precision=highest)]
    unnamed x1 -> x0, blocking collectives: 13.6 us -> none
    ppermute x0 -> x13, waiting for transfers between devices: none -> 11.3 us  [the longest x4 5.05 us: on_device(): lax.ppermute(total, axis, [(i, i ^ step) for i in range(lax.axis_size(axi...]
    add x4 -> x5, other arithmetic: 3.63 us -> 0.03 us  [the longest x1 0.02 us: on_device(): keep + lax.ppermute(send, 'head', [(i, i ^ step) for i in range(parts)])]
  transfers between devices with their start and end apart: 4 -> 13, of which waited for: 2 -> 8; matrix products, arithmetic and copies ran while one was open for 14% -> 1% of each run, Pallas kernels for 0% -> 15%
where the time goes in v1:
time: 75.6 us; the launch traced here: 75.1 us
  starting transfers between devices  39 us (52%)
  Pallas kernels  17.7 us (23%)
  waiting for transfers between devices  11.3 us (15%)
  local copies, waits for them, and re-layouts  6.32 us (8%)
  between operations  0.85 us (1%)
    ppermute x6, starting transfers between devices, on_device(): h['got'] = lax.ppermute(h['pay'], 'ctx', swap(r))  29 us
    pallas_call x8, Pallas kernels, call(): pl.pallas_call(body, out_shape=outs, in_specs=[SMEM if a.ndim == 1 else V...  10.3 us
    pallas_call x2, Pallas kernels, on_device(): pl.pallas_call(functools.partial(last_body, group, width, final, scales),...  7.32 us
    ppermute x4, starting transfers between devices, on_device(): lax.ppermute(total, axis, [(i, i ^ step) for i in range(lax.axis_size(axi...  7.16 us
    unnamed x26, local copies, waits for them, and re-layouts  5.12 us
    ppermute x4, waiting for transfers between devices, on_device(): lax.ppermute(total, axis, [(i, i ^ step) for i in range(lax.axis_size(axi...  5.05 us
    ppermute x6, waiting for transfers between devices, on_device(): h['got'] = lax.ppermute(h['pay'], 'ctx', swap(r))  3.36 us
    ppermute x1, waiting for transfers between devices, on_device(): lax.ppermute(send, 'head', [(i, i ^ step) for i in range(parts)])  2.85 us
  transfers between devices with their start and end apart: 13, of which 8 were waited for; matrix products, arithmetic and copies ran while one was open for 1% of the time, Pallas kernels for 15%

profile of v1, /device:TPU:0, one launch (start us, length us, event | category | flops | bytes accessed | tf_op | source)
XLA Modules:
  0.0 75.1 jit_solution(5194156843088771670)
XLA Ops:
  0.6 0.0 copy-start.8
  0.6 0.0 copy-start.9
  0.7 0.7 copy-done.8
  1.3 1.0 %copy-done = bf16[1,8,256,128]{3,2,1,0:T(8,128)(2,1)S(1)} copy-done((bf16[1,8,256,128]{3,2,1,0:T(8,128)(2,1)S(1)}, bf16[1,8,256,128]{3,2,1,0:T(8,128)(2,1)}, u32[]{:S(2)}) %copy-start) | copy-done | bytes 524312
  2.4 1.0 %copy-done.2 = bf16[1,8,256,128]{3,2,1,0:T(8,128)(2,1)S(1)} copy-done((bf16[1,8,256,128]{3,2,1,0:T(8,128)(2,1)S(1)}, bf16[1,8,256,128]{3,2,1,0:T(8,128)(2,1)}, u32[]{:S(2)}) %copy-start.2) | copy-done | bytes 524312
  3.4 0.8 %copy-done.4 = bf16[1,256,128]{2,1,0:T(8,128)(2,1)S(1)} copy-done((bf16[1,256,128]{2,1,0:T(8,128)(2,1)S(1)}, bf16[1,256,128]{2,1,0:T(8,128)(2,1)}, u32[]{:S(2)}) %copy-start.4) | copy-done | bytes 65560
  4.3 0.8 %copy-done.6 = bf16[1,256,128]{2,1,0:T(8,128)(2,1)S(1)} copy-done((bf16[1,256,128]{2,1,0:T(8,128)(2,1)S(1)}, bf16[1,256,128]{2,1,0:T(8,128)(2,1)}, u32[]{:S(2)}) %copy-start.6) | copy-done | bytes 65560
  5.1 0.7 copy-done.11
  5.8 2.3 %shard_map.139 = (f32[4,128,128]{2,1,0:T(8,128)S(1)}, f32[4,128,128]{2,1,0:T(8,128)S(1)}, f32[4,128,128]{2,1,0:T(8,128)S(1)}, f32[4,1,128]{2,1,0:T(1,128)S(1)}) custom-call(bf16[8,256,128]{2,1,0:T(8,128)(2,1)S(1)} %bitcast.14, bf16[8,256,128]{2,1,0:T(8,128)(2,1)S(1)} %bitcast.18, bf16[256,128]{1,0:T(8,128)(2,1)S(1)} %bitcast.28, ...), custom_call_target="tpu_custom_call" | custom-call | flops 400000000 | bytes 1048576 | tf_op jit(solution)/shard_map/pallas_call | solution.py:26
  8.1 0.0 copy-start.12
  8.1 0.0 copy-start.5
  8.1 3.1 %collective-permute-start.5 = (f32[4,128,128]{2,1,0:T(8,128)S(1)}, f32[4,128,128]{2,1,0:T(8,128)S(1)}, u32[]{:S(2)}, u32[]{:S(2)}) collective-permute-start(f32[4,128,128]{2,1,0:T(8,128)S(1)} %get-tuple-element.58), channel_id=1, source_target_pairs={{0,8},{8,0},{24,16},{16,24},{1,9},{9,1},{25,17},{17,25},{2,10},{10... | collective-permute-start | bytes 786440 | tf_op jit(solution)/shard_map/ppermute | solution.py:285
  11.2 2.3 %shard_map.135 = (f32[4,128,128]{2,1,0:T(8,128)S(1)}, f32[4,128,128]{2,1,0:T(8,128)S(1)}, f32[4,128,128]{2,1,0:T(8,128)S(1)}, f32[4,1,128]{2,1,0:T(1,128)S(1)}) custom-call(bf16[8,256,128]{2,1,0:T(8,128)(2,1)S(1)} %bitcast.15, bf16[8,256,128]{2,1,0:T(8,128)(2,1)S(1)} %bitcast.19, bf16[256,128]{1,0:T(8,128)(2,1)S(1)} %bitcast.29, ...), custom_call_target="tpu_custom_call" | custom-call | flops 400000000 | bytes 1048576 | tf_op jit(solution)/shard_map/pallas_call | solution.py:26
  13.5 0.6 collective-permute-start.2
  14.1 0.7 collective-permute-start.1
  14.8 0.7 collective-permute-start
  15.5 0.0 collective-permute-done.1.refs_5_
  15.5 0.0 collective-permute-done.refs_4_
  15.5 2.2 %shard_map.140 = (f32[4,128,128]{2,1,0:T(8,128)S(1)}, f32[4,128,128]{2,1,0:T(8,128)S(1)}) custom-call(bf16[256,128]{1,0:T(8,128)(2,1)S(1)} %bitcast.24, f32[8,256]{1,0:T(8,128)S(1)} %bitcast.34, f32[8]{0:T(128)S(1)} %copy-done.9, f32[8]{0:T(128)S(1)} %copy-done.12, f32[272,128]{1,0:T(8,128)S(1)} %collective-permute-done.refs_4_, ...), custom_call_target="tpu_custom_call" | custom-call | flops 100000000 | bytes 1048576 | tf_op jit(solution)/shard_map/pallas_call | solution.py:26
  17.8 0.5 collective-permute-done.5.got
  18.3 0.3 shard_map.141
  18.7 0.7 collective-permute-start.6
  19.3 2.2 %shard_map.136 = (f32[4,128,128]{2,1,0:T(8,128)S(1)}, f32[4,128,128]{2,1,0:T(8,128)S(1)}) custom-call(bf16[256,128]{1,0:T(8,128)(2,1)S(1)} %bitcast.25, f32[8,256]{1,0:T(8,128)S(1)} %bitcast.35, f32[8]{0:T(128)S(1)} %copy-done.9, f32[8]{0:T(128)S(1)} %copy-done.12, f32[272,128]{1,0:T(8,128)S(1)} %collective-permute-done.refs_4_, ...), custom_call_target="tpu_custom_call" | custom-call | flops 100000000 | bytes 1048576 | tf_op jit(solution)/shard_map/pallas_call | solution.py:26
  21.6 1.5 %collective-permute-done.2.got = f32[4,128,128]{2,1,0:T(8,128)S(1)} collective-permute-done((f32[4,128,128]{2,1,0:T(8,128)S(1)}, f32[4,128,128]{2,1,0:T(8,128)S(1)}, u32[]{:S(2)}, u32[]{:S(2)}) %collective-permute-start.2) | collective-permute-done | bytes 262176 | tf_op jit(solution)/shard_map/ppermute | solution.py:285
  23.1 0.3 shard_map.137
  23.4 0.9 %collective-permute-start.3 = (f32[4,128,128]{2,1,0:T(8,128)S(1)}, f32[4,128,128]{2,1,0:T(8,128)S(1)}, u32[]{:S(2)}, u32[]{:S(2)}) collective-permute-start(f32[4,128,128]{2,1,0:T(8,128)S(1)} %get-tuple-element.47), channel_id=1, source_target_pairs={{8,16},{16,8},{9,17},{17,9},{10,18},{18,10},{11,19},{19,11},{12,20... | collective-permute-start | bytes 786440 | tf_op jit(solution)/shard_map/ppermute | solution.py:285
  24.3 0.0 collective-permute-done.6.got
  24.3 0.3 shard_map.142
  24.6 18.4 %collective-permute-start.7 = (f32[4,128,128]{2,1,0:T(8,128)S(1)}, f32[4,128,128]{2,1,0:T(8,128)S(1)}, u32[]{:S(2)}, u32[]{:S(2)}) collective-permute-start(f32[4,128,128]{2,1,0:T(8,128)S(1)} %get-tuple-element.62), channel_id=1, source_target_pairs={{16,24},{24,16},{8,0},{0,8},{17,25},{25,17},{9,1},{1,9},{18,26},{2... | collective-permute-start | bytes 786440 | tf_op jit(solution)/shard_map/ppermute | solution.py:285
  43.0 0.0 collective-permute-done.3.got
  43.0 0.3 shard_map.138
  43.3 5.3 %collective-permute-start.4 = (f32[4,128,128]{2,1,0:T(8,128)S(1)}, f32[4,128,128]{2,1,0:T(8,128)S(1)}, u32[]{:S(2)}, u32[]{:S(2)}) collective-permute-start(f32[4,128,128]{2,1,0:T(8,128)S(1)} %get-tuple-element.50), channel_id=1, source_target_pairs={{16,24},{24,16},{8,0},{0,8},{17,25},{25,17},{9,1},{1,9},{18,26},{2... | collective-permute-start | bytes 786440 | tf_op jit(solution)/shard_map/ppermute | solution.py:285
  48.7 0.0 collective-permute-done.7.refs_11_
  48.7 3.1 %shard_map.143 = (bf16[4,256,128]{2,1,0:T(8,128)(2,1)S(1)}, f32[2,256,128]{2,1,0:T(8,128)S(1)}, f32[256,128]{1,0:T(8,128)S(1)}, f32[256,128]{1,0:T(8,128)S(1)}, f32[8,128]{1,0:T(8,128)S(1)}) custom-call(bf16[8,256,128]{2,1,0:T(8,128)(2,1)S(1)} %bitcast.16, bf16[8,256,128]{2,1,0:T(8,128)(2,1)S(1)} %bitcast.20, bf16[256,128]{1,0:T(8,128)(2,1)S(1)} %bitcast.30, ...), custom_call_target="tpu_custom_call" | custom-call | flops 400000000 | bytes 1048576 | tf_op jit(solution)/shard_map/pallas_call | solution.py:301
  51.8 1.3 %collective-permute-done.4.refs_11_ = f32[4,128,128]{2,1,0:T(8,128)S(1)} collective-permute-done((f32[4,128,128]{2,1,0:T(8,128)S(1)}, f32[4,128,128]{2,1,0:T(8,128)S(1)}, u32[]{:S(2)}, u32[]{:S(2)}) %collective-permute-start.4) | collective-permute-done | bytes 262176 | tf_op jit(solution)/shard_map/ppermute | solution.py:285
  53.1 4.2 %shard_map.144 = (bf16[8,256,128]{2,1,0:T(8,128)(2,1)}, f32[8,256]{1,0:T(8,128)}, f32[2,128,128]{2,1,0:T(8,128)S(1)}, f32[2,128,128]{2,1,0:T(8,128)S(1)}, f32[8,128]{1,0:T(8,128)S(1)}) custom-call(bf16[8,256,128]{2,1,0:T(8,128)(2,1)S(1)} %bitcast.17, bf16[8,256,128]{2,1,0:T(8,128)(2,1)S(1)} %bitcast.21, bf16[256,128]{1,0:T(8,128)(2,1)S(1)} %bitcast.31, ...), custom_call_target="tpu_custom_call" | custom-call | flops 400000000 | bytes 1048576 | tf_op jit(solution)/shard_map/pallas_call | solution.py:301
  57.3 0.0 collective-permute-start.9
  57.3 1.2 %collective-permute-done.9 = f32[8,128]{1,0:T(8,128)S(1)} collective-permute-done((f32[8,128]{1,0:T(8,128)S(1)}, f32[8,128]{1,0:T(8,128)S(1)}, u32[]{:S(2)}, u32[]{:S(2)}) %collective-permute-start.9) | collective-permute-done | bytes 4128 | tf_op jit(solution)/shard_map/ppermute | solution.py:327
  58.5 1.5 %collective-permute-start.10 = (f32[8,128]{1,0:T(8,128)S(1)}, f32[8,128]{1,0:T(8,128)S(1)}, u32[]{:S(2)}, u32[]{:S(2)}) collective-permute-start(f32[8,128]{1,0:T(8,128)S(1)} %add.16), channel_id=1, source_target_pairs={{0,2},{1,3},{2,0},{3,1},{4,6},{5,7},{6,4},{7,5},{8,10},{9,11},{10,... | collective-permute-start | bytes 12296 | tf_op jit(solution)/shard_map/ppermute | solution.py:327
  60.0 2.1 %collective-permute-done.10 = f32[8,128]{1,0:T(8,128)S(1)} collective-permute-done((f32[8,128]{1,0:T(8,128)S(1)}, f32[8,128]{1,0:T(8,128)S(1)}, u32[]{:S(2)}, u32[]{:S(2)}) %collective-permute-start.10) | collective-permute-done | bytes 4128 | tf_op jit(solution)/shard_map/ppermute | solution.py:327
  62.1 1.9 %collective-permute-start.11 = (f32[8,128]{1,0:T(8,128)S(1)}, f32[8,128]{1,0:T(8,128)S(1)}, u32[]{:S(2)}, u32[]{:S(2)}) collective-permute-start(f32[8,128]{1,0:T(8,128)S(1)} %add.17), channel_id=1, source_target_pairs={{0,8},{8,0},{16,24},{24,16},{1,9},{9,1},{17,25},{25,17},{2,10},{10... | collective-permute-start | bytes 12296 | tf_op jit(solution)/shard_map/ppermute | solution.py:327
  64.0 1.7 %collective-permute-done.11 = f32[8,128]{1,0:T(8,128)S(1)} collective-permute-done((f32[8,128]{1,0:T(8,128)S(1)}, f32[8,128]{1,0:T(8,128)S(1)}, u32[]{:S(2)}, u32[]{:S(2)}) %collective-permute-start.11) | collective-permute-done | bytes 4128 | tf_op jit(solution)/shard_map/ppermute | solution.py:327
  65.7 3.8 %collective-permute-start.12 = (f32[8,128]{1,0:T(8,128)S(1)}, f32[8,128]{1,0:T(8,128)S(1)}, u32[]{:S(2)}, u32[]{:S(2)}) collective-permute-start(f32[8,128]{1,0:T(8,128)S(1)} %add.18), channel_id=1, source_target_pairs={{0,16},{8,24},{16,0},{24,8},{1,17},{9,25},{17,1},{25,9},{2,18},{10... | collective-permute-start | bytes 12296 | tf_op jit(solution)/shard_map/ppermute | solution.py:327
  69.5 1.5 %collective-permute-start.8 = (f32[2,128,128]{2,1,0:T(8,128)S(1)}, f32[2,128,128]{2,1,0:T(8,128)S(1)}, u32[]{:S(2)}, u32[]{:S(2)}) collective-permute-start(f32[2,128,128]{2,1,0:T(8,128)S(1)} %get-tuple-element.72), channel_id=1, source_target_pairs={{0,4},{4,0},{1,5},{5,1},{2,6},{6,2},{3,7},{7,3},{8,12},{12,8},{9,1... | collective-permute-start | bytes 393224 | tf_op jit(solution)/shard_map/ppermute | solution.py:315
  71.0 0.1 collective-permute-done.12
  71.1 0.5 slice_bitcast_fusion
  71.6 2.9 %collective-permute-done.8 = f32[2,128,128]{2,1,0:T(8,128)S(1)} collective-permute-done((f32[2,128,128]{2,1,0:T(8,128)S(1)}, f32[2,128,128]{2,1,0:T(8,128)S(1)}, u32[]{:S(2)}, u32[]{:S(2)}) %collective-permute-start.8) | collective-permute-done | bytes 131104 | tf_op jit(solution)/shard_map/ppermute | solution.py:315
  74.5 0.7 fusion
  (25 shorter events, 0.1 us)
Async XLA Ops:
  0.6 0.7 copy-start.8
  0.6 0.7 copy-start.9
  0.7 0.7 copy-start.10
  1.3 1.0 %copy-start = (bf16[1,8,256,128]{3,2,1,0:T(8,128)(2,1)S(1)}, bf16[1,8,256,128]{3,2,1,0:T(8,128)(2,1)}, u32[]{:S(2)}) copy-start(bf16[1,8,256,128]{3,2,1,0:T(8,128)(2,1)} %param.8) | copy-start | bytes 1572868
  2.4 1.0 %copy-start.2 = (bf16[1,8,256,128]{3,2,1,0:T(8,128)(2,1)S(1)}, bf16[1,8,256,128]{3,2,1,0:T(8,128)(2,1)}, u32[]{:S(2)}) copy-start(bf16[1,8,256,128]{3,2,1,0:T(8,128)(2,1)} %param.9) | copy-start | bytes 1572868
  3.4 0.8 %copy-start.4 = (bf16[1,256,128]{2,1,0:T(8,128)(2,1)S(1)}, bf16[1,256,128]{2,1,0:T(8,128)(2,1)}, u32[]{:S(2)}) copy-start(bf16[1,256,128]{2,1,0:T(8,128)(2,1)} %param.11) | copy-start | bytes 196612
  4.3 0.8 %copy-start.6 = (bf16[1,256,128]{2,1,0:T(8,128)(2,1)S(1)}, bf16[1,256,128]{2,1,0:T(8,128)(2,1)}, u32[]{:S(2)}) copy-start(bf16[1,256,128]{2,1,0:T(8,128)(2,1)} %param.10) | copy-start | bytes 196612
  5.1 0.7 copy-start.11
  8.1 3.1 %copy-start.12 = (f32[8]{0:T(128)S(1)}, f32[8]{0:T(128)}, u32[]{:S(2)}) copy-start(f32[8]{0:T(128)} %refs_7_.3) | copy-start | bytes 100
  8.1 6.0 %copy-start.5 = (bf16[1,256,128]{2,1,0:T(8,128)(2,1)S(1)}, bf16[1,256,128]{2,1,0:T(8,128)(2,1)}, u32[]{:S(2)}) copy-start(bf16[1,256,128]{2,1,0:T(8,128)(2,1)} %param.11) | copy-start | bytes 196612
  8.1 10.2 %collective-permute-start.5 = (f32[4,128,128]{2,1,0:T(8,128)S(1)}, f32[4,128,128]{2,1,0:T(8,128)S(1)}, u32[]{:S(2)}, u32[]{:S(2)}) collective-permute-start(f32[4,128,128]{2,1,0:T(8,128)S(1)} %get-tuple-element.58), channel_id=1, source_target_pairs={{0,8},{8,0},{24,16},{16,24},{1,9},{9,1},{25,17},{17,25},{2,10},{10... | collective-permute-start | bytes 786440 | tf_op jit(solution)/shard_map/ppermute | solution.py:285
  13.5 9.6 %collective-permute-start.2 = (f32[4,128,128]{2,1,0:T(8,128)S(1)}, f32[4,128,128]{2,1,0:T(8,128)S(1)}, u32[]{:S(2)}, u32[]{:S(2)}) collective-permute-start(f32[4,128,128]{2,1,0:T(8,128)S(1)} %get-tuple-element.46), channel_id=1, source_target_pairs={{0,8},{8,0},{24,16},{16,24},{1,9},{9,1},{25,17},{17,25},{2,10},{10... | collective-permute-start | bytes 786440 | tf_op jit(solution)/shard_map/ppermute | solution.py:285
  14.1 1.4 %collective-permute-start.1 = (f32[272,128]{1,0:T(8,128)S(1)}, f32[272,128]{1,0:T(8,128)S(1)}, u32[]{:S(2)}, u32[]{:S(2)}) collective-permute-start(f32[272,128]{1,0:T(8,128)S(1)} %pad_maximum_fusion), channel_id=1, source_target_pairs={{24,8},{25,9},{26,10},{27,11},{28,12},{29,13},{30,14},{31,15}} | collective-permute-start | bytes 417800 | tf_op jit(solution)/shard_map/ppermute | solution.py:249
  14.8 0.7 collective-permute-start
  18.7 5.6 %collective-permute-start.6 = (f32[4,128,128]{2,1,0:T(8,128)S(1)}, f32[4,128,128]{2,1,0:T(8,128)S(1)}, u32[]{:S(2)}, u32[]{:S(2)}) collective-permute-start(f32[4,128,128]{2,1,0:T(8,128)S(1)} %get-tuple-element.59), channel_id=1, source_target_pairs={{8,16},{16,8},{9,17},{17,9},{10,18},{18,10},{11,19},{19,11},{12,20... | collective-permute-start | bytes 786440 | tf_op jit(solution)/shard_map/ppermute | solution.py:285
  23.4 19.6 %collective-permute-start.3 = (f32[4,128,128]{2,1,0:T(8,128)S(1)}, f32[4,128,128]{2,1,0:T(8,128)S(1)}, u32[]{:S(2)}, u32[]{:S(2)}) collective-permute-start(f32[4,128,128]{2,1,0:T(8,128)S(1)} %get-tuple-element.47), channel_id=1, source_target_pairs={{8,16},{16,8},{9,17},{17,9},{10,18},{18,10},{11,19},{19,11},{12,20... | collective-permute-start | bytes 786440 | tf_op jit(solution)/shard_map/ppermute | solution.py:285
  24.6 24.1 %collective-permute-start.7 = (f32[4,128,128]{2,1,0:T(8,128)S(1)}, f32[4,128,128]{2,1,0:T(8,128)S(1)}, u32[]{:S(2)}, u32[]{:S(2)}) collective-permute-start(f32[4,128,128]{2,1,0:T(8,128)S(1)} %get-tuple-element.62), channel_id=1, source_target_pairs={{16,24},{24,16},{8,0},{0,8},{17,25},{25,17},{9,1},{1,9},{18,26},{2... | collective-permute-start | bytes 786440 | tf_op jit(solution)/shard_map/ppermute | solution.py:285
  43.0 5.7 %copy-start.1 = (bf16[1,8,256,128]{3,2,1,0:T(8,128)(2,1)S(1)}, bf16[1,8,256,128]{3,2,1,0:T(8,128)(2,1)}, u32[]{:S(2)}) copy-start(bf16[1,8,256,128]{3,2,1,0:T(8,128)(2,1)} %param.8) | copy-start | bytes 1572868
  43.0 5.7 %copy-start.3 = (bf16[1,8,256,128]{3,2,1,0:T(8,128)(2,1)S(1)}, bf16[1,8,256,128]{3,2,1,0:T(8,128)(2,1)}, u32[]{:S(2)}) copy-start(bf16[1,8,256,128]{3,2,1,0:T(8,128)(2,1)} %param.9) | copy-start | bytes 1572868
  43.0 5.7 %copy-start.7 = (bf16[1,256,128]{2,1,0:T(8,128)(2,1)S(1)}, bf16[1,256,128]{2,1,0:T(8,128)(2,1)}, u32[]{:S(2)}) copy-start(bf16[1,256,128]{2,1,0:T(8,128)(2,1)} %param.10) | copy-start | bytes 196612
  43.3 9.8 %collective-permute-start.4 = (f32[4,128,128]{2,1,0:T(8,128)S(1)}, f32[4,128,128]{2,1,0:T(8,128)S(1)}, u32[]{:S(2)}, u32[]{:S(2)}) collective-permute-start(f32[4,128,128]{2,1,0:T(8,128)S(1)} %get-tuple-element.50), channel_id=1, source_target_pairs={{16,24},{24,16},{8,0},{0,8},{17,25},{25,17},{9,1},{1,9},{18,26},{2... | collective-permute-start | bytes 786440 | tf_op jit(solution)/shard_map/ppermute | solution.py:285
  57.3 1.2 %collective-permute-start.9 = (f32[8,128]{1,0:T(8,128)S(1)}, f32[8,128]{1,0:T(8,128)S(1)}, u32[]{:S(2)}, u32[]{:S(2)}) collective-permute-start(f32[8,128]{1,0:T(8,128)S(1)} %get-tuple-element.74), channel_id=1, source_target_pairs={{0,1},{1,0},{2,3},{3,2},{4,5},{5,4},{6,7},{7,6},{8,9},{9,8},{10,11... | collective-permute-start | bytes 12296 | tf_op jit(solution)/shard_map/ppermute | solution.py:327
  58.5 3.6 %collective-permute-start.10 = (f32[8,128]{1,0:T(8,128)S(1)}, f32[8,128]{1,0:T(8,128)S(1)}, u32[]{:S(2)}, u32[]{:S(2)}) collective-permute-start(f32[8,128]{1,0:T(8,128)S(1)} %add.16), channel_id=1, source_target_pairs={{0,2},{1,3},{2,0},{3,1},{4,6},{5,7},{6,4},{7,5},{8,10},{9,11},{10,... | collective-permute-start | bytes 12296 | tf_op jit(solution)/shard_map/ppermute | solution.py:327
  62.1 3.6 %collective-permute-start.11 = (f32[8,128]{1,0:T(8,128)S(1)}, f32[8,128]{1,0:T(8,128)S(1)}, u32[]{:S(2)}, u32[]{:S(2)}) collective-permute-start(f32[8,128]{1,0:T(8,128)S(1)} %add.17), channel_id=1, source_target_pairs={{0,8},{8,0},{16,24},{24,16},{1,9},{9,1},{17,25},{25,17},{2,10},{10... | collective-permute-start | bytes 12296 | tf_op jit(solution)/shard_map/ppermute | solution.py:327
  65.7 5.3 %collective-permute-start.12 = (f32[8,128]{1,0:T(8,128)S(1)}, f32[8,128]{1,0:T(8,128)S(1)}, u32[]{:S(2)}, u32[]{:S(2)}) collective-permute-start(f32[8,128]{1,0:T(8,128)S(1)} %add.18), channel_id=1, source_target_pairs={{0,16},{8,24},{16,0},{24,8},{1,17},{9,25},{17,1},{25,9},{2,18},{10... | collective-permute-start | bytes 12296 | tf_op jit(solution)/shard_map/ppermute | solution.py:327
  69.5 5.0 %collective-permute-start.8 = (f32[2,128,128]{2,1,0:T(8,128)S(1)}, f32[2,128,128]{2,1,0:T(8,128)S(1)}, u32[]{:S(2)}, u32[]{:S(2)}) collective-permute-start(f32[2,128,128]{2,1,0:T(8,128)S(1)} %get-tuple-element.72), channel_id=1, source_target_pairs={{0,4},{4,0},{1,5},{5,1},{2,6},{6,2},{3,7},{7,3},{8,12},{12,8},{9,1... | collective-permute-start | bytes 393224 | tf_op jit(solution)/shard_map/ppermute | solution.py:315

commit v2 on v1

v2 whole, which is shorter than its diff:
```python
import functools
import jax
import jax.numpy as jnp
from jax import lax
from jax.experimental import pallas as pl
from jax.experimental.pallas import tpu as pltpu
from jax.sharding import PartitionSpec as P

CHUNKS = 2
f32, bf16 = jnp.float32, jnp.bfloat16
highest = lax.Precision.HIGHEST
VMEM = pl.BlockSpec(memory_space=pltpu.VMEM)
SMEM = pl.BlockSpec(memory_space=pltpu.SMEM)
HBM = pl.BlockSpec(memory_space=pltpu.HBM)
LIMIT = 48 * 1024 * 1024
shape = jax.ShapeDtypeStruct


def dot(a, b):
    return jnp.dot(a, b, preferred_element_type=f32)


def dot_nt(a, b):
    return lax.dot_general(a, b, (((1,), (1,)), ((), ())), preferred_element_type=f32)


def call(body, outs, *args, flops=10**8, ins=None, out_specs=None, scratch=()):
    return pl.pallas_call(
        body,
        out_shape=outs,
        in_specs=ins or [SMEM if a.ndim == 1 else VMEM for a in args],
        out_specs=out_specs or [VMEM] * len(outs),
        scratch_shapes=scratch,
        compiler_params=pltpu.CompilerParams(vmem_limit_bytes=LIMIT),
        cost_estimate=pl.CostEstimate(flops=flops // 10**5, bytes_accessed=1 << 8, transcendentals=0),
    )(*args)


def triangle(size, lower):
    rows = lax.broadcasted_iota(jnp.int32, (size, size), 0)
    cols = lax.broadcasted_iota(jnp.int32, (size, size), 1)
    return rows >= cols if lower else cols >= rows


def head_row(values, width):
    lanes = lax.broadcasted_iota(jnp.int32, (1, width), 1)
    row = jnp.zeros((1, width), f32)
    for h in range(values.shape[0]):
        row = jnp.where(lanes == h, values[h], row)
    return row


def steps_of(raw, bias, rate, width):
    heads, size = raw.shape
    columns = jnp.concatenate([raw, jnp.zeros((width - heads, size), f32)], axis=0).T
    shifted = columns + bias
    dt = jnp.maximum(shifted, 0.0) + jnp.log1p(jnp.exp(-jnp.abs(shifted)))
    lower = jnp.where(triangle(size, True), 1.0, 0.0).astype(f32)
    return shifted, dt, jnp.dot(lower, -rate * dt, precision=highest, preferred_element_type=f32)


def load_body(x, t, b, c, raw, xv, tv, bv, cv, rawv, own, sems):
    copies = [
        pltpu.make_async_copy(src, dst, sems.at[i])
        for i, (src, dst) in enumerate(((c, cv), (raw, rawv), (b, bv), (x, xv), (t, tv)))
    ]
    for copy in copies:
        copy.start()
    copies[0].wait()
    copies[1].wait()
    size, state = c.shape
    heads = raw.shape[0]
    own[:size, :] = cv[...].astype(f32)
    for s in range(size // state):
        own[size + s * heads : size + (s + 1) * heads, :] = rawv[:, s * state : (s + 1) * state]
    for copy in copies[2:]:
        copy.wait()


def prepare_body(b, c, raw, a_log, skip, dt_bias, cols_out, low_out, low_t_out, b_t_out, c_t_out, sq_out, rows_out):
    size, width = b.shape
    lanes = lax.broadcasted_iota(jnp.int32, (1, width), 1)
    rate = jnp.where(lanes < a_log.shape[0], jnp.exp(head_row(a_log, width)), 0.0)
    bias = head_row(dt_bias, width)
    shifted, dt, logs = steps_of(raw[...], bias, rate, width)
    mid = 0.5 * logs[size - 1 : size, :]
    cols_out[0] = jnp.exp(logs - mid)
    cols_out[1] = dt * jnp.exp(mid - logs)
    cols_out[2] = dt
    cols_out[3] = shifted
    half = jnp.exp(mid)
    rows_out[...] = jnp.concatenate([half, half * half, rate, head_row(skip, width), bias, jnp.zeros((3, width), f32)], axis=0)
    sq_out[...] = jnp.exp(2.0 * logs).T
    low_out[...] = jnp.where(triangle(size, True), dot_nt(c[...], b[...]), 0.0).astype(bf16)
    low_t_out[...] = jnp.where(triangle(size, False), dot_nt(b[...], c[...]), 0.0).astype(bf16)
    b_t_out[...] = b[...].T
    c_t_out[...] = c[...].T


def first_body(heads, x, t, cols, low, b_t, c_t, rows, f_out, p_out, xr_out, y_out, err_out):
    for k, h in enumerate(heads):
        xs = x[h].astype(f32)
        g, scale, skip = cols[0, :, h : h + 1], rows[0:1, h : h + 1], rows[3:4, h : h + 1]
        xr = (xs * cols[1, :, h : h + 1]).astype(bf16)
        y = dot(low[...], xr)
        err = g * y + skip * xs - t[h].astype(f32)
        ew = (err * g).astype(bf16)
        xr_out[k] = xr
        y_out[k] = y
        err_out[k] = err
        f_out[k] = scale * dot(b_t[...], xr)
        p_out[k] = scale * dot(c_t[...], ew)


def send_body(f, p, *refs):
    got, (pay_out, *low_outs) = refs[:-3], refs[-3:] if len(refs) == 4 else refs
    pay_out[...] = jnp.where(lax.axis_index("ctx") == 0, f[...], p[...])
    if got:
        c = got[0][: low_outs[0].shape[0], :].astype(bf16)
        low_outs[0][...] = c
        low_outs[1][...] = c.T


def own_map_body(c, c_t, sq, m_out):
    wide = c_t[...].astype(f32)
    for h in range(m_out.shape[0]):
        m_out[h] = dot((wide * sq[h : h + 1, :]).astype(bf16), c[...])


def later_maps_body(reach, rows, c_first, c_t_first, *refs):
    later, outs = refs[:reach], refs[reach:]
    heads, width = outs[0].shape[0], outs[0].shape[2]
    size = c_first.shape[0]
    factor = jnp.ones((1, width), f32)
    for i, (got, out) in enumerate(zip(later, outs)):
        raw = jnp.concatenate([got[size + s * heads : size + (s + 1) * heads, :] for s in range(size // width)], axis=1)
        _, _, logs = steps_of(raw, rows[4:5, :], rows[2:3, :], width)
        c = got[:size, :].astype(bf16) if i else c_first[...]
        c_t = (c.T if i else c_t_first[...]).astype(f32)
        sq = jnp.exp(2.0 * logs).T
        for h in range(heads):
            added = factor[:, h : h + 1] * dot((c_t * sq[h : h + 1, :]).astype(bf16), c)
            out[h] = outs[i - 1][h] + added if i else added
        factor = factor * jnp.exp(2.0 * logs[size - 1 : size, :])


def times(m, s):
    high = m.astype(bf16)
    low = (m - high.astype(f32)).astype(bf16)
    s_low = s.astype(bf16)
    return dot(high, s_low) + dot(low, s_low)


def round_body(heads, n, r, f, p, m, mc, rows, got, s_in, d_in, pay_out, s_out, d_out):
    place = lax.axis_index("ctx")
    came_up, came_down = place == r - 1, place == n - r
    for k, h in enumerate(heads):
        s = jnp.where(came_up, got[k], s_in[k])
        d = jnp.where(came_down, got[k], d_in[k])
        s_out[k] = s
        d_out[k] = d
        total = rows[1:2, h : h + 1]
        after = total * s + f[k]
        full = p[k] + times(m[h], s) + total * (d + times(mc[h], after))
        pay_out[k] = jnp.where(place == r - 1, after, full)


def last_body(heads, scales, *refs):
    (x, cols, low, low_t, b, c, rows, xr, y_in, err_in, f, mc, got, s_in, d_in, v_in, sums_in) = refs[:17]
    gx_out, ew_out, s_low_out, a_low_out, v_out, sums_out = refs[17:23]
    n = lax.axis_size("ctx")
    place = lax.axis_index("ctx")
    size, width = b.shape
    channels = x.shape[2]
    lanes = lax.broadcasted_iota(jnp.int32, (1, width), 1)
    v_all, w_all = v_in[0], v_in[1]
    ends, skips = sums_in[0:1, :], sums_in[1:2, :]
    for k, h in enumerate(heads):
        g, r = cols[0, :, h : h + 1], cols[1, :, h : h + 1]
        scale, total, skip = rows[0:1, h : h + 1], rows[1:2, h : h + 1], rows[3:4, h : h + 1]
        s = jnp.where(place == n - 1, got[k], s_in[k]) if n > 1 else s_in[k]
        d = jnp.where(place == 0, got[k], d_in[k]) if n > 1 else d_in[k]
        after = total * s + f[k]
        adjoint = d + times(mc[h], after)
        s_low = (scale * s).astype(bf16)
        a_low = (scale * adjoint).astype(bf16)
        carried = dot(c[...], s_low)
        y = y_in[k] + carried
        err = err_in[k] + g * carried
        ew = (err * g).astype(bf16)
        z = dot(low_t[...], ew) + dot(b[...], a_low)
        gx_out[k] = (r * z + skip * err).astype(bf16)
        here = lanes == h
        v_all = jnp.where(here, jnp.sum(ew.astype(f32) * y, axis=1, keepdims=True), v_all)
        w_all = jnp.where(here, jnp.sum(xr[k].astype(f32) * z, axis=1, keepdims=True), w_all)
        ends = jnp.where(here, jnp.sum(jnp.sum(adjoint * after, axis=0, keepdims=True), axis=1, keepdims=True), ends)
        skips = jnp.where(here, jnp.sum(jnp.sum(err * x[h].astype(f32), axis=0, keepdims=True), axis=1, keepdims=True), skips)
        span = slice(k * channels, (k + 1) * channels)
        ew_out[:, span] = ew
        s_low_out[:, span] = s_low
        a_low_out[:, span] = a_low
    if scales is None:
        v_out[0] = v_all
        v_out[1] = w_all
        sums_out[...] = jnp.concatenate([ends, skips, jnp.zeros((6, width), f32)], axis=0)
        return
    count = v_out.shape[0]
    rate, dt = rows[2:3, :], cols[2]
    last = lax.broadcasted_iota(jnp.int32, (size, width), 0) == size - 1
    grad_logs = v_all - w_all + jnp.where(last, ends, 0.0)
    upper = jnp.where(triangle(size, False), 1.0, 0.0).astype(f32)
    log_rate = jnp.dot(upper, grad_logs, precision=highest, preferred_element_type=f32)
    grad_raw = (w_all / dt - rate * log_rate) / (1.0 + jnp.exp(-cols[3]))
    v_out[...] = grad_raw.T[:count, :]
    alog = -rate * jnp.sum(log_rate * dt, axis=0, keepdims=True)
    bias = jnp.sum(grad_raw, axis=0, keepdims=True)
    sums_out[...] = jnp.concatenate(
        [alog * scales[0], skips * scales[1], bias * scales[0], jnp.zeros((5, width), f32)], axis=0
    )


def project_body(b, c, xr, ew, s_low, a_low, grads_in, grads_out):
    size = b.shape[0]
    wide = jnp.concatenate([xr[k] for k in range(xr.shape[0])], axis=1)
    score = jnp.where(triangle(size, True), dot_nt(ew[...], wide), 0.0).astype(bf16)
    score_t = jnp.where(triangle(size, False), dot_nt(wide, ew[...]), 0.0).astype(bf16)
    grads_out[0] = grads_in[0] + dot(score_t, c[...]) + dot_nt(wide, a_low[...])
    grads_out[1] = grads_in[1] + dot(score, b[...]) + dot_nt(ew[...], s_low[...])


def output_body(chunks, *refs):
    parts = refs[:chunks]
    sums, sums_got = refs[chunks + 7 : chunks + 9]
    keep_out, send_out, gx_out, sums_out, grads, sems = refs[chunks + 9 :]
    sums_out[...] = sums[...] + sums_got[...]
    per = parts[0].shape[0]
    copies = [pltpu.make_async_copy(part, gx_out.at[pl.ds(i * per, per)], sems.at[i]) for i, part in enumerate(parts)]
    for copy in copies:
        copy.start()
    project_body(*refs[chunks : chunks + 7], grads)
    cut, size = keep_out.shape[1], grads.shape[1]
    upper = lax.axis_index("head") >= lax.axis_size("head") // 2
    for i in range(2):
        grad = grads[i]
        keep_out[i] = jnp.where(upper, grad[size - cut :, :], grad[:cut, :])
        send_out[i] = jnp.where(upper, grad[:cut, :], grad[size - cut :, :])
    for copy in copies:
        copy.wait()


def add_body(a, b, c, d, first_out, second_out):
    first_out[...] = a[...] + b[...]
    second_out[...] = c[...] + d[...]


def on_device(x_heads, target, b_proj, c_proj, dt_raw, a_log, skip_gain, dt_bias):
    heads, size, channels = x_heads.shape[1:]
    width = b_proj.shape[2]
    n = lax.axis_size("ctx")
    parts = lax.axis_size("head")
    chunks = CHUNKS if heads % CHUNKS == 0 else 1
    per = heads // chunks
    groups = [tuple(range(i * per, (i + 1) * per)) for i in range(chunks)]
    square, states, all_states = shape((size, size), bf16), shape((per, width, channels), f32), shape((heads, width, width), f32)
    flat = shape((width, size), bf16)
    panel = shape((per, size, channels), f32)

    x, t, b, c, raw, own = call(
        load_body,
        [shape(a.shape[1:], a.dtype) for a in (x_heads, target, b_proj, c_proj, dt_raw)]
        + [shape((size + heads * size // width, width), f32)],
        *[pltpu.with_memory_space_constraint(a[0], pltpu.HBM) for a in (x_heads, target, b_proj, c_proj, dt_raw)],
        ins=[HBM] * 5, scratch=[pltpu.SemaphoreType.DMA((5,))], flops=10**6,
    )
    lowest = max(n // 2 - 1, 0)
    later = []
    for s in range(1, n - lowest):
        own = lax.ppermute(own, "ctx", [(i + 1, i) for i in range(lowest, n - s)])
        later.append(own)
    cols, low, low_t, b_t, c_t, sq, rows = call(
        prepare_body,
        [shape((4, size, width), f32), square, square, flat, flat, shape((width, size), f32), shape((8, width), f32)],
        b, c, raw, a_log, skip_gain, dt_bias,
    )
    held = []
    maps = [jnp.zeros(all_states.shape, f32)]
    for i, group in enumerate(groups):
        f, p, xr, y, err = call(
            functools.partial(first_body, group),
            [states, states, shape(panel.shape, bf16), panel, panel],
            x, t, cols, low, b_t, c_t, rows, flops=4 * 10**8,
        )
        if i == 0 and later:
            pay, *lows = call(send_body, [states, shape((size, width), bf16), flat], f, p, later[0])
        else:
            (pay,) = call(send_body, [states], f, p)
        zero = jnp.zeros(states.shape, f32)
        held.append(dict(f=f, p=p, pay=pay, xr=xr, y=y, err=err, s=zero, d=zero))
    (m,) = call(own_map_body, [all_states], c, c_t, sq)
    if later:
        maps += call(functools.partial(later_maps_body, len(later)), [all_states] * len(later), rows, *lows, *later)

    def swap(r):
        pairs = [(r - 1, r), (r, r - 1)]
        other = [(n - r, n - 1 - r), (n - 1 - r, n - r)]
        return pairs if r - 1 == n - 1 - r else pairs + other

    for stage in range(1, n - 1 + chunks):
        for i, h in enumerate(held):
            r = stage - i
            if not 1 <= r <= n - 1:
                continue
            if r > 1:
                h["pay"], h["s"], h["d"] = call(
                    functools.partial(round_body, groups[i], n, r), [states, states, states],
                    h["f"], h["p"], m, maps[min(r - 1, len(later))], rows, h["got"], h["s"], h["d"],
                )
            h["got"] = lax.ppermute(h["pay"], "ctx", swap(r))

    tokens = size * n * x_heads.shape[0] * lax.axis_size("seq")
    scales = (1.0 / tokens, 1.0 / (tokens * channels))
    cut = size if parts == 1 else size // 2
    v, total = jnp.zeros((2, size, width), f32), jnp.zeros((8, width), f32)
    grads = jnp.zeros((2, size, width), f32)
    grad_x = []
    for i, h in enumerate(held):
        final = i == chunks - 1
        gx, ew, s_low, a_low, v, total = call(
            functools.partial(last_body, groups[i], scales if final else None),
            [shape(panel.shape, bf16), shape((size, per * channels), bf16)] + [shape((width, per * channels), bf16)] * 2
            + [shape(raw.shape if final else v.shape, f32), shape((8, width), f32)],
            x, cols, low, low_t, b, c, rows, h["xr"], h["y"], h["err"], h["f"], maps[-1],
            h.get("got", h["s"]), h["s"], h["d"], v, total, flops=4 * 10**8,
        )
        grad_x.append(gx)
        args = (b, c, h["xr"], ew, s_low, a_low, grads)
        if not final:
            (grads,) = call(project_body, [shape(grads.shape, f32)], *args, flops=2 * 10**8)
    swaps = [(axis, 1 << k) for axis in ("seq", "ctx") for k in reversed(range(lax.axis_size(axis).bit_length() - 1))]
    if ("seq", 1) in swaps:
        swaps.remove(("seq", 1))
        got = lax.ppermute(total, "seq", [(i, i ^ 1) for i in range(lax.axis_size("seq"))])
    else:
        got = jnp.zeros(total.shape, f32)
    halves = shape((2, cut, width), f32)
    keep, send, grad_x, total = call(
        functools.partial(output_body, chunks),
        [halves, halves, shape((heads, size, channels), bf16), shape(total.shape, f32)],
        *grad_x, *args, total, got, out_specs=[VMEM, VMEM, HBM, VMEM], flops=2 * 10**8,
        scratch=[pltpu.VMEM(grads.shape, f32), pltpu.SemaphoreType.DMA((chunks,))],
    )
    step = parts // 2
    while step >= 1:
        received = lax.ppermute(send, "head", [(i, i ^ step) for i in range(parts)])
        if swaps:
            axis, by = swaps.pop()
            got = lax.ppermute(total, axis, [(i, i ^ by) for i in range(lax.axis_size(axis))])
            keep, total = call(add_body, [shape(keep.shape, f32), shape(total.shape, f32)], keep, received, total, got)
        else:
            keep = keep + received
        step //= 2
        if step >= 1:
            cut = keep.shape[1] // 2
            upper = (lax.axis_index("head") // step) % 2 == 1
            keep, send = (
                jnp.where(upper, keep[:, cut:], keep[:, :cut]),
                jnp.where(upper, keep[:, :cut], keep[:, cut:]),
            )
    while swaps:
        axis, by = swaps.pop()
        total = total + lax.ppermute(total, axis, [(i, i ^ by) for i in range(lax.axis_size(axis))])
    return (
        grad_x[None], keep[0][None], keep[1][None], v[None],
        total[0, :heads], total[1, :heads], total[2, :heads],
    )


def solution(mesh):
    return jax.shard_map(
        on_device,
        mesh=mesh,
        in_specs=(
            P("seq", "head", "ctx", None),
            P("seq", "head", "ctx", None),
            P("seq", "ctx", None),
            P("seq", "ctx", None),
            P("seq", "head", "ctx"),
            P("head"),
            P("head"),
            P("head"),
        ),
        out_specs=(
            P("seq", "head", "ctx", None),
            P("seq", ("ctx", "head"), None),
            P("seq", ("ctx", "head"), None),
            P("seq", "head", "ctx"),
            P("head"),
            P("head"),
            P("head"),
        ),
        check_vma=False,
    )
```

time: 75.6 us -> 63.8 us (0.84)
  starting transfers between devices: 39 us -> 30.4 us
  waiting for transfers between devices: 11.3 us -> 16.6 us
  local copies, waits for them, and re-layouts: 6.32 us -> 1.88 us
  Pallas kernels: 17.7 us -> 13.8 us
    ppermute x6, starting transfers between devices: 29 us -> 21.5 us  [on_device(): h['got'] = lax.ppermute(h['pay'], 'ctx', swap(r))]
    ppermute x6, waiting for transfers between devices: 3.36 us -> 10.5 us  [on_device(): h['got'] = lax.ppermute(h['pay'], 'ctx', swap(r))]
    unnamed x26 -> x6, local copies, waits for them, and re-layouts: 5.12 us -> 0.67 us
    pallas_call x10 -> x17, Pallas kernels: 17.7 us -> 13.8 us  [call(): pl.pallas_call(body, out_shape=outs, in_specs=ins or [SMEM if a.ndim == 1...]
    ppermute x7, waiting for transfers between devices: 7.91 us -> 6.13 us  [the longest x3 5.13 us: on_device(): lax.ppermute(total, axis, [(i, i ^ by) for i in range(lax.axis_size(axis))])]
    ppermute x7, starting transfers between devices: 10 us -> 8.93 us  [the longest x3 6 us: on_device(): lax.ppermute(total, axis, [(i, i ^ by) for i in range(lax.axis_size(axis))])]
  transfers between devices with their start and end apart: 13 -> 13, of which waited for: 8 -> 9; matrix products, arithmetic and copies ran while one was open for 1% -> 1% of each run, Pallas kernels for 15% -> 14%
where the time goes in v2:
time: 63.8 us; the launch traced here: 63.6 us
  starting transfers between devices  30.4 us (48%)
  waiting for transfers between devices  16.6 us (26%)
  Pallas kernels  13.8 us (22%)
  local copies, waits for them, and re-layouts  1.88 us (3%)
  between operations  0.83 us (1%)
    ppermute x6, starting transfers between devices, on_device(): h['got'] = lax.ppermute(h['pay'], 'ctx', swap(r))  21.5 us
    pallas_call x17, Pallas kernels, call(): pl.pallas_call(body, out_shape=outs, in_specs=ins or [SMEM if a.ndim == 1...  13.8 us
    ppermute x6, waiting for transfers between devices, on_device(): h['got'] = lax.ppermute(h['pay'], 'ctx', swap(r))  10.5 us
    ppermute x3, starting transfers between devices, on_device(): lax.ppermute(total, axis, [(i, i ^ by) for i in range(lax.axis_size(axis))])  6 us
    ppermute x3, waiting for transfers between devices, on_device(): lax.ppermute(total, axis, [(i, i ^ by) for i in range(lax.axis_size(axis))])  5.13 us
    ppermute x1, starting transfers between devices, on_device(): received = lax.ppermute(send, 'head', [(i, i ^ step) for i in range(parts)])  1.59 us
    ppermute x2, starting transfers between devices, on_device(): own = lax.ppermute(own, 'ctx', [(i + 1, i) for i in range(lowest, n - s)])  1.34 us
  transfers between devices with their start and end apart: 13, of which 9 were waited for; matrix products, arithmetic and copies ran while one was open for 1% of the time, Pallas kernels for 14%

profile of v2, /device:TPU:0, one launch (start us, length us, event | category | flops | bytes accessed | tf_op | source)
XLA Modules:
  0.0 63.6 jit_solution(7152627185212930959)
XLA Ops:
  0.6 1.3 %shard_map.135 = (bf16[8,256,128]{2,1,0:T(8,128)(2,1)S(1)}, bf16[8,256,128]{2,1,0:T(8,128)(2,1)S(1)}, bf16[256,128]{1,0:T(8,128)(2,1)S(1)}, bf16[256,128]{1,0:T(...) custom-call(bf16[8,256,128]{2,1,0:T(8,128)(2,1)} %bitcast.13, bf16[8,256,128]{2,1,0:T(8,128)(2,1)} %bitcast.14, ...), custom_call_target="tpu_custom_call" | custom-call | flops 10 | bytes 256 | tf_op jit(solution)/shard_map/pallas_call | solution.py:28
  2.0 0.7 %collective-permute-start = (f32[272,128]{1,0:T(8,128)S(1)}, f32[272,128]{1,0:T(8,128)S(1)}, u32[]{:S(2)}, u32[]{:S(2)}) collective-permute-start(f32[272,128]{1,0:T(8,128)S(1)} %get-tuple-element.81), channel_id=1, source_target_pairs={{16,8},{24,16},{17,9},{25,17},{18,10},{26,18},{19,11},{27,19},{20,... | collective-permute-start | bytes 417800 | tf_op jit(solution)/shard_map/ppermute | solution.py:278
  2.7 0.0 copy-start
  2.7 0.0 copy-start.1
  2.7 0.0 copy-start.2
  2.7 0.6 copy-done
  3.3 0.0 copy-done.1
  3.3 0.0 copy-done.2
  3.3 1.2 %shard_map.136 = (f32[4,256,128]{2,1,0:T(8,128)S(1)}, bf16[256,256]{1,0:T(8,128)(2,1)S(1)}, bf16[256,256]{1,0:T(8,128)(2,1)S(1)}, bf16[128,256]{1,0:T(8,128)(2,1...) custom-call(bf16[256,128]{1,0:T(8,128)(2,1)S(1)} %get-tuple-element.66.b.refs_4_.refs_2_, ...), custom_call_target="tpu_custom_call" | custom-call | flops 1000 | bytes 256 | tf_op jit(solution)/shard_map/pallas_call | solution.py:28
  4.6 0.7 %shard_map.137 = (f32[4,128,128]{2,1,0:T(8,128)S(1)}, f32[4,128,128]{2,1,0:T(8,128)S(1)}, bf16[4,256,128]{2,1,0:T(8,128)(2,1)S(1)}, f32[4,256,128]{2,1,0:T(8,128)S(1)}, f32[4,256,128]{2,1,0:T(8,128)S(1)}) custom-call(bf16[8,256,128]{2,1,0:T(8,128)(2,1)S(1)} %get-tuple-element.65.x.refs_0_, bf16[8,256,128]{2,1,0:T(8,128)(2,1)S(1)} %get-tuple-element.73.t, ...), custom_call_target="tpu_custom_call" | custom-call | flops 4000 | bytes 256 | tf_op jit(solution)/shard_map/pallas_call | solution.py:28
  5.3 0.0 collective-permute-done.refs_0_
  5.3 0.1 shard_map.138
  5.4 7.0 %collective-permute-start.2 = (f32[4,128,128]{2,1,0:T(8,128)S(1)}, f32[4,128,128]{2,1,0:T(8,128)S(1)}, u32[]{:S(2)}, u32[]{:S(2)}) collective-permute-start(f32[4,128,128]{2,1,0:T(8,128)S(1)} %get-tuple-element.87), channel_id=1, source_target_pairs={{0,8},{8,0},{24,16},{16,24},{1,9},{9,1},{25,17},{17,25},{2,10},{10... | collective-permute-start | bytes 786440 | tf_op jit(solution)/shard_map/ppermute | solution.py:318
  12.5 0.7 %shard_map.144 = (f32[4,128,128]{2,1,0:T(8,128)S(1)}, f32[4,128,128]{2,1,0:T(8,128)S(1)}, bf16[4,256,128]{2,1,0:T(8,128)(2,1)S(1)}, f32[4,256,128]{2,1,0:T(8,128)S(1)}, f32[4,256,128]{2,1,0:T(8,128)S(1)}) custom-call(bf16[8,256,128]{2,1,0:T(8,128)(2,1)S(1)} %get-tuple-element.65.x.refs_0_, bf16[8,256,128]{2,1,0:T(8,128)(2,1)S(1)} %get-tuple-element.73.t, ...), custom_call_target="tpu_custom_call" | custom-call | flops 4000 | bytes 256 | tf_op jit(solution)/shard_map/pallas_call | solution.py:28
  13.2 0.1 collective-permute-start.5
  13.3 0.7 %collective-permute-start.1 = (f32[272,128]{1,0:T(8,128)S(1)}, f32[272,128]{1,0:T(8,128)S(1)}, u32[]{:S(2)}, u32[]{:S(2)}) collective-permute-start(f32[272,128]{1,0:T(8,128)S(1)} %collective-permute-done.refs_0_), channel_id=1, source_target_pairs={{16,8},{17,9},{18,10},{19,11},{20,12},{21,13},{22,14},{23,15}} | collective-permute-start | bytes 417800 | tf_op jit(solution)/shard_map/ppermute | solution.py:278
  14.0 0.3 shard_map.140.m
  14.2 0.0 collective-permute-done.1.refs_1_
  14.3 2.0 %shard_map.139 = (f32[8,128,128]{2,1,0:T(8,128)S(1)}, f32[8,128,128]{2,1,0:T(8,128)S(1)}) custom-call(f32[8,128]{1,0:T(8,128)S(1)} %get-tuple-element.72.rows.refs_6_, bf16[256,128]{1,0:T(8,128)(2,1)S(1)} %get-tuple-element.82.c_first, bf16[128,256]{1,0:T(8,128)(2,1)S(1)} %get-tuple-element.83.c_t_first, f32[272,128]{1,0:T(8,128)S(1)} %collective-permute-done.refs_0_, ...), custom_call_target="tpu_custom_call" | custom-call | flops 1000 | bytes 256 | tf_op jit(solution)/shard_map/pallas_call | solution.py:28
  16.3 3.4 %collective-permute-done.2.got = f32[4,128,128]{2,1,0:T(8,128)S(1)} collective-permute-done((f32[4,128,128]{2,1,0:T(8,128)S(1)}, f32[4,128,128]{2,1,0:T(8,128)S(1)}, u32[]{:S(2)}, u32[]{:S(2)}) %collective-permute-start.2) | collective-permute-done | bytes 262176 | tf_op jit(solution)/shard_map/ppermute | solution.py:318
  19.7 0.4 shard_map.141
  20.1 0.7 %collective-permute-start.3 = (f32[4,128,128]{2,1,0:T(8,128)S(1)}, f32[4,128,128]{2,1,0:T(8,128)S(1)}, u32[]{:S(2)}, u32[]{:S(2)}) collective-permute-start(f32[4,128,128]{2,1,0:T(8,128)S(1)} %get-tuple-element.88), channel_id=1, source_target_pairs={{8,16},{16,8},{9,17},{17,9},{10,18},{18,10},{11,19},{19,11},{12,20... | collective-permute-start | bytes 786440 | tf_op jit(solution)/shard_map/ppermute | solution.py:318
  20.8 2.7 %collective-permute-done.5.got = f32[4,128,128]{2,1,0:T(8,128)S(1)} collective-permute-done((f32[4,128,128]{2,1,0:T(8,128)S(1)}, f32[4,128,128]{2,1,0:T(8,128)S(1)}, u32[]{:S(2)}, u32[]{:S(2)}) %collective-permute-start.5) | collective-permute-done | bytes 262176 | tf_op jit(solution)/shard_map/ppermute | solution.py:318
  23.5 0.4 shard_map.146
  23.9 0.7 %collective-permute-start.6 = (f32[4,128,128]{2,1,0:T(8,128)S(1)}, f32[4,128,128]{2,1,0:T(8,128)S(1)}, u32[]{:S(2)}, u32[]{:S(2)}) collective-permute-start(f32[4,128,128]{2,1,0:T(8,128)S(1)} %get-tuple-element.100), channel_id=1, source_target_pairs={{8,16},{16,8},{9,17},{17,9},{10,18},{18,10},{11,19},{19,11},{12,20... | collective-permute-start | bytes 786440 | tf_op jit(solution)/shard_map/ppermute | solution.py:318
  24.6 0.0 collective-permute-done.3.got
  24.6 0.4 shard_map.142
  25.0 10.6 %collective-permute-start.4 = (f32[4,128,128]{2,1,0:T(8,128)S(1)}, f32[4,128,128]{2,1,0:T(8,128)S(1)}, u32[]{:S(2)}, u32[]{:S(2)}) collective-permute-start(f32[4,128,128]{2,1,0:T(8,128)S(1)} %get-tuple-element.91), channel_id=1, source_target_pairs={{16,24},{24,16},{8,0},{0,8},{17,25},{25,17},{9,1},{1,9},{18,26},{2... | collective-permute-start | bytes 786440 | tf_op jit(solution)/shard_map/ppermute | solution.py:318
  35.6 0.0 collective-permute-done.6.got
  35.6 0.4 shard_map.147
  36.0 2.4 %collective-permute-start.7 = (f32[4,128,128]{2,1,0:T(8,128)S(1)}, f32[4,128,128]{2,1,0:T(8,128)S(1)}, u32[]{:S(2)}, u32[]{:S(2)}) collective-permute-start(f32[4,128,128]{2,1,0:T(8,128)S(1)} %get-tuple-element.103), channel_id=1, source_target_pairs={{16,24},{24,16},{8,0},{0,8},{17,25},{25,17},{9,1},{1,9},{18,26},{2... | collective-permute-start | bytes 786440 | tf_op jit(solution)/shard_map/ppermute | solution.py:318
  38.4 3.1 %collective-permute-done.4.refs_12_ = f32[4,128,128]{2,1,0:T(8,128)S(1)} collective-permute-done((f32[4,128,128]{2,1,0:T(8,128)S(1)}, f32[4,128,128]{2,1,0:T(8,128)S(1)}, u32[]{:S(2)}, u32[]{:S(2)}) %collective-permute-start.4) | collective-permute-done | bytes 262176 | tf_op jit(solution)/shard_map/ppermute | solution.py:318
  41.5 1.5 %shard_map.143 = (bf16[4,256,128]{2,1,0:T(8,128)(2,1)S(1)}, bf16[256,512]{1,0:T(8,128)(2,1)S(1)}, bf16[128,512]{1,0:T(8,128)(2,1)S(1)}, bf16[128,512]{1,0:T(8,12...) custom-call(bf16[8,256,128]{2,1,0:T(8,128)(2,1)S(1)} %get-tuple-element.65.x.refs_0_, ...), custom_call_target="tpu_custom_call" | custom-call | flops 4000 | bytes 256 | tf_op jit(solution)/shard_map/pallas_call | solution.py:28
  43.0 1.2 %collective-permute-done.7.refs_12_ = f32[4,128,128]{2,1,0:T(8,128)S(1)} collective-permute-done((f32[4,128,128]{2,1,0:T(8,128)S(1)}, f32[4,128,128]{2,1,0:T(8,128)S(1)}, u32[]{:S(2)}, u32[]{:S(2)}) %collective-permute-start.7) | collective-permute-done | bytes 262176 | tf_op jit(solution)/shard_map/ppermute | solution.py:318
  44.3 2.6 %shard_map.148 = (bf16[4,256,128]{2,1,0:T(8,128)(2,1)S(1)}, bf16[256,512]{1,0:T(8,128)(2,1)S(1)}, bf16[128,512]{1,0:T(8,128)(2,1)S(1)}, bf16[128,512]{1,0:T(8,12...) custom-call(bf16[8,256,128]{2,1,0:T(8,128)(2,1)S(1)} %get-tuple-element.65.x.refs_0_, ...), custom_call_target="tpu_custom_call" | custom-call | flops 4000 | bytes 256 | tf_op jit(solution)/shard_map/pallas_call | solution.py:28
  46.9 0.6 shard_map.149.refs_8_
  47.5 0.6 collective-permute-done.8.refs_10_
  48.0 1.2 %shard_map.150 = (f32[2,128,128]{2,1,0:T(8,128)S(1)}, f32[2,128,128]{2,1,0:T(8,128)S(1)}, bf16[8,256,128]{2,1,0:T(8,128)(2,1)}, f32[8,128]{1,0:T(8,128)S(1)}) custom-call(bf16[4,256,128]{2,1,0:T(8,128)(2,1)S(1)} %get-tuple-element.94.refs_0_, bf16[4,256,128]{2,1,0:T(8,128)(2,1)S(1)} %get-tuple-element.108.refs_1_, ...), custom_call_target="tpu_custom_call" | custom-call | flops 2000 | bytes 256 | tf_op jit(solution)/shard_map/pallas_call | solution.py:28
  49.3 1.6 %collective-permute-start.9 = (f32[2,128,128]{2,1,0:T(8,128)S(1)}, f32[2,128,128]{2,1,0:T(8,128)S(1)}, u32[]{:S(2)}, u32[]{:S(2)}) collective-permute-start(f32[2,128,128]{2,1,0:T(8,128)S(1)} %get-tuple-element.118), channel_id=1, source_target_pairs={{0,4},{4,0},{1,5},{5,1},{2,6},{6,2},{3,7},{7,3},{8,12},{12,8},{9,1... | collective-permute-start | bytes 393224 | tf_op jit(solution)/shard_map/ppermute | solution.py:354
  50.8 1.7 %collective-permute-start.10 = (f32[8,128]{1,0:T(8,128)S(1)}, f32[8,128]{1,0:T(8,128)S(1)}, u32[]{:S(2)}, u32[]{:S(2)}) collective-permute-start(f32[8,128]{1,0:T(8,128)S(1)} %get-tuple-element.119.c), channel_id=1, source_target_pairs={{0,8},{8,0},{16,24},{24,16},{1,9},{9,1},{17,25},{25,17},{2,10},{10... | collective-permute-start | bytes 12296 | tf_op jit(solution)/shard_map/ppermute | solution.py:357
  52.6 1.9 %collective-permute-done.10.d = f32[8,128]{1,0:T(8,128)S(1)} collective-permute-done((f32[8,128]{1,0:T(8,128)S(1)}, f32[8,128]{1,0:T(8,128)S(1)}, u32[]{:S(2)}, u32[]{:S(2)}) %collective-permute-start.10) | collective-permute-done | bytes 4128 | tf_op jit(solution)/shard_map/ppermute | solution.py:357
  54.5 0.4 collective-permute-done.9.b
  54.9 2.8 %collective-permute-start.11 = (f32[8,128]{1,0:T(8,128)S(1)}, f32[8,128]{1,0:T(8,128)S(1)}, u32[]{:S(2)}, u32[]{:S(2)}) collective-permute-start(f32[8,128]{1,0:T(8,128)S(1)} %get-tuple-element.122), channel_id=1, source_target_pairs={{0,16},{8,24},{16,0},{24,8},{1,17},{9,25},{17,1},{25,9},{2,18},{10... | collective-permute-start | bytes 12296 | tf_op jit(solution)/shard_map/ppermute | solution.py:371
  57.7 1.8 %collective-permute-done.11 = f32[8,128]{1,0:T(8,128)S(1)} collective-permute-done((f32[8,128]{1,0:T(8,128)S(1)}, f32[8,128]{1,0:T(8,128)S(1)}, u32[]{:S(2)}, u32[]{:S(2)}) %collective-permute-start.11) | collective-permute-done | bytes 4128 | tf_op jit(solution)/shard_map/ppermute | solution.py:371
  59.5 1.5 %collective-permute-start.12 = (f32[8,128]{1,0:T(8,128)S(1)}, f32[8,128]{1,0:T(8,128)S(1)}, u32[]{:S(2)}, u32[]{:S(2)}) collective-permute-start(f32[8,128]{1,0:T(8,128)S(1)} %add.6), channel_id=1, source_target_pairs={{0,2},{1,3},{2,0},{3,1},{4,6},{5,7},{6,4},{7,5},{8,10},{9,11},{10,... | collective-permute-start | bytes 12296 | tf_op jit(solution)/shard_map/ppermute | solution.py:371
  61.0 0.7 %fusion = (f32[1,128,128]{2,1,0:T(8,128)}, f32[1,128,128]{2,1,0:T(8,128)}) fusion(f32[2,128,128]{2,1,0:T(8,128)S(1)} %get-tuple-element.120), kind=kLoop, calls=%fused_computation.3 | loop fusion | bytes 262144 | tf_op jit(solution)/shard_map/slice | solution.py:373
  61.6 1.5 %collective-permute-done.12 = f32[8,128]{1,0:T(8,128)S(1)} collective-permute-done((f32[8,128]{1,0:T(8,128)S(1)}, f32[8,128]{1,0:T(8,128)S(1)}, u32[]{:S(2)}, u32[]{:S(2)}) %collective-permute-start.12) | collective-permute-done | bytes 4128 | tf_op jit(solution)/shard_map/ppermute | solution.py:371
  63.1 0.5 slice_bitcast_fusion
  (8 shorter events, 0.1 us)
Async XLA Ops:
  2.0 3.3 %collective-permute-start = (f32[272,128]{1,0:T(8,128)S(1)}, f32[272,128]{1,0:T(8,128)S(1)}, u32[]{:S(2)}, u32[]{:S(2)}) collective-permute-start(f32[272,128]{1,0:T(8,128)S(1)} %get-tuple-element.81), channel_id=1, source_target_pairs={{16,8},{24,16},{17,9},{25,17},{18,10},{26,18},{19,11},{27,19},{20,... | collective-permute-start | bytes 417800 | tf_op jit(solution)/shard_map/ppermute | solution.py:278
  2.7 0.7 %copy-start = (f32[8]{0:T(128)S(1)}, f32[8]{0:T(128)}, u32[]{:S(2)}) copy-start(f32[8]{0:T(128)} %a_log.1) | copy-start | bytes 100
  2.7 0.7 %copy-start.1 = (f32[8]{0:T(128)S(1)}, f32[8]{0:T(128)}, u32[]{:S(2)}) copy-start(f32[8]{0:T(128)} %skip.1) | copy-start | bytes 100
  2.7 0.7 %copy-start.2 = (f32[8]{0:T(128)S(1)}, f32[8]{0:T(128)}, u32[]{:S(2)}) copy-start(f32[8]{0:T(128)} %dt_bias.1) | copy-start | bytes 100
  5.4 14.3 %collective-permute-start.2 = (f32[4,128,128]{2,1,0:T(8,128)S(1)}, f32[4,128,128]{2,1,0:T(8,128)S(1)}, u32[]{:S(2)}, u32[]{:S(2)}) collective-permute-start(f32[4,128,128]{2,1,0:T(8,128)S(1)} %get-tuple-element.87), channel_id=1, source_target_pairs={{0,8},{8,0},{24,16},{16,24},{1,9},{9,1},{25,17},{17,25},{2,10},{10... | collective-permute-start | bytes 786440 | tf_op jit(solution)/shard_map/ppermute | solution.py:318
  13.2 10.3 %collective-permute-start.5 = (f32[4,128,128]{2,1,0:T(8,128)S(1)}, f32[4,128,128]{2,1,0:T(8,128)S(1)}, u32[]{:S(2)}, u32[]{:S(2)}) collective-permute-start(f32[4,128,128]{2,1,0:T(8,128)S(1)} %shard_map.145), channel_id=1, source_target_pairs={{0,8},{8,0},{24,16},{16,24},{1,9},{9,1},{25,17},{17,25},{2,10},{10... | collective-permute-start | bytes 786440 | tf_op jit(solution)/shard_map/ppermute | solution.py:318
  13.3 1.0 %collective-permute-start.1 = (f32[272,128]{1,0:T(8,128)S(1)}, f32[272,128]{1,0:T(8,128)S(1)}, u32[]{:S(2)}, u32[]{:S(2)}) collective-permute-start(f32[272,128]{1,0:T(8,128)S(1)} %collective-permute-done.refs_0_), channel_id=1, source_target_pairs={{16,8},{17,9},{18,10},{19,11},{20,12},{21,13},{22,14},{23,15}} | collective-permute-start | bytes 417800 | tf_op jit(solution)/shard_map/ppermute | solution.py:278
  20.1 4.5 %collective-permute-start.3 = (f32[4,128,128]{2,1,0:T(8,128)S(1)}, f32[4,128,128]{2,1,0:T(8,128)S(1)}, u32[]{:S(2)}, u32[]{:S(2)}) collective-permute-start(f32[4,128,128]{2,1,0:T(8,128)S(1)} %get-tuple-element.88), channel_id=1, source_target_pairs={{8,16},{16,8},{9,17},{17,9},{10,18},{18,10},{11,19},{19,11},{12,20... | collective-permute-start | bytes 786440 | tf_op jit(solution)/shard_map/ppermute | solution.py:318
  23.9 11.7 %collective-permute-start.6 = (f32[4,128,128]{2,1,0:T(8,128)S(1)}, f32[4,128,128]{2,1,0:T(8,128)S(1)}, u32[]{:S(2)}, u32[]{:S(2)}) collective-permute-start(f32[4,128,128]{2,1,0:T(8,128)S(1)} %get-tuple-element.100), channel_id=1, source_target_pairs={{8,16},{16,8},{9,17},{17,9},{10,18},{18,10},{11,19},{19,11},{12,20... | collective-permute-start | bytes 786440 | tf_op jit(solution)/shard_map/ppermute | solution.py:318
  25.0 16.5 %collective-permute-start.4 = (f32[4,128,128]{2,1,0:T(8,128)S(1)}, f32[4,128,128]{2,1,0:T(8,128)S(1)}, u32[]{:S(2)}, u32[]{:S(2)}) collective-permute-start(f32[4,128,128]{2,1,0:T(8,128)S(1)} %get-tuple-element.91), channel_id=1, source_target_pairs={{16,24},{24,16},{8,0},{0,8},{17,25},{25,17},{9,1},{1,9},{18,26},{2... | collective-permute-start | bytes 786440 | tf_op jit(solution)/shard_map/ppermute | solution.py:318
  36.0 8.3 %collective-permute-start.7 = (f32[4,128,128]{2,1,0:T(8,128)S(1)}, f32[4,128,128]{2,1,0:T(8,128)S(1)}, u32[]{:S(2)}, u32[]{:S(2)}) collective-permute-start(f32[4,128,128]{2,1,0:T(8,128)S(1)} %get-tuple-element.103), channel_id=1, source_target_pairs={{16,24},{24,16},{8,0},{0,8},{17,25},{25,17},{9,1},{1,9},{18,26},{2... | collective-permute-start | bytes 786440 | tf_op jit(solution)/shard_map/ppermute | solution.py:318
  46.9 1.2 %collective-permute-start.8 = (f32[8,128]{1,0:T(8,128)S(1)}, f32[8,128]{1,0:T(8,128)S(1)}, u32[]{:S(2)}, u32[]{:S(2)}) collective-permute-start(f32[8,128]{1,0:T(8,128)S(1)} %get-tuple-element.115.refs_9_), channel_id=1, source_target_pairs={{0,1},{1,0},{2,3},{3,2},{4,5},{5,4},{6,7},{7,6},{8,9},{9,8},{10,11... | collective-permute-start | bytes 12296 | tf_op jit(solution)/shard_map/ppermute | solution.py:342
  49.3 5.6 %collective-permute-start.9 = (f32[2,128,128]{2,1,0:T(8,128)S(1)}, f32[2,128,128]{2,1,0:T(8,128)S(1)}, u32[]{:S(2)}, u32[]{:S(2)}) collective-permute-start(f32[2,128,128]{2,1,0:T(8,128)S(1)} %get-tuple-element.118), channel_id=1, source_target_pairs={{0,4},{4,0},{1,5},{5,1},{2,6},{6,2},{3,7},{7,3},{8,12},{12,8},{9,1... | collective-permute-start | bytes 393224 | tf_op jit(solution)/shard_map/ppermute | solution.py:354
  50.8 3.6 %collective-permute-start.10 = (f32[8,128]{1,0:T(8,128)S(1)}, f32[8,128]{1,0:T(8,128)S(1)}, u32[]{:S(2)}, u32[]{:S(2)}) collective-permute-start(f32[8,128]{1,0:T(8,128)S(1)} %get-tuple-element.119.c), channel_id=1, source_target_pairs={{0,8},{8,0},{16,24},{24,16},{1,9},{9,1},{17,25},{25,17},{2,10},{10... | collective-permute-start | bytes 12296 | tf_op jit(solution)/shard_map/ppermute | solution.py:357
  54.9 4.6 %collective-permute-start.11 = (f32[8,128]{1,0:T(8,128)S(1)}, f32[8,128]{1,0:T(8,128)S(1)}, u32[]{:S(2)}, u32[]{:S(2)}) collective-permute-start(f32[8,128]{1,0:T(8,128)S(1)} %get-tuple-element.122), channel_id=1, source_target_pairs={{0,16},{8,24},{16,0},{24,8},{1,17},{9,25},{17,1},{25,9},{2,18},{10... | collective-permute-start | bytes 12296 | tf_op jit(solution)/shard_map/ppermute | solution.py:371
  59.5 3.6 %collective-permute-start.12 = (f32[8,128]{1,0:T(8,128)S(1)}, f32[8,128]{1,0:T(8,128)S(1)}, u32[]{:S(2)}, u32[]{:S(2)}) collective-permute-start(f32[8,128]{1,0:T(8,128)S(1)} %add.6), channel_id=1, source_target_pairs={{0,2},{1,3},{2,0},{3,1},{4,6},{5,7},{6,4},{7,5},{8,10},{9,11},{10,... | collective-permute-start | bytes 12296 | tf_op jit(solution)/shard_map/ppermute | solution.py:371

commit v3 on v2

--- a/solution.py
+++ b/solution.py
@@ -10,7 +10,6 @@
 f32, bf16 = jnp.float32, jnp.bfloat16
 highest = lax.Precision.HIGHEST
 VMEM = pl.BlockSpec(memory_space=pltpu.VMEM)
-SMEM = pl.BlockSpec(memory_space=pltpu.SMEM)
 HBM = pl.BlockSpec(memory_space=pltpu.HBM)
 LIMIT = 48 * 1024 * 1024
 shape = jax.ShapeDtypeStruct
@@ -28,7 +27,7 @@
     return pl.pallas_call(
         body,
         out_shape=outs,
-        in_specs=ins or [SMEM if a.ndim == 1 else VMEM for a in args],
+        in_specs=ins or [VMEM] * len(args),
         out_specs=out_specs or [VMEM] * len(outs),
         scratch_shapes=scratch,
         compiler_params=pltpu.CompilerParams(vmem_limit_bytes=LIMIT),
@@ -43,11 +42,11 @@
 
 
 def head_row(values, width):
-    lanes = lax.broadcasted_iota(jnp.int32, (1, width), 1)
-    row = jnp.zeros((1, width), f32)
-    for h in range(values.shape[0]):
-        row = jnp.where(lanes == h, values[h], row)
-    return row
+    heads = values.shape[1]
+    rows = lax.broadcasted_iota(jnp.int32, (heads, width), 0)
+    cols = lax.broadcasted_iota(jnp.int32, (heads, width), 1)
+    spread = jnp.where(rows == cols, 1.0, 0.0).astype(f32)
+    return jnp.dot(values, spread, precision=highest, preferred_element_type=f32)
 
 
 def steps_of(raw, bias, rate, width):
@@ -59,37 +58,46 @@
     return shifted, dt, jnp.dot(lower, -rate * dt, precision=highest, preferred_element_type=f32)
 
 
-def load_body(x, t, b, c, raw, xv, tv, bv, cv, rawv, own, sems):
-    copies = [
-        pltpu.make_async_copy(src, dst, sems.at[i])
-        for i, (src, dst) in enumerate(((c, cv), (raw, rawv), (b, bv), (x, xv), (t, tv)))
-    ]
+def fetch(pairs, sems):
+    copies = [pltpu.make_async_copy(src, dst, sems.at[i]) for i, (src, dst) in enumerate(pairs)]
     for copy in copies:
         copy.start()
-    copies[0].wait()
-    copies[1].wait()
+    return copies
+
+
+def own_body(c, raw, cv, rawv, own, sems):
+    for copy in fetch(((c, cv), (raw, rawv)), sems):
+        copy.wait()
     size, state = c.shape
     heads = raw.shape[0]
     own[:size, :] = cv[...].astype(f32)
     for s in range(size // state):
         own[size + s * heads : size + (s + 1) * heads, :] = rawv[:, s * state : (s + 1) * state]
-    for copy in copies[2:]:
+
+
+def load_body(*refs):
+    count = len(refs) // 2
+    for copy in fetch(zip(refs[:count], refs[count : 2 * count]), refs[-1]):
         copy.wait()
 
 
 def prepare_body(b, c, raw, a_log, skip, dt_bias, cols_out, low_out, low_t_out, b_t_out, c_t_out, sq_out, rows_out):
     size, width = b.shape
     lanes = lax.broadcasted_iota(jnp.int32, (1, width), 1)
-    rate = jnp.where(lanes < a_log.shape[0], jnp.exp(head_row(a_log, width)), 0.0)
-    bias = head_row(dt_bias, width)
+    rate = jnp.where(lanes < a_log.shape[1], jnp.exp(head_row(a_log[...], width)), 0.0)
+    bias = head_row(dt_bias[...], width)
     shifted, dt, logs = steps_of(raw[...], bias, rate, width)
     mid = 0.5 * logs[size - 1 : size, :]
     cols_out[0] = jnp.exp(logs - mid)
     cols_out[1] = dt * jnp.exp(mid - logs)
     cols_out[2] = dt
-    cols_out[3] = shifted
     half = jnp.exp(mid)
-    rows_out[...] = jnp.concatenate([half, half * half, rate, head_row(skip, width), bias, jnp.zeros((3, width), f32)], axis=0)
+    rows_out[...] = jnp.concatenate([half, half * half, rate, head_row(skip[...], width), bias, jnp.zeros((3, width), f32)], axis=0)
+    sigma = 1.0 / (1.0 + jnp.exp(-shifted))
+    cols_out[3] = sigma
+    cols_out[4] = logs
+    lower = jnp.where(triangle(size, True), 1.0, 0.0).astype(f32)
+    cols_out[5] = jnp.dot(lower, rate * sigma, precision=highest, preferred_element_type=f32)
     sq_out[...] = jnp.exp(2.0 * logs).T
     low_out[...] = jnp.where(triangle(size, True), dot_nt(c[...], b[...]), 0.0).astype(bf16)
     low_t_out[...] = jnp.where(triangle(size, False), dot_nt(b[...], c[...]), 0.0).astype(bf16)
@@ -112,13 +120,12 @@
         p_out[k] = scale * dot(c_t[...], ew)
 
 
-def send_body(f, p, *refs):
-    got, (pay_out, *low_outs) = refs[:-3], refs[-3:] if len(refs) == 4 else refs
-    pay_out[...] = jnp.where(lax.axis_index("ctx") == 0, f[...], p[...])
-    if got:
-        c = got[0][: low_outs[0].shape[0], :].astype(bf16)
-        low_outs[0][...] = c
-        low_outs[1][...] = c.T
+def send_body(chunks, *refs):
+    got, refs = refs[0], refs[1:]
+    first = lax.axis_index("ctx") == 0
+    for f, p, pay in zip(refs[:chunks], refs[chunks : 2 * chunks], refs[2 * chunks :]):
+        pay[...] = jnp.where(first, f[...], p[...])
+    refs[-1][...] = got[...]
 
 
 def own_map_body(c, c_t, sq, m_out):
@@ -127,21 +134,20 @@
         m_out[h] = dot((wide * sq[h : h + 1, :]).astype(bf16), c[...])
 
 
-def later_maps_body(reach, rows, c_first, c_t_first, *refs):
-    later, outs = refs[:reach], refs[reach:]
-    heads, width = outs[0].shape[0], outs[0].shape[2]
-    size = c_first.shape[0]
-    factor = jnp.ones((1, width), f32)
-    for i, (got, out) in enumerate(zip(later, outs)):
-        raw = jnp.concatenate([got[size + s * heads : size + (s + 1) * heads, :] for s in range(size // width)], axis=1)
-        _, _, logs = steps_of(raw, rows[4:5, :], rows[2:3, :], width)
-        c = got[:size, :].astype(bf16) if i else c_first[...]
-        c_t = (c.T if i else c_t_first[...]).astype(f32)
-        sq = jnp.exp(2.0 * logs).T
-        for h in range(heads):
-            added = factor[:, h : h + 1] * dot((c_t * sq[h : h + 1, :]).astype(bf16), c)
-            out[h] = outs[i - 1][h] + added if i else added
-        factor = factor * jnp.exp(2.0 * logs[size - 1 : size, :])
+def later_map_body(rows, got, *refs):
+    before, (mc_out, factor_out) = refs[:-2], refs[-2:]
+    heads, width = mc_out.shape[0], mc_out.shape[2]
+    size = got.shape[0] * width // (width + heads)
+    raw = jnp.concatenate([got[size + s * heads : size + (s + 1) * heads, :] for s in range(size // width)], axis=1)
+    _, _, logs = steps_of(raw, rows[4:5, :], rows[2:3, :], width)
+    c = got[:size, :].astype(bf16)
+    c_t = c.T.astype(f32)
+    sq = jnp.exp(2.0 * logs).T
+    factor = before[1][...] if before else jnp.ones((1, width), f32)
+    for h in range(heads):
+        added = factor[:, h : h + 1] * dot((c_t * sq[h : h + 1, :]).astype(bf16), c)
+        mc_out[h] = before[0][h] + added if before else added
+    factor_out[...] = factor * jnp.exp(2.0 * logs[size - 1 : size, :])
 
 
 def times(m, s):
@@ -204,16 +210,13 @@
         v_out[1] = w_all
         sums_out[...] = jnp.concatenate([ends, skips, jnp.zeros((6, width), f32)], axis=0)
         return
-    count = v_out.shape[0]
-    rate, dt = rows[2:3, :], cols[2]
     last = lax.broadcasted_iota(jnp.int32, (size, width), 0) == size - 1
     grad_logs = v_all - w_all + jnp.where(last, ends, 0.0)
-    upper = jnp.where(triangle(size, False), 1.0, 0.0).astype(f32)
-    log_rate = jnp.dot(upper, grad_logs, precision=highest, preferred_element_type=f32)
-    grad_raw = (w_all / dt - rate * log_rate) / (1.0 + jnp.exp(-cols[3]))
-    v_out[...] = grad_raw.T[:count, :]
-    alog = -rate * jnp.sum(log_rate * dt, axis=0, keepdims=True)
-    bias = jnp.sum(grad_raw, axis=0, keepdims=True)
+    by_step = w_all / cols[2]
+    v_out[0] = grad_logs
+    v_out[1] = by_step
+    alog = jnp.sum(grad_logs * cols[4], axis=0, keepdims=True)
+    bias = jnp.sum(by_step * cols[3] - grad_logs * cols[5], axis=0, keepdims=True)
     sums_out[...] = jnp.concatenate(
         [alog * scales[0], skips * scales[1], bias * scales[0], jnp.zeros((5, width), f32)], axis=0
     )
@@ -228,29 +231,32 @@
     grads_out[1] = grads_in[1] + dot(score, b[...]) + dot_nt(ew[...], s_low[...])
 
 
-def output_body(chunks, *refs):
-    parts = refs[:chunks]
-    sums, sums_got = refs[chunks + 7 : chunks + 9]
-    keep_out, send_out, gx_out, sums_out, grads, sems = refs[chunks + 9 :]
-    sums_out[...] = sums[...] + sums_got[...]
-    per = parts[0].shape[0]
-    copies = [pltpu.make_async_copy(part, gx_out.at[pl.ds(i * per, per)], sems.at[i]) for i, part in enumerate(parts)]
-    for copy in copies:
-        copy.start()
-    project_body(*refs[chunks : chunks + 7], grads)
+def cut_body(grads, *refs):
+    *sums, keep_out, send_out, sums_out = refs
     cut, size = keep_out.shape[1], grads.shape[1]
     upper = lax.axis_index("head") >= lax.axis_size("head") // 2
     for i in range(2):
         grad = grads[i]
         keep_out[i] = jnp.where(upper, grad[size - cut :, :], grad[:cut, :])
         send_out[i] = jnp.where(upper, grad[:cut, :], grad[size - cut :, :])
+    sums_out[...] = sums[0][...] + sums[1][...] if len(sums) > 1 else sums[0][...]
+
+
+def output_body(chunks, *refs):
+    parts, (cols, rows, v), (gx_out, raw_out, sems) = refs[:chunks], refs[chunks : chunks + 3], refs[chunks + 3 :]
+    per, size = parts[0].shape[0], v.shape[1]
+    copies = fetch([(part, gx_out.at[pl.ds(i * per, per)]) for i, part in enumerate(parts)], sems)
+    later = jnp.where(triangle(size, False), 1.0, 0.0).astype(f32)
+    log_rate = jnp.dot(later, v[0], precision=highest, preferred_element_type=f32)
+    raw_out[...] = ((v[1] - rows[2:3, :] * log_rate) * cols[3]).T[: raw_out.shape[0], :]
     for copy in copies:
         copy.wait()
 
 
-def add_body(a, b, c, d, first_out, second_out):
-    first_out[...] = a[...] + b[...]
-    second_out[...] = c[...] + d[...]
+def add_body(*refs):
+    count = len(refs) // 3
+    for a, b, out in zip(refs[:count], refs[count : 2 * count], refs[2 * count :]):
+        out[...] = a[...] + b[...]
 
 
 def on_device(x_heads, target, b_proj, c_proj, dt_raw, a_log, skip_gain, dt_bias):
@@ -265,40 +271,53 @@
     flat = shape((width, size), bf16)
     panel = shape((per, size, channels), f32)
 
-    x, t, b, c, raw, own = call(
-        load_body,
-        [shape(a.shape[1:], a.dtype) for a in (x_heads, target, b_proj, c_proj, dt_raw)]
-        + [shape((size + heads * size // width, width), f32)],
-        *[pltpu.with_memory_space_constraint(a[0], pltpu.HBM) for a in (x_heads, target, b_proj, c_proj, dt_raw)],
-        ins=[HBM] * 5, scratch=[pltpu.SemaphoreType.DMA((5,))], flops=10**6,
+    def held_in_hbm(*arrays):
+        return [pltpu.with_memory_space_constraint(a, pltpu.HBM) for a in arrays]
+
+    def like(*arrays):
+        return [shape(a.shape, a.dtype) for a in arrays]
+
+    shared = held_in_hbm(c_proj[0], dt_raw[0])
+    c, raw, own = call(
+        own_body, like(*shared) + [shape((size + heads * size // width, width), f32)], *shared,
+        ins=[HBM] * 2, scratch=[pltpu.SemaphoreType.DMA((2,))], flops=10**6,
+    )
+    rest = held_in_hbm(a_log[None], skip_gain[None], dt_bias[None], b_proj[0], x_heads[0], target[0])
+    a_log, skip_gain, dt_bias, b, x, t = call(
+        load_body, like(*rest), *rest, ins=[HBM] * 6, scratch=[pltpu.SemaphoreType.DMA((6,))], flops=10**6
     )
     lowest = max(n // 2 - 1, 0)
-    later = []
-    for s in range(1, n - lowest):
-        own = lax.ppermute(own, "ctx", [(i + 1, i) for i in range(lowest, n - s)])
-        later.append(own)
+
+    def down(step, value):
+        return lax.ppermute(value, "ctx", [(i + 1, i) for i in range(lowest, n - step)])
+
+    later = down(1, own)
     cols, low, low_t, b_t, c_t, sq, rows = call(
         prepare_body,
-        [shape((4, size, width), f32), square, square, flat, flat, shape((width, size), f32), shape((8, width), f32)],
+        [shape((6, size, width), f32), square, square, flat, flat, shape((width, size), f32), shape((8, width), f32)],
         b, c, raw, a_log, skip_gain, dt_bias,
     )
     held = []
-    maps = [jnp.zeros(all_states.shape, f32)]
-    for i, group in enumerate(groups):
+    for group in groups:
         f, p, xr, y, err = call(
             functools.partial(first_body, group),
             [states, states, shape(panel.shape, bf16), panel, panel],
             x, t, cols, low, b_t, c_t, rows, flops=4 * 10**8,
         )
-        if i == 0 and later:
-            pay, *lows = call(send_body, [states, shape((size, width), bf16), flat], f, p, later[0])
-        else:
-            (pay,) = call(send_body, [states], f, p)
         zero = jnp.zeros(states.shape, f32)
-        held.append(dict(f=f, p=p, pay=pay, xr=xr, y=y, err=err, s=zero, d=zero))
+        held.append(dict(f=f, p=p, xr=xr, y=y, err=err, s=zero, d=zero))
+    *pays, later = call(
+        functools.partial(send_body, chunks), [states] * chunks + [shape(own.shape, f32)],
+        later, *[h["f"] for h in held], *[h["p"] for h in held],
+    )
+    for h, pay in zip(held, pays):
+        h["pay"] = pay
     (m,) = call(own_map_body, [all_states], c, c_t, sq)
-    if later:
-        maps += call(functools.partial(later_maps_body, len(later)), [all_states] * len(later), rows, *lows, *later)
+    mc, before = jnp.zeros(all_states.shape, f32), ()
+    for step in range(1, n - lowest):
+        if step > 1:
+            later = down(step, later)
+        mc, factor = before = call(later_map_body, [all_states, shape((1, width), f32)], rows, later, *before)
 
     def swap(r):
         pairs = [(r - 1, r), (r, r - 1)]
@@ -313,7 +332,7 @@
             if r > 1:
                 h["pay"], h["s"], h["d"] = call(
                     functools.partial(round_body, groups[i], n, r), [states, states, states],
-                    h["f"], h["p"], m, maps[min(r - 1, len(later))], rows, h["got"], h["s"], h["d"],
+                    h["f"], h["p"], m, mc, rows, h["got"], h["s"], h["d"],
                 )
             h["got"] = lax.ppermute(h["pay"], "ctx", swap(r))
 
@@ -328,34 +347,35 @@
         gx, ew, s_low, a_low, v, total = call(
             functools.partial(last_body, groups[i], scales if final else None),
             [shape(panel.shape, bf16), shape((size, per * channels), bf16)] + [shape((width, per * channels), bf16)] * 2
-            + [shape(raw.shape if final else v.shape, f32), shape((8, width), f32)],
-            x, cols, low, low_t, b, c, rows, h["xr"], h["y"], h["err"], h["f"], maps[-1],
+            + [shape(v.shape, f32), shape((8, width), f32)],
+            x, cols, low, low_t, b, c, rows, h["xr"], h["y"], h["err"], h["f"], mc,
             h.get("got", h["s"]), h["s"], h["d"], v, total, flops=4 * 10**8,
         )
         grad_x.append(gx)
         args = (b, c, h["xr"], ew, s_low, a_low, grads)
-        if not final:
-            (grads,) = call(project_body, [shape(grads.shape, f32)], *args, flops=2 * 10**8)
-    swaps = [(axis, 1 << k) for axis in ("seq", "ctx") for k in reversed(range(lax.axis_size(axis).bit_length() - 1))]
+        (grads,) = call(project_body, [shape(grads.shape, f32)], *args, flops=2 * 10**8)
+    spans = {axis: lax.axis_size(axis) for axis in ("seq", "ctx")}
+    swaps = [(axis, 1 << k) for axis in ("seq", "ctx") for k in range(spans[axis].bit_length() - 1)]
+
+    def swapped(value, axis, by):
+        return lax.ppermute(value, axis, [(i, i ^ by) for i in range(spans[axis])])
+
+    halves, sums = shape((2, cut, width), f32), shape(total.shape, f32)
+    firsts = [total]
     if ("seq", 1) in swaps:
         swaps.remove(("seq", 1))
-        got = lax.ppermute(total, "seq", [(i, i ^ 1) for i in range(lax.axis_size("seq"))])
-    else:
-        got = jnp.zeros(total.shape, f32)
-    halves = shape((2, cut, width), f32)
-    keep, send, grad_x, total = call(
-        functools.partial(output_body, chunks),
-        [halves, halves, shape((heads, size, channels), bf16), shape(total.shape, f32)],
-        *grad_x, *args, total, got, out_specs=[VMEM, VMEM, HBM, VMEM], flops=2 * 10**8,
-        scratch=[pltpu.VMEM(grads.shape, f32), pltpu.SemaphoreType.DMA((chunks,))],
+        firsts.append(swapped(total, "seq", 1))
+    keep, send, total = call(cut_body, [halves, halves, sums], grads, *firsts)
+    grad_x, grad_raw = call(
+        functools.partial(output_body, chunks), [shape((heads, size, channels), bf16), shape(raw.shape, f32)],
+        *grad_x, cols, rows, v, out_specs=[HBM, VMEM], scratch=[pltpu.SemaphoreType.DMA((chunks,))],
     )
     step = parts // 2
     while step >= 1:
         received = lax.ppermute(send, "head", [(i, i ^ step) for i in range(parts)])
         if swaps:
-            axis, by = swaps.pop()
-            got = lax.ppermute(total, axis, [(i, i ^ by) for i in range(lax.axis_size(axis))])
-            keep, total = call(add_body, [shape(keep.shape, f32), shape(total.shape, f32)], keep, received, total, got)
+            got = swapped(total, *swaps.pop())
+            keep, total = call(add_body, [shape(keep.shape, f32), sums], keep, total, received, got)
         else:
             keep = keep + received
         step //= 2
@@ -367,10 +387,9 @@
                 jnp.where(upper, keep[:, :cut], keep[:, cut:]),
             )
     while swaps:
-        axis, by = swaps.pop()
-        total = total + lax.ppermute(total, axis, [(i, i ^ by) for i in range(lax.axis_size(axis))])
+        total = total + swapped(total, *swaps.pop())
     return (
-        grad_x[None], keep[0][None], keep[1][None], v[None],
+        grad_x[None], keep[0][None], keep[1][None], grad_raw[None],
         total[0, :heads], total[1, :heads], total[2, :heads],
     )
 

time: 63.8 us -> 59.7 us (0.936)
  starting transfers between devices: 30.4 us -> 28 us
  waiting for transfers between devices: 16.6 us -> 15.2 us
  local copies, waits for them, and re-layouts: 1.88 us -> 1.22 us
    ppermute x6, starting transfers between devices: 21.5 us -> 19 us  [on_device(): h['got'] = lax.ppermute(h['pay'], 'ctx', swap(r))]
    ppermute x6, waiting for transfers between devices: 5.69 us -> 3.78 us  [the longest x4 3.78 us: swapped(): return lax.ppermute(value, axis, [(i, i ^ by) for i in range(spans[axis])])]
    ppermute x6, waiting for transfers between devices: 10.5 us -> 11.5 us  [on_device(): h['got'] = lax.ppermute(h['pay'], 'ctx', swap(r))]
    unnamed x6 -> x0, local copies, waits for them, and re-layouts: 0.67 us -> none
    pallas_call x17 -> x20, Pallas kernels: 13.8 us -> 14.2 us  [call(): pl.pallas_call(body, out_shape=outs, in_specs=ins or [VMEM] * len(args),...]
  transfers between devices with their start and end apart: 13 -> 13, of which waited for: 9 -> 7; matrix products, arithmetic and copies ran while one was open for 1% -> 1% of each run, Pallas kernels for 14% -> 20%
where the time goes in v3:
time: 59.7 us; the launch traced here: 59.5 us
  starting transfers between devices  28 us (47%)
  waiting for transfers between devices  15.2 us (25%)
  Pallas kernels  14.2 us (24%)
  local copies, waits for them, and re-layouts  1.22 us (2%)
  between operations  0.84 us (1%)
    ppermute x6, starting transfers between devices, on_device(): h['got'] = lax.ppermute(h['pay'], 'ctx', swap(r))  19 us
    pallas_call x20, Pallas kernels, call(): pl.pallas_call(body, out_shape=outs, in_specs=ins or [VMEM] * len(args),...  14.2 us
    ppermute x6, waiting for transfers between devices, on_device(): h['got'] = lax.ppermute(h['pay'], 'ctx', swap(r))  11.5 us
    ppermute x4, starting transfers between devices, swapped(): return lax.ppermute(value, axis, [(i, i ^ by) for i in range(spans[axis])])  6 us
    ppermute x4, waiting for transfers between devices, swapped(): return lax.ppermute(value, axis, [(i, i ^ by) for i in range(spans[axis])])  3.78 us
    ppermute x1, starting transfers between devices, on_device(): received = lax.ppermute(send, 'head', [(i, i ^ step) for i in range(parts)])  1.59 us
    ppermute x2, starting transfers between devices, down(): lax.ppermute(value, 'ctx', [(i + 1, i) for i in range(lowest, n - step)])  1.33 us
  transfers between devices with their start and end apart: 13, of which 7 were waited for; matrix products, arithmetic and copies ran while one was open for 1% of the time, Pallas kernels for 20%

profile of v3, /device:TPU:0, one launch (start us, length us, event | category | flops | bytes accessed | tf_op | source)
XLA Modules:
  0.0 59.5 jit_solution(5780946470751662044)
XLA Ops:
  0.6 0.9 %shard_map.136 = (bf16[256,128]{1,0:T(8,128)(2,1)S(1)}, f32[8,256]{1,0:T(8,128)S(1)}, f32[272,128]{1,0:T(8,128)S(1)}) custom-call(bf16[256,128]{1,0:T(8,128)(2,1)} %bitcast.19, f32[8,256]{1,0:T(8,128)} %bitcast.20), custom_call_target="tpu_custom_call" | custom-call | flops 10 | bytes 256 | tf_op jit(solution)/shard_map/pallas_call | solution.py:27
  1.5 0.7 %collective-permute-start = (f32[272,128]{1,0:T(8,128)S(1)}, f32[272,128]{1,0:T(8,128)S(1)}, u32[]{:S(2)}, u32[]{:S(2)}) collective-permute-start(f32[272,128]{1,0:T(8,128)S(1)} %get-tuple-element.88), channel_id=1, source_target_pairs={{16,8},{24,16},{17,9},{25,17},{18,10},{26,18},{19,11},{27,19},{20,... | collective-permute-start | bytes 417800 | tf_op jit(solution)/shard_map/ppermute | solution.py:292
  2.2 1.3 %shard_map.135 = (f32[1,8]{1,0:T(1,128)S(1)}, f32[1,8]{1,0:T(1,128)S(1)}, f32[1,8]{1,0:T(1,128)S(1)}, bf16[256,128]{1,0:T(8,128)(2,1)S(1)}, bf16[8,256,128]{2,1,...) custom-call(f32[1,8]{1,0:T(1,128)} %bitcast.21, f32[1,8]{1,0:T(1,128)} %bitcast.22, f32[1,8]{1,0:T(1,128)} %bitcast.23, ...), custom_call_target="tpu_custom_call" | custom-call | flops 10 | bytes 256 | tf_op jit(solution)/shard_map/pallas_call | solution.py:27
  3.5 1.0 %shard_map.137 = (f32[6,256,128]{2,1,0:T(8,128)S(1)}, bf16[256,256]{1,0:T(8,128)(2,1)S(1)}, bf16[256,256]{1,0:T(8,128)(2,1)S(1)}, bf16[128,256]{1,0:T(8,128)(2,1...) custom-call(bf16[256,128]{1,0:T(8,128)(2,1)S(1)} %get-tuple-element.71.b.refs_4_, ...), custom_call_target="tpu_custom_call" | custom-call | flops 1000 | bytes 256 | tf_op jit(solution)/shard_map/pallas_call | solution.py:27
  4.5 0.7 %shard_map.139 = (f32[4,128,128]{2,1,0:T(8,128)S(1)}, f32[4,128,128]{2,1,0:T(8,128)S(1)}, bf16[4,256,128]{2,1,0:T(8,128)(2,1)S(1)}, f32[4,256,128]{2,1,0:T(8,128)S(1)}, f32[4,256,128]{2,1,0:T(8,128)S(1)}) custom-call(bf16[8,256,128]{2,1,0:T(8,128)(2,1)S(1)} %get-tuple-element.70.x.refs_0_, bf16[8,256,128]{2,1,0:T(8,128)(2,1)S(1)} %get-tuple-element.81.t, ...), custom_call_target="tpu_custom_call" | custom-call | flops 4000 | bytes 256 | tf_op jit(solution)/shard_map/pallas_call | solution.py:27
  5.2 0.7 %shard_map.138 = (f32[4,128,128]{2,1,0:T(8,128)S(1)}, f32[4,128,128]{2,1,0:T(8,128)S(1)}, bf16[4,256,128]{2,1,0:T(8,128)(2,1)S(1)}, f32[4,256,128]{2,1,0:T(8,128)S(1)}, f32[4,256,128]{2,1,0:T(8,128)S(1)}) custom-call(bf16[8,256,128]{2,1,0:T(8,128)(2,1)S(1)} %get-tuple-element.70.x.refs_0_, bf16[8,256,128]{2,1,0:T(8,128)(2,1)S(1)} %get-tuple-element.81.t, ...), custom_call_target="tpu_custom_call" | custom-call | flops 4000 | bytes 256 | tf_op jit(solution)/shard_map/pallas_call | solution.py:27
  6.0 0.0 collective-permute-done.refs_0_
  6.0 0.1 shard_map.140
  6.1 5.9 %collective-permute-start.2 = (f32[4,128,128]{2,1,0:T(8,128)S(1)}, f32[4,128,128]{2,1,0:T(8,128)S(1)}, u32[]{:S(2)}, u32[]{:S(2)}) collective-permute-start(f32[4,128,128]{2,1,0:T(8,128)S(1)} %get-tuple-element.97), channel_id=1, source_target_pairs={{0,8},{8,0},{24,16},{16,24},{1,9},{9,1},{25,17},{17,25},{2,10},{10... | collective-permute-start | bytes 786440 | tf_op jit(solution)/shard_map/ppermute | solution.py:337
  12.0 0.1 collective-permute-start.5
  12.1 0.7 %collective-permute-start.1 = (f32[272,128]{1,0:T(8,128)S(1)}, f32[272,128]{1,0:T(8,128)S(1)}, u32[]{:S(2)}, u32[]{:S(2)}) collective-permute-start(f32[272,128]{1,0:T(8,128)S(1)} %get-tuple-element.92.got), channel_id=1, source_target_pairs={{16,8},{17,9},{18,10},{19,11},{20,12},{21,13},{22,14},{23,15}} | collective-permute-start | bytes 417800 | tf_op jit(solution)/shard_map/ppermute | solution.py:292
  12.7 0.3 shard_map.143.m
  13.0 1.1 %shard_map.141 = (f32[8,128,128]{2,1,0:T(8,128)S(1)}, f32[1,128]{1,0:T(1,128)S(1)}) custom-call(f32[8,128]{1,0:T(8,128)S(1)} %get-tuple-element.80.rows.refs_6_.refs_3_, f32[272,128]{1,0:T(8,128)S(1)} %get-tuple-element.92.got), custom_call_target="tpu_custom_call" | custom-call | flops 1000 | bytes 256 | tf_op jit(solution)/shard_map/pallas_call | solution.py:27
  14.1 0.0 collective-permute-done.1.got
  14.1 1.2 %shard_map.142 = (f32[8,128,128]{2,1,0:T(8,128)S(1)}, f32[1,128]{1,0:T(1,128)}) custom-call(f32[8,128]{1,0:T(8,128)S(1)} %get-tuple-element.80.rows.refs_6_.refs_3_, f32[272,128]{1,0:T(8,128)S(1)} %collective-permute-done.1.got, f32[8,128,128]{2,1,0:T(8,128)S(1)} %get-tuple-element.93.refs_0_, f32[1,128]{1,0:T(1,128)S(1)} %get-tuple-element.94.refs_1_), custom_call_target="tpu_custom_call" | custom-call | flops 1000 | bytes 256 | tf_op jit(solution)/shard_map/pallas_call | solution.py:27
  15.3 4.0 %collective-permute-done.2.got = f32[4,128,128]{2,1,0:T(8,128)S(1)} collective-permute-done((f32[4,128,128]{2,1,0:T(8,128)S(1)}, f32[4,128,128]{2,1,0:T(8,128)S(1)}, u32[]{:S(2)}, u32[]{:S(2)}) %collective-permute-start.2) | collective-permute-done | bytes 262176 | tf_op jit(solution)/shard_map/ppermute | solution.py:337
  19.2 0.4 shard_map.144
  19.6 0.7 %collective-permute-start.3 = (f32[4,128,128]{2,1,0:T(8,128)S(1)}, f32[4,128,128]{2,1,0:T(8,128)S(1)}, u32[]{:S(2)}, u32[]{:S(2)}) collective-permute-start(f32[4,128,128]{2,1,0:T(8,128)S(1)} %get-tuple-element.98), channel_id=1, source_target_pairs={{8,16},{16,8},{9,17},{17,9},{10,18},{18,10},{11,19},{19,11},{12,20... | collective-permute-start | bytes 786440 | tf_op jit(solution)/shard_map/ppermute | solution.py:337
  20.3 2.7 %collective-permute-done.5.got = f32[4,128,128]{2,1,0:T(8,128)S(1)} collective-permute-done((f32[4,128,128]{2,1,0:T(8,128)S(1)}, f32[4,128,128]{2,1,0:T(8,128)S(1)}, u32[]{:S(2)}, u32[]{:S(2)}) %collective-permute-start.5) | collective-permute-done | bytes 262176 | tf_op jit(solution)/shard_map/ppermute | solution.py:337
  23.0 0.4 shard_map.147
  23.4 0.7 %collective-permute-start.6 = (f32[4,128,128]{2,1,0:T(8,128)S(1)}, f32[4,128,128]{2,1,0:T(8,128)S(1)}, u32[]{:S(2)}, u32[]{:S(2)}) collective-permute-start(f32[4,128,128]{2,1,0:T(8,128)S(1)} %get-tuple-element.109), channel_id=1, source_target_pairs={{8,16},{16,8},{9,17},{17,9},{10,18},{18,10},{11,19},{19,11},{12,20... | collective-permute-start | bytes 786440 | tf_op jit(solution)/shard_map/ppermute | solution.py:337
  24.1 0.0 collective-permute-done.3.got
  24.1 0.4 shard_map.145
  24.5 9.3 %collective-permute-start.4 = (f32[4,128,128]{2,1,0:T(8,128)S(1)}, f32[4,128,128]{2,1,0:T(8,128)S(1)}, u32[]{:S(2)}, u32[]{:S(2)}) collective-permute-start(f32[4,128,128]{2,1,0:T(8,128)S(1)} %get-tuple-element.101), channel_id=1, source_target_pairs={{16,24},{24,16},{8,0},{0,8},{17,25},{25,17},{9,1},{1,9},{18,26},{2... | collective-permute-start | bytes 786440 | tf_op jit(solution)/shard_map/ppermute | solution.py:337
  33.8 0.0 collective-permute-done.6.got
  33.8 0.4 shard_map.148
  34.2 2.4 %collective-permute-start.7 = (f32[4,128,128]{2,1,0:T(8,128)S(1)}, f32[4,128,128]{2,1,0:T(8,128)S(1)}, u32[]{:S(2)}, u32[]{:S(2)}) collective-permute-start(f32[4,128,128]{2,1,0:T(8,128)S(1)} %get-tuple-element.112), channel_id=1, source_target_pairs={{16,24},{24,16},{8,0},{0,8},{17,25},{25,17},{9,1},{1,9},{18,26},{2... | collective-permute-start | bytes 786440 | tf_op jit(solution)/shard_map/ppermute | solution.py:337
  36.6 3.5 %collective-permute-done.4.refs_12_ = f32[4,128,128]{2,1,0:T(8,128)S(1)} collective-permute-done((f32[4,128,128]{2,1,0:T(8,128)S(1)}, f32[4,128,128]{2,1,0:T(8,128)S(1)}, u32[]{:S(2)}, u32[]{:S(2)}) %collective-permute-start.4) | collective-permute-done | bytes 262176 | tf_op jit(solution)/shard_map/ppermute | solution.py:337
  40.1 1.5 %shard_map.146 = (bf16[4,256,128]{2,1,0:T(8,128)(2,1)S(1)}, bf16[256,512]{1,0:T(8,128)(2,1)S(1)}, bf16[128,512]{1,0:T(8,128)(2,1)S(1)}, bf16[128,512]{1,0:T(8,12...) custom-call(bf16[8,256,128]{2,1,0:T(8,128)(2,1)S(1)} %get-tuple-element.70.x.refs_0_, ...), custom_call_target="tpu_custom_call" | custom-call | flops 4000 | bytes 256 | tf_op jit(solution)/shard_map/pallas_call | solution.py:27
  41.7 1.2 %collective-permute-done.7.refs_12_ = f32[4,128,128]{2,1,0:T(8,128)S(1)} collective-permute-done((f32[4,128,128]{2,1,0:T(8,128)S(1)}, f32[4,128,128]{2,1,0:T(8,128)S(1)}, u32[]{:S(2)}, u32[]{:S(2)}) %collective-permute-start.7) | collective-permute-done | bytes 262176 | tf_op jit(solution)/shard_map/ppermute | solution.py:337
  42.9 1.3 %shard_map.149 = (bf16[4,256,128]{2,1,0:T(8,128)(2,1)S(1)}, bf16[256,512]{1,0:T(8,128)(2,1)S(1)}, bf16[128,512]{1,0:T(8,128)(2,1)S(1)}, bf16[128,512]{1,0:T(8,12...) custom-call(bf16[8,256,128]{2,1,0:T(8,128)(2,1)S(1)} %get-tuple-element.70.x.refs_0_, ...), custom_call_target="tpu_custom_call" | custom-call | flops 4000 | bytes 256 | tf_op jit(solution)/shard_map/pallas_call | solution.py:27
  44.2 0.1 collective-permute-start.8
  44.3 0.6 %shard_map.151.grads_in = f32[2,256,128]{2,1,0:T(8,128)S(1)} custom-call(bf16[256,128]{1,0:T(8,128)(2,1)S(1)} %get-tuple-element.71.b.refs_4_, bf16[256,128]{1,0:T(8,128)(2,1)S(1)} %get-tuple-element.72.c.refs_5_, bf16[4,256,128]{2,1,0:T(8,128)(2,1)S(1)} %get-tuple-element.84.refs_7_.xr, bf16[256,512]{1,0:T(8,128)(2,1)S(1)} %get-tuple-element.123.ew, ...), custom_call_target="tpu_custom_call" | custom-call | flops 2000 | bytes 256 | tf_op jit(solution)/shard_map/pallas_call | solution.py:27
  44.9 0.6 %shard_map.152.grads = f32[2,256,128]{2,1,0:T(8,128)S(1)} custom-call(bf16[256,128]{1,0:T(8,128)(2,1)S(1)} %get-tuple-element.71.b.refs_4_, bf16[256,128]{1,0:T(8,128)(2,1)S(1)} %get-tuple-element.72.c.refs_5_, bf16[4,256,128]{2,1,0:T(8,128)(2,1)S(1)} %get-tuple-element.105.refs_7_.xr, bf16[256,512]{1,0:T(8,128)(2,1)S(1)} %get-tuple-element.120.ew, ...), custom_call_target="tpu_custom_call" | custom-call | flops 2000 | bytes 256 | tf_op jit(solution)/shard_map/pallas_call | solution.py:27
  45.5 0.0 collective-permute-done.8.refs_1_
  45.5 1.6 %collective-permute-start.9 = (f32[2,128,128]{2,1,0:T(8,128)S(1)}, f32[2,128,128]{2,1,0:T(8,128)S(1)}, u32[]{:S(2)}, u32[]{:S(2)}) collective-permute-start(f32[2,128,128]{2,1,0:T(8,128)S(1)} %get-tuple-element.129), channel_id=1, source_target_pairs={{0,4},{4,0},{1,5},{5,1},{2,6},{6,2},{3,7},{7,3},{8,12},{12,8},{9,1... | collective-permute-start | bytes 393224 | tf_op jit(solution)/shard_map/ppermute | solution.py:375
  47.1 2.6 %collective-permute-start.10 = (f32[8,128]{1,0:T(8,128)S(1)}, f32[8,128]{1,0:T(8,128)S(1)}, u32[]{:S(2)}, u32[]{:S(2)}) collective-permute-start(f32[8,128]{1,0:T(8,128)S(1)} %get-tuple-element.128.refs_1_), channel_id=1, source_target_pairs={{0,16},{8,24},{16,0},{24,8},{1,17},{9,25},{17,1},{25,9},{2,18},{10... | collective-permute-start | bytes 12296 | tf_op jit(solution)/shard_map/ppermute | solution.py:361
  49.8 1.9 %collective-permute-done.10.refs_3_ = f32[8,128]{1,0:T(8,128)S(1)} collective-permute-done((f32[8,128]{1,0:T(8,128)S(1)}, f32[8,128]{1,0:T(8,128)S(1)}, u32[]{:S(2)}, u32[]{:S(2)}) %collective-permute-start.10) | collective-permute-done | bytes 4128 | tf_op jit(solution)/shard_map/ppermute | solution.py:361
  51.6 0.0 collective-permute-done.9.refs_2_
  51.7 1.8 %collective-permute-start.11 = (f32[8,128]{1,0:T(8,128)S(1)}, f32[8,128]{1,0:T(8,128)S(1)}, u32[]{:S(2)}, u32[]{:S(2)}) collective-permute-start(f32[8,128]{1,0:T(8,128)S(1)} %get-tuple-element.132), channel_id=1, source_target_pairs={{0,8},{8,0},{16,24},{24,16},{1,9},{9,1},{17,25},{25,17},{2,10},{10... | collective-permute-start | bytes 12296 | tf_op jit(solution)/shard_map/ppermute | solution.py:361
  53.5 1.4 %shard_map.150 = (bf16[8,256,128]{2,1,0:T(8,128)(2,1)}, f32[8,256]{1,0:T(8,128)}) custom-call(bf16[4,256,128]{2,1,0:T(8,128)(2,1)S(1)} %get-tuple-element.104.refs_0_, bf16[4,256,128]{2,1,0:T(8,128)(2,1)S(1)} %get-tuple-element.117.refs_1_, f32[6,256,128]{2,1,0:T(8,128)S(1)} %get-tuple-element.77.cols.refs_1_.refs_2_, ...), custom_call_target="tpu_custom_call" | custom-call | flops 1000 | bytes 256 | tf_op jit(solution)/shard_map/pallas_call | solution.py:27
  54.9 0.5 collective-permute-done.11
  55.3 1.5 %collective-permute-start.12 = (f32[8,128]{1,0:T(8,128)S(1)}, f32[8,128]{1,0:T(8,128)S(1)}, u32[]{:S(2)}, u32[]{:S(2)}) collective-permute-start(f32[8,128]{1,0:T(8,128)S(1)} %add.6), channel_id=1, source_target_pairs={{0,2},{1,3},{2,0},{3,1},{4,6},{5,7},{6,4},{7,5},{8,10},{9,11},{10,... | collective-permute-start | bytes 12296 | tf_op jit(solution)/shard_map/ppermute | solution.py:361
  56.8 0.7 %fusion = (f32[1,128,128]{2,1,0:T(8,128)}, f32[1,128,128]{2,1,0:T(8,128)}) fusion(f32[2,128,128]{2,1,0:T(8,128)S(1)} %get-tuple-element.130), kind=kLoop, calls=%fused_computation.3 | loop fusion | bytes 262144 | tf_op jit(solution)/shard_map/slice | solution.py:392
  57.5 1.5 %collective-permute-done.12 = f32[8,128]{1,0:T(8,128)S(1)} collective-permute-done((f32[8,128]{1,0:T(8,128)S(1)}, f32[8,128]{1,0:T(8,128)S(1)}, u32[]{:S(2)}, u32[]{:S(2)}) %collective-permute-start.12) | collective-permute-done | bytes 4128 | tf_op jit(solution)/shard_map/ppermute | solution.py:361
  59.0 0.5 slice_bitcast_fusion
  (7 shorter events, 0.1 us)
Async XLA Ops:
  1.5 4.5 %collective-permute-start = (f32[272,128]{1,0:T(8,128)S(1)}, f32[272,128]{1,0:T(8,128)S(1)}, u32[]{:S(2)}, u32[]{:S(2)}) collective-permute-start(f32[272,128]{1,0:T(8,128)S(1)} %get-tuple-element.88), channel_id=1, source_target_pairs={{16,8},{24,16},{17,9},{25,17},{18,10},{26,18},{19,11},{27,19},{20,... | collective-permute-start | bytes 417800 | tf_op jit(solution)/shard_map/ppermute | solution.py:292
  6.1 13.2 %collective-permute-start.2 = (f32[4,128,128]{2,1,0:T(8,128)S(1)}, f32[4,128,128]{2,1,0:T(8,128)S(1)}, u32[]{:S(2)}, u32[]{:S(2)}) collective-permute-start(f32[4,128,128]{2,1,0:T(8,128)S(1)} %get-tuple-element.97), channel_id=1, source_target_pairs={{0,8},{8,0},{24,16},{16,24},{1,9},{9,1},{25,17},{17,25},{2,10},{10... | collective-permute-start | bytes 786440 | tf_op jit(solution)/shard_map/ppermute | solution.py:337
  12.0 11.1 %collective-permute-start.5 = (f32[4,128,128]{2,1,0:T(8,128)S(1)}, f32[4,128,128]{2,1,0:T(8,128)S(1)}, u32[]{:S(2)}, u32[]{:S(2)}) collective-permute-start(f32[4,128,128]{2,1,0:T(8,128)S(1)} %get-tuple-element.108), channel_id=1, source_target_pairs={{0,8},{8,0},{24,16},{16,24},{1,9},{9,1},{25,17},{17,25},{2,10},{10... | collective-permute-start | bytes 786440 | tf_op jit(solution)/shard_map/ppermute | solution.py:337
  12.1 2.0 %collective-permute-start.1 = (f32[272,128]{1,0:T(8,128)S(1)}, f32[272,128]{1,0:T(8,128)S(1)}, u32[]{:S(2)}, u32[]{:S(2)}) collective-permute-start(f32[272,128]{1,0:T(8,128)S(1)} %get-tuple-element.92.got), channel_id=1, source_target_pairs={{16,8},{17,9},{18,10},{19,11},{20,12},{21,13},{22,14},{23,15}} | collective-permute-start | bytes 417800 | tf_op jit(solution)/shard_map/ppermute | solution.py:292
  19.6 4.5 %collective-permute-start.3 = (f32[4,128,128]{2,1,0:T(8,128)S(1)}, f32[4,128,128]{2,1,0:T(8,128)S(1)}, u32[]{:S(2)}, u32[]{:S(2)}) collective-permute-start(f32[4,128,128]{2,1,0:T(8,128)S(1)} %get-tuple-element.98), channel_id=1, source_target_pairs={{8,16},{16,8},{9,17},{17,9},{10,18},{18,10},{11,19},{19,11},{12,20... | collective-permute-start | bytes 786440 | tf_op jit(solution)/shard_map/ppermute | solution.py:337
  23.4 10.3 %collective-permute-start.6 = (f32[4,128,128]{2,1,0:T(8,128)S(1)}, f32[4,128,128]{2,1,0:T(8,128)S(1)}, u32[]{:S(2)}, u32[]{:S(2)}) collective-permute-start(f32[4,128,128]{2,1,0:T(8,128)S(1)} %get-tuple-element.109), channel_id=1, source_target_pairs={{8,16},{16,8},{9,17},{17,9},{10,18},{18,10},{11,19},{19,11},{12,20... | collective-permute-start | bytes 786440 | tf_op jit(solution)/shard_map/ppermute | solution.py:337
  24.5 15.6 %collective-permute-start.4 = (f32[4,128,128]{2,1,0:T(8,128)S(1)}, f32[4,128,128]{2,1,0:T(8,128)S(1)}, u32[]{:S(2)}, u32[]{:S(2)}) collective-permute-start(f32[4,128,128]{2,1,0:T(8,128)S(1)} %get-tuple-element.101), channel_id=1, source_target_pairs={{16,24},{24,16},{8,0},{0,8},{17,25},{25,17},{9,1},{1,9},{18,26},{2... | collective-permute-start | bytes 786440 | tf_op jit(solution)/shard_map/ppermute | solution.py:337
  34.2 8.7 %collective-permute-start.7 = (f32[4,128,128]{2,1,0:T(8,128)S(1)}, f32[4,128,128]{2,1,0:T(8,128)S(1)}, u32[]{:S(2)}, u32[]{:S(2)}) collective-permute-start(f32[4,128,128]{2,1,0:T(8,128)S(1)} %get-tuple-element.112), channel_id=1, source_target_pairs={{16,24},{24,16},{8,0},{0,8},{17,25},{25,17},{9,1},{1,9},{18,26},{2... | collective-permute-start | bytes 786440 | tf_op jit(solution)/shard_map/ppermute | solution.py:337
  44.2 1.3 %collective-permute-start.8 = (f32[8,128]{1,0:T(8,128)S(1)}, f32[8,128]{1,0:T(8,128)S(1)}, u32[]{:S(2)}, u32[]{:S(2)}) collective-permute-start(f32[8,128]{1,0:T(8,128)S(1)} %get-tuple-element.126.refs_0_), channel_id=1, source_target_pairs={{0,1},{1,0},{2,3},{3,2},{4,5},{5,4},{6,7},{7,6},{8,9},{9,8},{10,11... | collective-permute-start | bytes 12296 | tf_op jit(solution)/shard_map/ppermute | solution.py:361
  45.5 6.1 %collective-permute-start.9 = (f32[2,128,128]{2,1,0:T(8,128)S(1)}, f32[2,128,128]{2,1,0:T(8,128)S(1)}, u32[]{:S(2)}, u32[]{:S(2)}) collective-permute-start(f32[2,128,128]{2,1,0:T(8,128)S(1)} %get-tuple-element.129), channel_id=1, source_target_pairs={{0,4},{4,0},{1,5},{5,1},{2,6},{6,2},{3,7},{7,3},{8,12},{12,8},{9,1... | collective-permute-start | bytes 393224 | tf_op jit(solution)/shard_map/ppermute | solution.py:375
  47.1 4.5 %collective-permute-start.10 = (f32[8,128]{1,0:T(8,128)S(1)}, f32[8,128]{1,0:T(8,128)S(1)}, u32[]{:S(2)}, u32[]{:S(2)}) collective-permute-start(f32[8,128]{1,0:T(8,128)S(1)} %get-tuple-element.128.refs_1_), channel_id=1, source_target_pairs={{0,16},{8,24},{16,0},{24,8},{1,17},{9,25},{17,1},{25,9},{2,18},{10... | collective-permute-start | bytes 12296 | tf_op jit(solution)/shard_map/ppermute | solution.py:361
  51.7 3.7 %collective-permute-start.11 = (f32[8,128]{1,0:T(8,128)S(1)}, f32[8,128]{1,0:T(8,128)S(1)}, u32[]{:S(2)}, u32[]{:S(2)}) collective-permute-start(f32[8,128]{1,0:T(8,128)S(1)} %get-tuple-element.132), channel_id=1, source_target_pairs={{0,8},{8,0},{16,24},{24,16},{1,9},{9,1},{17,25},{25,17},{2,10},{10... | collective-permute-start | bytes 12296 | tf_op jit(solution)/shard_map/ppermute | solution.py:361
  55.3 3.6 %collective-permute-start.12 = (f32[8,128]{1,0:T(8,128)S(1)}, f32[8,128]{1,0:T(8,128)S(1)}, u32[]{:S(2)}, u32[]{:S(2)}) collective-permute-start(f32[8,128]{1,0:T(8,128)S(1)} %add.6), channel_id=1, source_target_pairs={{0,2},{1,3},{2,0},{3,1},{4,6},{5,7},{6,4},{7,5},{8,10},{9,11},{10,... | collective-permute-start | bytes 12296 | tf_op jit(solution)/shard_map/ppermute | solution.py:361

commit v4 on v3

--- a/solution.py
+++ b/solution.py
@@ -134,13 +134,15 @@
         m_out[h] = dot((wide * sq[h : h + 1, :]).astype(bf16), c[...])
 
 
-def later_map_body(rows, got, *refs):
+def later_map_body(step, lowest, rows, got, *refs):
     before, (mc_out, factor_out) = refs[:-2], refs[-2:]
     heads, width = mc_out.shape[0], mc_out.shape[2]
     size = got.shape[0] * width // (width + heads)
+    n, place = lax.axis_size("ctx"), lax.axis_index("ctx")
+    needed = (place >= lowest) & (place < n - step)
     raw = jnp.concatenate([got[size + s * heads : size + (s + 1) * heads, :] for s in range(size // width)], axis=1)
     _, _, logs = steps_of(raw, rows[4:5, :], rows[2:3, :], width)
-    c = got[:size, :].astype(bf16)
+    c = jnp.where(needed, got[:size, :], 0.0).astype(bf16)
     c_t = c.T.astype(f32)
     sq = jnp.exp(2.0 * logs).T
     factor = before[1][...] if before else jnp.ones((1, width), f32)
@@ -288,10 +290,18 @@
     )
     lowest = max(n // 2 - 1, 0)
 
+    def exchange(value, links):
+        to, width = dict(links), lax.axis_size("seq")
+        if width % 2:
+            return lax.ppermute(value, "ctx", links)
+        places = [(i, j) for i in range(n) for j in range(width)]
+        pairs = [(i * width + j, to[i] * width + j if i in to else i * width + (j ^ 1)) for i, j in places]
+        return lax.ppermute(value, ("ctx", "seq"), pairs)
+
     def down(step, value):
-        return lax.ppermute(value, "ctx", [(i + 1, i) for i in range(lowest, n - step)])
-
-    later = down(1, own)
+        return exchange(value, [(i + 1, i) for i in range(lowest, n - step)] + [(lowest, n - step)])
+
+    later = down(1, own) if n > 1 else own
     cols, low, low_t, b_t, c_t, sq, rows = call(
         prepare_body,
         [shape((6, size, width), f32), square, square, flat, flat, shape((width, size), f32), shape((8, width), f32)],
@@ -317,7 +327,7 @@
     for step in range(1, n - lowest):
         if step > 1:
             later = down(step, later)
-        mc, factor = before = call(later_map_body, [all_states, shape((1, width), f32)], rows, later, *before)
+        mc, factor = before = call(functools.partial(later_map_body, step, lowest), [all_states, shape((1, width), f32)], rows, later, *before)
 
     def swap(r):
         pairs = [(r - 1, r), (r, r - 1)]
@@ -334,7 +344,7 @@
                     functools.partial(round_body, groups[i], n, r), [states, states, states],
                     h["f"], h["p"], m, mc, rows, h["got"], h["s"], h["d"],
                 )
-            h["got"] = lax.ppermute(h["pay"], "ctx", swap(r))
+            h["got"] = exchange(h["pay"], swap(r))
 
     tokens = size * n * x_heads.shape[0] * lax.axis_size("seq")
     scales = (1.0 / tokens, 1.0 / (tokens * channels))

time: 59.7 us -> 55.5 us (0.930)
  starting transfers between devices: 28 us -> 23.3 us
  waiting for transfers between devices: 15.2 us -> 15.8 us
    ppermute x8, starting transfers between devices: 20.4 us -> 15.2 us  [exchange(): return lax.ppermute(value, ('ctx', 'seq'), pairs)]
    ppermute x8, waiting for transfers between devices: 11.5 us -> 12.3 us  [exchange(): return lax.ppermute(value, ('ctx', 'seq'), pairs)]
  transfers between devices with their start and end apart: 13 -> 13, of which waited for: 7 -> 6; matrix products, arithmetic and copies ran while one was open for 1% -> 1% of each run, Pallas kernels for 20% -> 22%
where the time goes in v4:
time: 55.5 us; the launch traced here: 55.4 us
  starting transfers between devices  23.3 us (42%)
  waiting for transfers between devices  15.8 us (28%)
  Pallas kernels  14.2 us (26%)
  local copies, waits for them, and re-layouts  1.22 us (2%)
  between operations  0.82 us (1%)
    ppermute x8, starting transfers between devices, exchange(): return lax.ppermute(value, ('ctx', 'seq'), pairs)  15.2 us
    pallas_call x20, Pallas kernels, call(): pl.pallas_call(body, out_shape=outs, in_specs=ins or [VMEM] * len(args),...  14.2 us
    ppermute x8, waiting for transfers between devices, exchange(): return lax.ppermute(value, ('ctx', 'seq'), pairs)  12.3 us
    ppermute x4, starting transfers between devices, swapped(): return lax.ppermute(value, axis, [(i, i ^ by) for i in range(spans[axis])])  6.56 us
    ppermute x4, waiting for transfers between devices, swapped(): return lax.ppermute(value, axis, [(i, i ^ by) for i in range(spans[axis])])  3.51 us
    ppermute x1, starting transfers between devices, on_device(): received = lax.ppermute(send, 'head', [(i, i ^ step) for i in range(parts)])  1.58 us
  transfers between devices with their start and end apart: 13, of which 6 were waited for; matrix products, arithmetic and copies ran while one was open for 1% of the time, Pallas kernels for 22%

profile of v4, /device:TPU:0, one launch (start us, length us, event | category | flops | bytes accessed | tf_op | source)
XLA Modules:
  0.0 55.4 jit_solution(8490640966487855786)
XLA Ops:
  0.6 0.9 %shard_map.136 = (bf16[256,128]{1,0:T(8,128)(2,1)S(1)}, f32[8,256]{1,0:T(8,128)S(1)}, f32[272,128]{1,0:T(8,128)S(1)}) custom-call(bf16[256,128]{1,0:T(8,128)(2,1)} %bitcast.19, f32[8,256]{1,0:T(8,128)} %bitcast.20), custom_call_target="tpu_custom_call" | custom-call | flops 10 | bytes 256 | tf_op jit(solution)/shard_map/pallas_call | solution.py:27
  1.5 0.5 collective-permute-start
  2.0 1.3 %shard_map.135 = (f32[1,8]{1,0:T(1,128)S(1)}, f32[1,8]{1,0:T(1,128)S(1)}, f32[1,8]{1,0:T(1,128)S(1)}, bf16[256,128]{1,0:T(8,128)(2,1)S(1)}, bf16[8,256,128]{2,1,...) custom-call(f32[1,8]{1,0:T(1,128)} %bitcast.21, f32[1,8]{1,0:T(1,128)} %bitcast.22, f32[1,8]{1,0:T(1,128)} %bitcast.23, ...), custom_call_target="tpu_custom_call" | custom-call | flops 10 | bytes 256 | tf_op jit(solution)/shard_map/pallas_call | solution.py:27
  3.4 1.0 %shard_map.137 = (f32[6,256,128]{2,1,0:T(8,128)S(1)}, bf16[256,256]{1,0:T(8,128)(2,1)S(1)}, bf16[256,256]{1,0:T(8,128)(2,1)S(1)}, bf16[128,256]{1,0:T(8,128)(2,1...) custom-call(bf16[256,128]{1,0:T(8,128)(2,1)S(1)} %get-tuple-element.71.b.refs_4_, ...), custom_call_target="tpu_custom_call" | custom-call | flops 1000 | bytes 256 | tf_op jit(solution)/shard_map/pallas_call | solution.py:27
  4.4 0.7 %shard_map.139 = (f32[4,128,128]{2,1,0:T(8,128)S(1)}, f32[4,128,128]{2,1,0:T(8,128)S(1)}, bf16[4,256,128]{2,1,0:T(8,128)(2,1)S(1)}, f32[4,256,128]{2,1,0:T(8,128)S(1)}, f32[4,256,128]{2,1,0:T(8,128)S(1)}) custom-call(bf16[8,256,128]{2,1,0:T(8,128)(2,1)S(1)} %get-tuple-element.70.x.refs_0_, bf16[8,256,128]{2,1,0:T(8,128)(2,1)S(1)} %get-tuple-element.81.t, ...), custom_call_target="tpu_custom_call" | custom-call | flops 4000 | bytes 256 | tf_op jit(solution)/shard_map/pallas_call | solution.py:27
  5.1 0.7 %shard_map.138 = (f32[4,128,128]{2,1,0:T(8,128)S(1)}, f32[4,128,128]{2,1,0:T(8,128)S(1)}, bf16[4,256,128]{2,1,0:T(8,128)(2,1)S(1)}, f32[4,256,128]{2,1,0:T(8,128)S(1)}, f32[4,256,128]{2,1,0:T(8,128)S(1)}) custom-call(bf16[8,256,128]{2,1,0:T(8,128)(2,1)S(1)} %get-tuple-element.70.x.refs_0_, bf16[8,256,128]{2,1,0:T(8,128)(2,1)S(1)} %get-tuple-element.81.t, ...), custom_call_target="tpu_custom_call" | custom-call | flops 4000 | bytes 256 | tf_op jit(solution)/shard_map/pallas_call | solution.py:27
  5.8 0.0 collective-permute-done.refs_0_
  5.8 0.1 shard_map.140
  5.9 5.2 %collective-permute-start.2 = (f32[4,128,128]{2,1,0:T(8,128)S(1)}, f32[4,128,128]{2,1,0:T(8,128)S(1)}, u32[]{:S(2)}, u32[]{:S(2)}) collective-permute-start(f32[4,128,128]{2,1,0:T(8,128)S(1)} %get-tuple-element.97), channel_id=1, source_target_pairs={{0,8},{1,9},{2,10},{3,11},{8,0},{9,1},{10,2},{11,3},{16,24},{17,25... | collective-permute-start | bytes 786440 | tf_op jit(solution)/shard_map/ppermute | solution.py:299
  11.1 0.1 collective-permute-start.5
  11.2 0.0 collective-permute-start.1
  11.2 0.3 shard_map.143.m
  11.5 1.1 %shard_map.141 = (f32[8,128,128]{2,1,0:T(8,128)S(1)}, f32[1,128]{1,0:T(1,128)S(1)}) custom-call(f32[8,128]{1,0:T(8,128)S(1)} %get-tuple-element.80.rows.refs_6_.refs_3_, f32[272,128]{1,0:T(8,128)S(1)} %get-tuple-element.92.got), custom_call_target="tpu_custom_call" | custom-call | flops 1000 | bytes 256 | tf_op jit(solution)/shard_map/pallas_call | solution.py:27
  12.5 0.0 collective-permute-done.1.got
  12.6 1.2 %shard_map.142 = (f32[8,128,128]{2,1,0:T(8,128)S(1)}, f32[1,128]{1,0:T(1,128)}) custom-call(f32[8,128]{1,0:T(8,128)S(1)} %get-tuple-element.80.rows.refs_6_.refs_3_, f32[272,128]{1,0:T(8,128)S(1)} %collective-permute-done.1.got, f32[8,128,128]{2,1,0:T(8,128)S(1)} %get-tuple-element.93.refs_0_, f32[1,128]{1,0:T(1,128)S(1)} %get-tuple-element.94.refs_1_), custom_call_target="tpu_custom_call" | custom-call | flops 1000 | bytes 256 | tf_op jit(solution)/shard_map/pallas_call | solution.py:27
  13.7 4.6 %collective-permute-done.2.got = f32[4,128,128]{2,1,0:T(8,128)S(1)} collective-permute-done((f32[4,128,128]{2,1,0:T(8,128)S(1)}, f32[4,128,128]{2,1,0:T(8,128)S(1)}, u32[]{:S(2)}, u32[]{:S(2)}) %collective-permute-start.2) | collective-permute-done | bytes 262176 | tf_op jit(solution)/shard_map/ppermute | solution.py:299
  18.3 0.4 shard_map.144
  18.7 0.1 collective-permute-start.3
  18.8 4.0 %collective-permute-done.5.got = f32[4,128,128]{2,1,0:T(8,128)S(1)} collective-permute-done((f32[4,128,128]{2,1,0:T(8,128)S(1)}, f32[4,128,128]{2,1,0:T(8,128)S(1)}, u32[]{:S(2)}, u32[]{:S(2)}) %collective-permute-start.5) | collective-permute-done | bytes 262176 | tf_op jit(solution)/shard_map/ppermute | solution.py:299
  22.8 0.4 shard_map.147
  23.1 0.1 collective-permute-start.6
  23.2 0.0 collective-permute-done.3.got
  23.2 0.4 shard_map.145
  23.6 4.9 %collective-permute-start.4 = (f32[4,128,128]{2,1,0:T(8,128)S(1)}, f32[4,128,128]{2,1,0:T(8,128)S(1)}, u32[]{:S(2)}, u32[]{:S(2)}) collective-permute-start(f32[4,128,128]{2,1,0:T(8,128)S(1)} %get-tuple-element.101), channel_id=1, source_target_pairs={{0,8},{1,9},{2,10},{3,11},{8,0},{9,1},{10,2},{11,3},{16,24},{17,25... | collective-permute-start | bytes 786440 | tf_op jit(solution)/shard_map/ppermute | solution.py:299
  28.6 0.0 collective-permute-done.6.got
  28.6 0.4 shard_map.148
  29.0 4.3 %collective-permute-start.7 = (f32[4,128,128]{2,1,0:T(8,128)S(1)}, f32[4,128,128]{2,1,0:T(8,128)S(1)}, u32[]{:S(2)}, u32[]{:S(2)}) collective-permute-start(f32[4,128,128]{2,1,0:T(8,128)S(1)} %get-tuple-element.112), channel_id=1, source_target_pairs={{0,8},{1,9},{2,10},{3,11},{8,0},{9,1},{10,2},{11,3},{16,24},{17,25... | collective-permute-start | bytes 786440 | tf_op jit(solution)/shard_map/ppermute | solution.py:299
  33.3 0.0 collective-permute-done.4.refs_12_
  33.3 1.5 %shard_map.146 = (bf16[4,256,128]{2,1,0:T(8,128)(2,1)S(1)}, bf16[256,512]{1,0:T(8,128)(2,1)S(1)}, bf16[128,512]{1,0:T(8,128)(2,1)S(1)}, bf16[128,512]{1,0:T(8,12...) custom-call(bf16[8,256,128]{2,1,0:T(8,128)(2,1)S(1)} %get-tuple-element.70.x.refs_0_, ...), custom_call_target="tpu_custom_call" | custom-call | flops 4000 | bytes 256 | tf_op jit(solution)/shard_map/pallas_call | solution.py:27
  34.8 3.7 %collective-permute-done.7.refs_12_ = f32[4,128,128]{2,1,0:T(8,128)S(1)} collective-permute-done((f32[4,128,128]{2,1,0:T(8,128)S(1)}, f32[4,128,128]{2,1,0:T(8,128)S(1)}, u32[]{:S(2)}, u32[]{:S(2)}) %collective-permute-start.7) | collective-permute-done | bytes 262176 | tf_op jit(solution)/shard_map/ppermute | solution.py:299
  38.5 1.3 %shard_map.149 = (bf16[4,256,128]{2,1,0:T(8,128)(2,1)S(1)}, bf16[256,512]{1,0:T(8,128)(2,1)S(1)}, bf16[128,512]{1,0:T(8,128)(2,1)S(1)}, bf16[128,512]{1,0:T(8,12...) custom-call(bf16[8,256,128]{2,1,0:T(8,128)(2,1)S(1)} %get-tuple-element.70.x.refs_0_, ...), custom_call_target="tpu_custom_call" | custom-call | flops 4000 | bytes 256 | tf_op jit(solution)/shard_map/pallas_call | solution.py:27
  39.8 0.1 collective-permute-start.8
  39.9 0.6 %shard_map.151.grads_in = f32[2,256,128]{2,1,0:T(8,128)S(1)} custom-call(bf16[256,128]{1,0:T(8,128)(2,1)S(1)} %get-tuple-element.71.b.refs_4_, bf16[256,128]{1,0:T(8,128)(2,1)S(1)} %get-tuple-element.72.c.refs_5_, bf16[4,256,128]{2,1,0:T(8,128)(2,1)S(1)} %get-tuple-element.84.refs_7_.xr, bf16[256,512]{1,0:T(8,128)(2,1)S(1)} %get-tuple-element.123.ew, ...), custom_call_target="tpu_custom_call" | custom-call | flops 2000 | bytes 256 | tf_op jit(solution)/shard_map/pallas_call | solution.py:27
  40.5 0.6 %shard_map.152.grads = f32[2,256,128]{2,1,0:T(8,128)S(1)} custom-call(bf16[256,128]{1,0:T(8,128)(2,1)S(1)} %get-tuple-element.71.b.refs_4_, bf16[256,128]{1,0:T(8,128)(2,1)S(1)} %get-tuple-element.72.c.refs_5_, bf16[4,256,128]{2,1,0:T(8,128)(2,1)S(1)} %get-tuple-element.105.refs_7_.xr, bf16[256,512]{1,0:T(8,128)(2,1)S(1)} %get-tuple-element.120.ew, ...), custom_call_target="tpu_custom_call" | custom-call | flops 2000 | bytes 256 | tf_op jit(solution)/shard_map/pallas_call | solution.py:27
  41.1 0.0 collective-permute-done.8.refs_1_
  41.1 1.6 %collective-permute-start.9 = (f32[2,128,128]{2,1,0:T(8,128)S(1)}, f32[2,128,128]{2,1,0:T(8,128)S(1)}, u32[]{:S(2)}, u32[]{:S(2)}) collective-permute-start(f32[2,128,128]{2,1,0:T(8,128)S(1)} %get-tuple-element.129), channel_id=1, source_target_pairs={{0,4},{4,0},{1,5},{5,1},{2,6},{6,2},{3,7},{7,3},{8,12},{12,8},{9,1... | collective-permute-start | bytes 393224 | tf_op jit(solution)/shard_map/ppermute | solution.py:385
  42.7 3.2 %collective-permute-start.10 = (f32[8,128]{1,0:T(8,128)S(1)}, f32[8,128]{1,0:T(8,128)S(1)}, u32[]{:S(2)}, u32[]{:S(2)}) collective-permute-start(f32[8,128]{1,0:T(8,128)S(1)} %get-tuple-element.128.refs_1_), channel_id=1, source_target_pairs={{0,16},{8,24},{16,0},{24,8},{1,17},{9,25},{17,1},{25,9},{2,18},{10... | collective-permute-start | bytes 12296 | tf_op jit(solution)/shard_map/ppermute | solution.py:371
  45.9 1.6 %collective-permute-done.10.refs_3_ = f32[8,128]{1,0:T(8,128)S(1)} collective-permute-done((f32[8,128]{1,0:T(8,128)S(1)}, f32[8,128]{1,0:T(8,128)S(1)}, u32[]{:S(2)}, u32[]{:S(2)}) %collective-permute-start.10) | collective-permute-done | bytes 4128 | tf_op jit(solution)/shard_map/ppermute | solution.py:371
  47.5 0.0 collective-permute-done.9.refs_2_
  47.5 1.8 %collective-permute-start.11 = (f32[8,128]{1,0:T(8,128)S(1)}, f32[8,128]{1,0:T(8,128)S(1)}, u32[]{:S(2)}, u32[]{:S(2)}) collective-permute-start(f32[8,128]{1,0:T(8,128)S(1)} %get-tuple-element.132), channel_id=1, source_target_pairs={{0,8},{8,0},{16,24},{24,16},{1,9},{9,1},{17,25},{25,17},{2,10},{10... | collective-permute-start | bytes 12296 | tf_op jit(solution)/shard_map/ppermute | solution.py:371
  49.3 1.4 %shard_map.150 = (bf16[8,256,128]{2,1,0:T(8,128)(2,1)}, f32[8,256]{1,0:T(8,128)}) custom-call(bf16[4,256,128]{2,1,0:T(8,128)(2,1)S(1)} %get-tuple-element.104.refs_0_, bf16[4,256,128]{2,1,0:T(8,128)(2,1)S(1)} %get-tuple-element.117.refs_1_, f32[6,256,128]{2,1,0:T(8,128)S(1)} %get-tuple-element.77.cols.refs_1_.refs_2_, ...), custom_call_target="tpu_custom_call" | custom-call | flops 1000 | bytes 256 | tf_op jit(solution)/shard_map/pallas_call | solution.py:27
  50.8 0.5 collective-permute-done.11
  51.2 1.5 %collective-permute-start.12 = (f32[8,128]{1,0:T(8,128)S(1)}, f32[8,128]{1,0:T(8,128)S(1)}, u32[]{:S(2)}, u32[]{:S(2)}) collective-permute-start(f32[8,128]{1,0:T(8,128)S(1)} %add.6), channel_id=1, source_target_pairs={{0,2},{1,3},{2,0},{3,1},{4,6},{5,7},{6,4},{7,5},{8,10},{9,11},{10,... | collective-permute-start | bytes 12296 | tf_op jit(solution)/shard_map/ppermute | solution.py:371
  52.7 0.7 %fusion = (f32[1,128,128]{2,1,0:T(8,128)}, f32[1,128,128]{2,1,0:T(8,128)}) fusion(f32[2,128,128]{2,1,0:T(8,128)S(1)} %get-tuple-element.130), kind=kLoop, calls=%fused_computation.3 | loop fusion | bytes 262144 | tf_op jit(solution)/shard_map/slice | solution.py:402
  53.4 1.5 %collective-permute-done.12 = f32[8,128]{1,0:T(8,128)S(1)} collective-permute-done((f32[8,128]{1,0:T(8,128)S(1)}, f32[8,128]{1,0:T(8,128)S(1)}, u32[]{:S(2)}, u32[]{:S(2)}) %collective-permute-start.12) | collective-permute-done | bytes 4128 | tf_op jit(solution)/shard_map/ppermute | solution.py:371
  54.8 0.5 slice_bitcast_fusion
  (7 shorter events, 0.1 us)
Async XLA Ops:
  1.5 4.3 %collective-permute-start = (f32[272,128]{1,0:T(8,128)S(1)}, f32[272,128]{1,0:T(8,128)S(1)}, u32[]{:S(2)}, u32[]{:S(2)}) collective-permute-start(f32[272,128]{1,0:T(8,128)S(1)} %get-tuple-element.88), channel_id=1, source_target_pairs={{0,1},{1,0},{2,3},{3,2},{8,24},{9,25},{10,26},{11,27},{16,8},{17,9... | collective-permute-start | bytes 417800 | tf_op jit(solution)/shard_map/ppermute | solution.py:299
  5.9 12.4 %collective-permute-start.2 = (f32[4,128,128]{2,1,0:T(8,128)S(1)}, f32[4,128,128]{2,1,0:T(8,128)S(1)}, u32[]{:S(2)}, u32[]{:S(2)}) collective-permute-start(f32[4,128,128]{2,1,0:T(8,128)S(1)} %get-tuple-element.97), channel_id=1, source_target_pairs={{0,8},{1,9},{2,10},{3,11},{8,0},{9,1},{10,2},{11,3},{16,24},{17,25... | collective-permute-start | bytes 786440 | tf_op jit(solution)/shard_map/ppermute | solution.py:299
  11.1 11.6 %collective-permute-start.5 = (f32[4,128,128]{2,1,0:T(8,128)S(1)}, f32[4,128,128]{2,1,0:T(8,128)S(1)}, u32[]{:S(2)}, u32[]{:S(2)}) collective-permute-start(f32[4,128,128]{2,1,0:T(8,128)S(1)} %get-tuple-element.108), channel_id=1, source_target_pairs={{0,8},{1,9},{2,10},{3,11},{8,0},{9,1},{10,2},{11,3},{16,24},{17,25... | collective-permute-start | bytes 786440 | tf_op jit(solution)/shard_map/ppermute | solution.py:299
  11.2 1.4 %collective-permute-start.1 = (f32[272,128]{1,0:T(8,128)S(1)}, f32[272,128]{1,0:T(8,128)S(1)}, u32[]{:S(2)}, u32[]{:S(2)}) collective-permute-start(f32[272,128]{1,0:T(8,128)S(1)} %get-tuple-element.92.got), channel_id=1, source_target_pairs={{0,1},{1,0},{2,3},{3,2},{8,16},{9,17},{10,18},{11,19},{16,8},{17,9... | collective-permute-start | bytes 417800 | tf_op jit(solution)/shard_map/ppermute | solution.py:299
  18.7 4.5 %collective-permute-start.3 = (f32[4,128,128]{2,1,0:T(8,128)S(1)}, f32[4,128,128]{2,1,0:T(8,128)S(1)}, u32[]{:S(2)}, u32[]{:S(2)}) collective-permute-start(f32[4,128,128]{2,1,0:T(8,128)S(1)} %get-tuple-element.98), channel_id=1, source_target_pairs={{0,1},{1,0},{2,3},{3,2},{8,16},{9,17},{10,18},{11,19},{16,8},{17,9... | collective-permute-start | bytes 786440 | tf_op jit(solution)/shard_map/ppermute | solution.py:299
  23.1 5.4 %collective-permute-start.6 = (f32[4,128,128]{2,1,0:T(8,128)S(1)}, f32[4,128,128]{2,1,0:T(8,128)S(1)}, u32[]{:S(2)}, u32[]{:S(2)}) collective-permute-start(f32[4,128,128]{2,1,0:T(8,128)S(1)} %get-tuple-element.109), channel_id=1, source_target_pairs={{0,1},{1,0},{2,3},{3,2},{8,16},{9,17},{10,18},{11,19},{16,8},{17,9... | collective-permute-start | bytes 786440 | tf_op jit(solution)/shard_map/ppermute | solution.py:299
  23.6 9.7 %collective-permute-start.4 = (f32[4,128,128]{2,1,0:T(8,128)S(1)}, f32[4,128,128]{2,1,0:T(8,128)S(1)}, u32[]{:S(2)}, u32[]{:S(2)}) collective-permute-start(f32[4,128,128]{2,1,0:T(8,128)S(1)} %get-tuple-element.101), channel_id=1, source_target_pairs={{0,8},{1,9},{2,10},{3,11},{8,0},{9,1},{10,2},{11,3},{16,24},{17,25... | collective-permute-start | bytes 786440 | tf_op jit(solution)/shard_map/ppermute | solution.py:299
  29.0 9.6 %collective-permute-start.7 = (f32[4,128,128]{2,1,0:T(8,128)S(1)}, f32[4,128,128]{2,1,0:T(8,128)S(1)}, u32[]{:S(2)}, u32[]{:S(2)}) collective-permute-start(f32[4,128,128]{2,1,0:T(8,128)S(1)} %get-tuple-element.112), channel_id=1, source_target_pairs={{0,8},{1,9},{2,10},{3,11},{8,0},{9,1},{10,2},{11,3},{16,24},{17,25... | collective-permute-start | bytes 786440 | tf_op jit(solution)/shard_map/ppermute | solution.py:299
  39.8 1.3 %collective-permute-start.8 = (f32[8,128]{1,0:T(8,128)S(1)}, f32[8,128]{1,0:T(8,128)S(1)}, u32[]{:S(2)}, u32[]{:S(2)}) collective-permute-start(f32[8,128]{1,0:T(8,128)S(1)} %get-tuple-element.126.refs_0_), channel_id=1, source_target_pairs={{0,1},{1,0},{2,3},{3,2},{4,5},{5,4},{6,7},{7,6},{8,9},{9,8},{10,11... | collective-permute-start | bytes 12296 | tf_op jit(solution)/shard_map/ppermute | solution.py:371
  41.1 6.4 %collective-permute-start.9 = (f32[2,128,128]{2,1,0:T(8,128)S(1)}, f32[2,128,128]{2,1,0:T(8,128)S(1)}, u32[]{:S(2)}, u32[]{:S(2)}) collective-permute-start(f32[2,128,128]{2,1,0:T(8,128)S(1)} %get-tuple-element.129), channel_id=1, source_target_pairs={{0,4},{4,0},{1,5},{5,1},{2,6},{6,2},{3,7},{7,3},{8,12},{12,8},{9,1... | collective-permute-start | bytes 393224 | tf_op jit(solution)/shard_map/ppermute | solution.py:385
  42.7 4.8 %collective-permute-start.10 = (f32[8,128]{1,0:T(8,128)S(1)}, f32[8,128]{1,0:T(8,128)S(1)}, u32[]{:S(2)}, u32[]{:S(2)}) collective-permute-start(f32[8,128]{1,0:T(8,128)S(1)} %get-tuple-element.128.refs_1_), channel_id=1, source_target_pairs={{0,16},{8,24},{16,0},{24,8},{1,17},{9,25},{17,1},{25,9},{2,18},{10... | collective-permute-start | bytes 12296 | tf_op jit(solution)/shard_map/ppermute | solution.py:371
  47.5 3.7 %collective-permute-start.11 = (f32[8,128]{1,0:T(8,128)S(1)}, f32[8,128]{1,0:T(8,128)S(1)}, u32[]{:S(2)}, u32[]{:S(2)}) collective-permute-start(f32[8,128]{1,0:T(8,128)S(1)} %get-tuple-element.132), channel_id=1, source_target_pairs={{0,8},{8,0},{16,24},{24,16},{1,9},{9,1},{17,25},{25,17},{2,10},{10... | collective-permute-start | bytes 12296 | tf_op jit(solution)/shard_map/ppermute | solution.py:371
  51.2 3.6 %collective-permute-start.12 = (f32[8,128]{1,0:T(8,128)S(1)}, f32[8,128]{1,0:T(8,128)S(1)}, u32[]{:S(2)}, u32[]{:S(2)}) collective-permute-start(f32[8,128]{1,0:T(8,128)S(1)} %add.6), channel_id=1, source_target_pairs={{0,2},{1,3},{2,0},{3,1},{4,6},{5,7},{6,4},{7,5},{8,10},{9,11},{10,... | collective-permute-start | bytes 12296 | tf_op jit(solution)/shard_map/ppermute | solution.py:371

commit v5 on v4

--- a/solution.py
+++ b/solution.py
@@ -81,7 +81,7 @@
         copy.wait()
 
 
-def prepare_body(b, c, raw, a_log, skip, dt_bias, cols_out, low_out, low_t_out, b_t_out, c_t_out, sq_out, rows_out):
+def prepare_body(b, c, raw, a_log, skip, dt_bias, cols_out, low_out, low_t_out, b_t_out, c_t_out, sq_out, rows_out, sides_out):
     size, width = b.shape
     lanes = lax.broadcasted_iota(jnp.int32, (1, width), 1)
     rate = jnp.where(lanes < a_log.shape[1], jnp.exp(head_row(a_log[...], width)), 0.0)
@@ -99,6 +99,7 @@
     lower = jnp.where(triangle(size, True), 1.0, 0.0).astype(f32)
     cols_out[5] = jnp.dot(lower, rate * sigma, precision=highest, preferred_element_type=f32)
     sq_out[...] = jnp.exp(2.0 * logs).T
+    sides_out[...] = jnp.concatenate([rate, bias, jnp.zeros((6, width), f32)], axis=0).T
     low_out[...] = jnp.where(triangle(size, True), dot_nt(c[...], b[...]), 0.0).astype(bf16)
     low_t_out[...] = jnp.where(triangle(size, False), dot_nt(b[...], c[...]), 0.0).astype(bf16)
     b_t_out[...] = b[...].T
@@ -120,12 +121,11 @@
         p_out[k] = scale * dot(c_t[...], ew)
 
 
-def send_body(chunks, *refs):
-    got, refs = refs[0], refs[1:]
-    first = lax.axis_index("ctx") == 0
-    for f, p, pay in zip(refs[:chunks], refs[chunks : 2 * chunks], refs[2 * chunks :]):
-        pay[...] = jnp.where(first, f[...], p[...])
-    refs[-1][...] = got[...]
+def send_body(f, p, *refs):
+    count = len(refs) // 2
+    refs[count][...] = jnp.where(lax.axis_index("ctx") == 0, f[...], p[...])
+    for relay, out in zip(refs[:count], refs[count + 1 :]):
+        out[...] = relay[...]
 
 
 def own_map_body(c, c_t, sq, m_out):
@@ -134,22 +134,25 @@
         m_out[h] = dot((wide * sq[h : h + 1, :]).astype(bf16), c[...])
 
 
-def later_map_body(step, lowest, rows, got, *refs):
+def later_map_body(step, lowest, sides, got, *refs):
     before, (mc_out, factor_out) = refs[:-2], refs[-2:]
     heads, width = mc_out.shape[0], mc_out.shape[2]
     size = got.shape[0] * width // (width + heads)
     n, place = lax.axis_size("ctx"), lax.axis_index("ctx")
     needed = (place >= lowest) & (place < n - step)
     raw = jnp.concatenate([got[size + s * heads : size + (s + 1) * heads, :] for s in range(size // width)], axis=1)
-    _, _, logs = steps_of(raw, rows[4:5, :], rows[2:3, :], width)
+    shifted = raw + sides[:heads, 1:2]
+    dt = jnp.maximum(shifted, 0.0) + jnp.log1p(jnp.exp(-jnp.abs(shifted)))
+    upper = jnp.where(triangle(size, False), 1.0, 0.0).astype(f32)
+    logs = jnp.dot(-sides[:heads, 0:1] * dt, upper, precision=highest, preferred_element_type=f32)
     c = jnp.where(needed, got[:size, :], 0.0).astype(bf16)
     c_t = c.T.astype(f32)
-    sq = jnp.exp(2.0 * logs).T
-    factor = before[1][...] if before else jnp.ones((1, width), f32)
+    sq = jnp.exp(2.0 * logs)
+    factor = before[1][:, 0:1] if before else jnp.ones((heads, 1), f32)
     for h in range(heads):
-        added = factor[:, h : h + 1] * dot((c_t * sq[h : h + 1, :]).astype(bf16), c)
+        added = factor[h : h + 1, :] * dot((c_t * sq[h : h + 1, :]).astype(bf16), c)
         mc_out[h] = before[0][h] + added if before else added
-    factor_out[...] = factor * jnp.exp(2.0 * logs[size - 1 : size, :])
+    factor_out[...] = jnp.broadcast_to(factor * sq[:, size - 1 : size], factor_out.shape)
 
 
 def times(m, s):
@@ -159,7 +162,11 @@
     return dot(high, s_low) + dot(low, s_low)
 
 
-def round_body(heads, n, r, f, p, m, mc, rows, got, s_in, d_in, pay_out, s_out, d_out):
+def round_body(heads, n, r, f, p, m, mc, rows, got, s_in, d_in, *refs):
+    relays = (len(refs) - 3) // 2
+    pay_out, s_out, d_out = refs[relays : relays + 3]
+    for relay, out in zip(refs[:relays], refs[relays + 3 :]):
+        out[...] = relay[...]
     place = lax.axis_index("ctx")
     came_up, came_down = place == r - 1, place == n - r
     for k, h in enumerate(heads):
@@ -175,7 +182,7 @@
 
 def last_body(heads, scales, *refs):
     (x, cols, low, low_t, b, c, rows, xr, y_in, err_in, f, mc, got, s_in, d_in, v_in, sums_in) = refs[:17]
-    gx_out, ew_out, s_low_out, a_low_out, v_out, sums_out = refs[17:23]
+    gx_out, ew_out, s_low_out, a_low_out, v_out, sums_out = refs[17:]
     n = lax.axis_size("ctx")
     place = lax.axis_index("ctx")
     size, width = b.shape
@@ -224,13 +231,16 @@
     )
 
 
-def project_body(b, c, xr, ew, s_low, a_low, grads_in, grads_out):
+def project_body(chunks, b, c, *refs):
     size = b.shape[0]
-    wide = jnp.concatenate([xr[k] for k in range(xr.shape[0])], axis=1)
-    score = jnp.where(triangle(size, True), dot_nt(ew[...], wide), 0.0).astype(bf16)
-    score_t = jnp.where(triangle(size, False), dot_nt(wide, ew[...]), 0.0).astype(bf16)
-    grads_out[0] = grads_in[0] + dot(score_t, c[...]) + dot_nt(wide, a_low[...])
-    grads_out[1] = grads_in[1] + dot(score, b[...]) + dot_nt(ew[...], s_low[...])
+    grads_out = refs[-1]
+    parts = [refs[i * chunks : (i + 1) * chunks] for i in range(4)]
+    wide = jnp.concatenate([xr[k] for xr in parts[0] for k in range(xr.shape[0])], axis=1)
+    ew, s_low, a_low = [jnp.concatenate([ref[...] for ref in part], axis=1) for part in parts[1:]]
+    score = jnp.where(triangle(size, True), dot_nt(ew, wide), 0.0).astype(bf16)
+    score_t = jnp.where(triangle(size, False), dot_nt(wide, ew), 0.0).astype(bf16)
+    grads_out[0] = dot(score_t, c[...]) + dot_nt(wide, a_low)
+    grads_out[1] = dot(score, b[...]) + dot_nt(ew, s_low)
 
 
 def cut_body(grads, *refs):
@@ -246,8 +256,10 @@
 
 def output_body(chunks, *refs):
     parts, (cols, rows, v), (gx_out, raw_out, sems) = refs[:chunks], refs[chunks : chunks + 3], refs[chunks + 3 :]
-    per, size = parts[0].shape[0], v.shape[1]
-    copies = fetch([(part, gx_out.at[pl.ds(i * per, per)]) for i, part in enumerate(parts)], sems)
+    size, starts = v.shape[1], [0]
+    for part in parts:
+        starts.append(starts[-1] + part.shape[0])
+    copies = fetch([(part, gx_out.at[pl.ds(start, part.shape[0])]) for part, start in zip(parts, starts)], sems)
     later = jnp.where(triangle(size, False), 1.0, 0.0).astype(f32)
     log_rate = jnp.dot(later, v[0], precision=highest, preferred_element_type=f32)
     raw_out[...] = ((v[1] - rows[2:3, :] * log_rate) * cols[3]).T[: raw_out.shape[0], :]
@@ -266,12 +278,11 @@
     width = b_proj.shape[2]
     n = lax.axis_size("ctx")
     parts = lax.axis_size("head")
-    chunks = CHUNKS if heads % CHUNKS == 0 else 1
-    per = heads // chunks
-    groups = [tuple(range(i * per, (i + 1) * per)) for i in range(chunks)]
-    square, states, all_states = shape((size, size), bf16), shape((per, width, channels), f32), shape((heads, width, width), f32)
+    chunks = min(CHUNKS, heads)
+    starts = [-(-heads * i // chunks) for i in range(chunks + 1)]
+    groups = [tuple(range(start, end)) for start, end in zip(starts, starts[1:])]
+    square, all_states = shape((size, size), bf16), shape((heads, width, width), f32)
     flat = shape((width, size), bf16)
-    panel = shape((per, size, channels), f32)
 
     def held_in_hbm(*arrays):
         return [pltpu.with_memory_space_constraint(a, pltpu.HBM) for a in arrays]
@@ -302,32 +313,40 @@
         return exchange(value, [(i + 1, i) for i in range(lowest, n - step)] + [(lowest, n - step)])
 
     later = down(1, own) if n > 1 else own
-    cols, low, low_t, b_t, c_t, sq, rows = call(
+    cols, low, low_t, b_t, c_t, sq, rows, sides = call(
         prepare_body,
-        [shape((6, size, width), f32), square, square, flat, flat, shape((width, size), f32), shape((8, width), f32)],
+        [shape((6, size, width), f32), square, square, flat, flat, shape((width, size), f32), shape((8, width), f32), shape((width, 8), f32)],
         b, c, raw, a_log, skip_gain, dt_bias,
     )
     held = []
     for group in groups:
+        states, panel = shape((len(group), width, channels), f32), (len(group), size, channels)
         f, p, xr, y, err = call(
             functools.partial(first_body, group),
-            [states, states, shape(panel.shape, bf16), panel, panel],
+            [states, states, shape(panel, bf16), shape(panel, f32), shape(panel, f32)],
             x, t, cols, low, b_t, c_t, rows, flops=4 * 10**8,
         )
         zero = jnp.zeros(states.shape, f32)
         held.append(dict(f=f, p=p, xr=xr, y=y, err=err, s=zero, d=zero))
-    *pays, later = call(
-        functools.partial(send_body, chunks), [states] * chunks + [shape(own.shape, f32)],
-        later, *[h["f"] for h in held], *[h["p"] for h in held],
-    )
-    for h, pay in zip(held, pays):
-        h["pay"] = pay
+    held[0]["pay"], = call(send_body, like(held[0]["f"]), held[0]["f"], held[0]["p"])
     (m,) = call(own_map_body, [all_states], c, c_t, sq)
-    mc, before = jnp.zeros(all_states.shape, f32), ()
-    for step in range(1, n - lowest):
-        if step > 1:
-            later = down(step, later)
-        mc, factor = before = call(functools.partial(later_map_body, step, lowest), [all_states, shape((1, width), f32)], rows, later, *before)
+    for h in held[1:]:
+        h["pay"], later = call(send_body, like(h["f"], later), h["f"], h["p"], later)
+    layouts = [later]
+    for step in range(2, n - lowest):
+        layouts.append(down(step, layouts[-1]))
+
+    def with_map(maps, layout):
+        step = len(maps)
+        mc, factor = call(
+            functools.partial(later_map_body, step, lowest), [all_states, shape((heads, width), f32)], sides, layout,
+            *(maps[-1] if step > 1 else ()),
+        )
+        return maps + [(mc, factor)]
+
+    maps = [(jnp.zeros(all_states.shape, f32), None)]
+    if n > 1:
+        maps = with_map(maps, later)
 
     def swap(r):
         pairs = [(r - 1, r), (r, r - 1)]
@@ -340,30 +359,34 @@
             if not 1 <= r <= n - 1:
                 continue
             if r > 1:
-                h["pay"], h["s"], h["d"] = call(
-                    functools.partial(round_body, groups[i], n, r), [states, states, states],
-                    h["f"], h["p"], m, mc, rows, h["got"], h["s"], h["d"],
+                relays = layouts[1:] if r == 2 and i == 0 else []
+                h["pay"], h["s"], h["d"], *relays = call(
+                    functools.partial(round_body, groups[i], n, r), like(h["f"]) * 3 + like(*relays),
+                    h["f"], h["p"], m, maps[r - 1 if i == 0 and r < len(maps) else -1][0], rows, h["got"], h["s"], h["d"], *relays,
                 )
+                for relay in relays:
+                    maps = with_map(maps, relay)
             h["got"] = exchange(h["pay"], swap(r))
 
     tokens = size * n * x_heads.shape[0] * lax.axis_size("seq")
     scales = (1.0 / tokens, 1.0 / (tokens * channels))
     cut = size if parts == 1 else size // 2
     v, total = jnp.zeros((2, size, width), f32), jnp.zeros((8, width), f32)
-    grads = jnp.zeros((2, size, width), f32)
     grad_x = []
     for i, h in enumerate(held):
         final = i == chunks - 1
-        gx, ew, s_low, a_low, v, total = call(
+        gx, h["ew"], h["s_low"], h["a_low"], v, total = call(
             functools.partial(last_body, groups[i], scales if final else None),
-            [shape(panel.shape, bf16), shape((size, per * channels), bf16)] + [shape((width, per * channels), bf16)] * 2
+            like(h["xr"]) + [shape((extent, len(groups[i]) * channels), bf16) for extent in (size, width, width)]
             + [shape(v.shape, f32), shape((8, width), f32)],
-            x, cols, low, low_t, b, c, rows, h["xr"], h["y"], h["err"], h["f"], mc,
+            x, cols, low, low_t, b, c, rows, h["xr"], h["y"], h["err"], h["f"], maps[-1][0],
             h.get("got", h["s"]), h["s"], h["d"], v, total, flops=4 * 10**8,
         )
         grad_x.append(gx)
-        args = (b, c, h["xr"], ew, s_low, a_low, grads)
-        (grads,) = call(project_body, [shape(grads.shape, f32)], *args, flops=2 * 10**8)
+    (grads,) = call(
+        functools.partial(project_body, chunks), [shape((2, size, width), f32)], b, c,
+        *[h[part] for part in ("xr", "ew", "s_low", "a_low") for h in held], flops=4 * 10**8,
+    )
     spans = {axis: lax.axis_size(axis) for axis in ("seq", "ctx")}
     swaps = [(axis, 1 << k) for axis in ("seq", "ctx") for k in range(spans[axis].bit_length() - 1)]
 

time: 55.5 us -> 54.4 us (0.980)
  starting transfers between devices: 23.3 us -> 21.7 us
  waiting for transfers between devices: 15.8 us -> 17 us
  Pallas kernels: 14.2 us -> 13.5 us
    ppermute x4, waiting for transfers between devices: 3.51 us -> 5.28 us  [swapped(): return lax.ppermute(value, axis, [(i, i ^ by) for i in range(spans[axis])])]
    ppermute x4, starting transfers between devices: 6.56 us -> 4.83 us  [swapped(): return lax.ppermute(value, axis, [(i, i ^ by) for i in range(spans[axis])])]
    pallas_call x20, Pallas kernels: 14.2 us -> 13.5 us  [call(): pl.pallas_call(body, out_shape=outs, in_specs=ins or [VMEM] * len(args),...]
  transfers between devices with their start and end apart: 13 -> 13, of which waited for: 6 -> 7; matrix products, arithmetic and copies ran while one was open for 1% -> 1% of each run, Pallas kernels for 22% -> 21%
where the time goes in v5:
time: 54.4 us; the launch traced here: 54.2 us
  starting transfers between devices  21.7 us (40%)
  waiting for transfers between devices  17 us (31%)
  Pallas kernels  13.5 us (25%)
  local copies, waits for them, and re-layouts  1.22 us (2%)
  between operations  0.82 us (2%)
    ppermute x8, starting transfers between devices, exchange(): return lax.ppermute(value, ('ctx', 'seq'), pairs)  15.3 us
    pallas_call x20, Pallas kernels, call(): pl.pallas_call(body, out_shape=outs, in_specs=ins or [VMEM] * len(args),...  13.5 us
    ppermute x8, waiting for transfers between devices, exchange(): return lax.ppermute(value, ('ctx', 'seq'), pairs)  11.8 us
    ppermute x4, waiting for transfers between devices, swapped(): return lax.ppermute(value, axis, [(i, i ^ by) for i in range(spans[axis])])  5.28 us
    ppermute x4, starting transfers between devices, swapped(): return lax.ppermute(value, axis, [(i, i ^ by) for i in range(spans[axis])])  4.83 us
    ppermute x1, starting transfers between devices, on_device(): received = lax.ppermute(send, 'head', [(i, i ^ step) for i in range(parts)])  1.59 us
  transfers between devices with their start and end apart: 13, of which 7 were waited for; matrix products, arithmetic and copies ran while one was open for 1% of the time, Pallas kernels for 21%

profile of v5, /device:TPU:0, one launch (start us, length us, event | category | flops | bytes accessed | tf_op | source)
XLA Modules:
  0.0 54.2 jit_solution(14790511093364565054)
XLA Ops:
  0.6 0.9 %shard_map.136 = (bf16[256,128]{1,0:T(8,128)(2,1)S(1)}, f32[8,256]{1,0:T(8,128)S(1)}, f32[272,128]{1,0:T(8,128)S(1)}) custom-call(bf16[256,128]{1,0:T(8,128)(2,1)} %bitcast.19, f32[8,256]{1,0:T(8,128)} %bitcast.20), custom_call_target="tpu_custom_call" | custom-call | flops 10 | bytes 256 | tf_op jit(solution)/shard_map/pallas_call | solution.py:27
  1.5 0.5 collective-permute-start
  2.0 1.3 %shard_map.135 = (f32[1,8]{1,0:T(1,128)S(1)}, f32[1,8]{1,0:T(1,128)S(1)}, f32[1,8]{1,0:T(1,128)S(1)}, bf16[256,128]{1,0:T(8,128)(2,1)S(1)}, bf16[8,256,128]{2,1,...) custom-call(f32[1,8]{1,0:T(1,128)} %bitcast.21, f32[1,8]{1,0:T(1,128)} %bitcast.22, f32[1,8]{1,0:T(1,128)} %bitcast.23, ...), custom_call_target="tpu_custom_call" | custom-call | flops 10 | bytes 256 | tf_op jit(solution)/shard_map/pallas_call | solution.py:27
  3.4 1.0 %shard_map.137 = (f32[6,256,128]{2,1,0:T(8,128)S(1)}, bf16[256,256]{1,0:T(8,128)(2,1)S(1)}, bf16[256,256]{1,0:T(8,128)(2,1)S(1)}, bf16[128,256]{1,0:T(8,128)(2,1...) custom-call(bf16[256,128]{1,0:T(8,128)(2,1)S(1)} %get-tuple-element., ...), custom_call_target="tpu_custom_call" | custom-call | flops 1000 | bytes 256 | tf_op jit(solution)/shard_map/pallas_call | solution.py:27
  4.3 0.7 %shard_map.138 = (f32[4,128,128]{2,1,0:T(8,128)S(1)}, f32[4,128,128]{2,1,0:T(8,128)S(1)}, bf16[4,256,128]{2,1,0:T(8,128)(2,1)S(1)}, f32[4,256,128]{2,1,0:T(8,128)S(1)}, f32[4,256,128]{2,1,0:T(8,128)S(1)}) custom-call(bf16[8,256,128]{2,1,0:T(8,128)(2,1)S(1)} %get-tuple-element.71.x.refs_0_, bf16[8,256,128]{2,1,0:T(8,128)(2,1)S(1)} %get-tuple-element.82.t, ...), custom_call_target="tpu_custom_call" | custom-call | flops 4000 | bytes 256 | tf_op jit(solution)/shard_map/pallas_call | solution.py:27
  5.1 5.2 %collective-permute-start.1 = (f32[4,128,128]{2,1,0:T(8,128)S(1)}, f32[4,128,128]{2,1,0:T(8,128)S(1)}, u32[]{:S(2)}, u32[]{:S(2)}) collective-permute-start(f32[4,128,128]{2,1,0:T(8,128)S(1)} %shard_map.143), channel_id=1, source_target_pairs={{0,8},{1,9},{2,10},{3,11},{8,0},{9,1},{10,2},{11,3},{16,24},{17,25... | collective-permute-start | bytes 786440 | tf_op jit(solution)/shard_map/ppermute | solution.py:310
  10.3 0.7 %shard_map.140 = (f32[4,128,128]{2,1,0:T(8,128)S(1)}, f32[4,128,128]{2,1,0:T(8,128)S(1)}, bf16[4,256,128]{2,1,0:T(8,128)(2,1)S(1)}, f32[4,256,128]{2,1,0:T(8,128)S(1)}, f32[4,256,128]{2,1,0:T(8,128)S(1)}) custom-call(bf16[8,256,128]{2,1,0:T(8,128)(2,1)S(1)} %get-tuple-element.71.x.refs_0_, bf16[8,256,128]{2,1,0:T(8,128)(2,1)S(1)} %get-tuple-element.82.t, ...), custom_call_target="tpu_custom_call" | custom-call | flops 4000 | bytes 256 | tf_op jit(solution)/shard_map/pallas_call | solution.py:27
  11.0 0.0 collective-permute-done.refs_0_
  11.1 0.1 collective-permute-start.5
  11.2 0.1 collective-permute-start.2
  11.3 0.3 shard_map.139.m
  11.6 0.8 %shard_map.142 = (f32[8,128,128]{2,1,0:T(8,128)S(1)}, f32[8,128]{1,0:T(8,128)S(1)}) custom-call(f32[128,8]{1,0:T(8,128)S(1)} %get-tuple-element.89.sides, f32[272,128]{1,0:T(8,128)S(1)} %get-tuple-element.95.got), custom_call_target="tpu_custom_call" | custom-call | flops 1000 | bytes 256 | tf_op jit(solution)/shard_map/pallas_call | solution.py:27
  12.3 5.2 %collective-permute-done.1.got = f32[4,128,128]{2,1,0:T(8,128)S(1)} collective-permute-done((f32[4,128,128]{2,1,0:T(8,128)S(1)}, f32[4,128,128]{2,1,0:T(8,128)S(1)}, u32[]{:S(2)}, u32[]{:S(2)}) %collective-permute-start.1) | collective-permute-done | bytes 262176 | tf_op jit(solution)/shard_map/ppermute | solution.py:310
  17.5 0.0 collective-permute-done.2.refs_0_
  17.5 0.4 shard_map.144
  17.9 0.1 collective-permute-start.3
  18.0 1.1 %shard_map.145 = (f32[8,128,128]{2,1,0:T(8,128)S(1)}, f32[8,128]{1,0:T(8,128)}) custom-call(f32[128,8]{1,0:T(8,128)S(1)} %get-tuple-element.89.sides, f32[272,128]{1,0:T(8,128)S(1)} %get-tuple-element.97.got, f32[8,128,128]{2,1,0:T(8,128)S(1)} %get-tuple-element.96.mc.refs_0_, f32[8,128]{1,0:T(8,128)S(1)} %get-tuple-element.98.refs_1_), custom_call_target="tpu_custom_call" | custom-call | flops 1000 | bytes 256 | tf_op jit(solution)/shard_map/pallas_call | solution.py:27
  19.1 2.8 %collective-permute-done.5.got = f32[4,128,128]{2,1,0:T(8,128)S(1)} collective-permute-done((f32[4,128,128]{2,1,0:T(8,128)S(1)}, f32[4,128,128]{2,1,0:T(8,128)S(1)}, u32[]{:S(2)}, u32[]{:S(2)}) %collective-permute-start.5) | collective-permute-done | bytes 262176 | tf_op jit(solution)/shard_map/ppermute | solution.py:310
  22.0 0.4 shard_map.148
  22.4 0.1 collective-permute-start.6
  22.5 0.0 collective-permute-done.3.got
  22.5 0.4 shard_map.146
  22.8 4.9 %collective-permute-start.4 = (f32[4,128,128]{2,1,0:T(8,128)S(1)}, f32[4,128,128]{2,1,0:T(8,128)S(1)}, u32[]{:S(2)}, u32[]{:S(2)}) collective-permute-start(f32[4,128,128]{2,1,0:T(8,128)S(1)} %get-tuple-element.103), channel_id=1, source_target_pairs={{0,8},{1,9},{2,10},{3,11},{8,0},{9,1},{10,2},{11,3},{16,24},{17,25... | collective-permute-start | bytes 786440 | tf_op jit(solution)/shard_map/ppermute | solution.py:310
  27.8 0.0 collective-permute-done.6.got
  27.8 0.4 shard_map.149
  28.2 4.3 %collective-permute-start.7 = (f32[4,128,128]{2,1,0:T(8,128)S(1)}, f32[4,128,128]{2,1,0:T(8,128)S(1)}, u32[]{:S(2)}, u32[]{:S(2)}) collective-permute-start(f32[4,128,128]{2,1,0:T(8,128)S(1)} %get-tuple-element.114), channel_id=1, source_target_pairs={{0,8},{1,9},{2,10},{3,11},{8,0},{9,1},{10,2},{11,3},{16,24},{17,25... | collective-permute-start | bytes 786440 | tf_op jit(solution)/shard_map/ppermute | solution.py:310
  32.5 0.0 collective-permute-done.4.refs_12_
  32.5 1.5 %shard_map.147 = (bf16[4,256,128]{2,1,0:T(8,128)(2,1)S(1)}, bf16[256,512]{1,0:T(8,128)(2,1)S(1)}, bf16[128,512]{1,0:T(8,128)(2,1)S(1)}, bf16[128,512]{1,0:T(8,12...) custom-call(bf16[8,256,128]{2,1,0:T(8,128)(2,1)S(1)} %get-tuple-element.71.x.refs_0_, ...), custom_call_target="tpu_custom_call" | custom-call | flops 4000 | bytes 256 | tf_op jit(solution)/shard_map/pallas_call | solution.py:27
  34.1 3.7 %collective-permute-done.7.refs_12_ = f32[4,128,128]{2,1,0:T(8,128)S(1)} collective-permute-done((f32[4,128,128]{2,1,0:T(8,128)S(1)}, f32[4,128,128]{2,1,0:T(8,128)S(1)}, u32[]{:S(2)}, u32[]{:S(2)}) %collective-permute-start.7) | collective-permute-done | bytes 262176 | tf_op jit(solution)/shard_map/ppermute | solution.py:310
  37.8 1.3 %shard_map.150 = (bf16[4,256,128]{2,1,0:T(8,128)(2,1)S(1)}, bf16[256,512]{1,0:T(8,128)(2,1)S(1)}, bf16[128,512]{1,0:T(8,128)(2,1)S(1)}, bf16[128,512]{1,0:T(8,12...) custom-call(bf16[8,256,128]{2,1,0:T(8,128)(2,1)S(1)} %get-tuple-element.71.x.refs_0_, ...), custom_call_target="tpu_custom_call" | custom-call | flops 4000 | bytes 256 | tf_op jit(solution)/shard_map/pallas_call | solution.py:27
  39.0 0.1 collective-permute-start.8
  39.1 0.8 %shard_map.152.grads = f32[2,256,128]{2,1,0:T(8,128)S(1)} custom-call(bf16[256,128]{1,0:T(8,128)(2,1)S(1)} %get-tuple-element.72.b.refs_4_, bf16[256,128]{1,0:T(8,128)(2,1)S(1)} %get-tuple-element.73.c.refs_5_, bf16[4,256,128]{2,1,0:T(8,128)(2,1)S(1)} %get-tuple-element.85.refs_7_.refs_0_, bf16[4,256,128]{2,1,0:T(8,128)(2,1)S(1)} %get-tuple-element.107.refs_7_.refs_1_, ...), custom_call_target="tpu_custom_call" | custom-call | flops 4000 | bytes 256 | tf_op jit(solution)/shard_map/pallas_call | solution.py:27
  39.9 0.3 collective-permute-done.8.refs_1_
  40.3 1.6 %collective-permute-start.9 = (f32[2,128,128]{2,1,0:T(8,128)S(1)}, f32[2,128,128]{2,1,0:T(8,128)S(1)}, u32[]{:S(2)}, u32[]{:S(2)}) collective-permute-start(f32[2,128,128]{2,1,0:T(8,128)S(1)} %get-tuple-element.131), channel_id=1, source_target_pairs={{0,4},{4,0},{1,5},{5,1},{2,6},{6,2},{3,7},{7,3},{8,12},{12,8},{9,1... | collective-permute-start | bytes 393224 | tf_op jit(solution)/shard_map/ppermute | solution.py:408
  41.9 1.2 %collective-permute-start.10 = (f32[8,128]{1,0:T(8,128)S(1)}, f32[8,128]{1,0:T(8,128)S(1)}, u32[]{:S(2)}, u32[]{:S(2)}) collective-permute-start(f32[8,128]{1,0:T(8,128)S(1)} %get-tuple-element.130.refs_1_), channel_id=1, source_target_pairs={{0,16},{8,24},{16,0},{24,8},{1,17},{9,25},{17,1},{25,9},{2,18},{10... | collective-permute-start | bytes 12296 | tf_op jit(solution)/shard_map/ppermute | solution.py:394
  43.1 3.3 %collective-permute-done.10.refs_3_ = f32[8,128]{1,0:T(8,128)S(1)} collective-permute-done((f32[8,128]{1,0:T(8,128)S(1)}, f32[8,128]{1,0:T(8,128)S(1)}, u32[]{:S(2)}, u32[]{:S(2)}) %collective-permute-start.10) | collective-permute-done | bytes 4128 | tf_op jit(solution)/shard_map/ppermute | solution.py:394
  46.4 0.0 collective-permute-done.9.refs_2_
  46.4 2.1 %collective-permute-start.11 = (f32[8,128]{1,0:T(8,128)S(1)}, f32[8,128]{1,0:T(8,128)S(1)}, u32[]{:S(2)}, u32[]{:S(2)}) collective-permute-start(f32[8,128]{1,0:T(8,128)S(1)} %get-tuple-element.134), channel_id=1, source_target_pairs={{0,8},{8,0},{16,24},{24,16},{1,9},{9,1},{17,25},{25,17},{2,10},{10... | collective-permute-start | bytes 12296 | tf_op jit(solution)/shard_map/ppermute | solution.py:394
  48.5 1.4 %shard_map.151 = (bf16[8,256,128]{2,1,0:T(8,128)(2,1)}, f32[8,256]{1,0:T(8,128)}) custom-call(bf16[4,256,128]{2,1,0:T(8,128)(2,1)S(1)} %get-tuple-element.106.refs_0_, bf16[4,256,128]{2,1,0:T(8,128)(2,1)S(1)} %get-tuple-element.119.refs_1_, f32[6,256,128]{2,1,0:T(8,128)S(1)} %get-tuple-element.78.cols.refs_1_.refs_2_, ...), custom_call_target="tpu_custom_call" | custom-call | flops 1000 | bytes 256 | tf_op jit(solution)/shard_map/pallas_call | solution.py:27
  49.9 0.2 collective-permute-done.11
  50.1 1.5 %collective-permute-start.12 = (f32[8,128]{1,0:T(8,128)S(1)}, f32[8,128]{1,0:T(8,128)S(1)}, u32[]{:S(2)}, u32[]{:S(2)}) collective-permute-start(f32[8,128]{1,0:T(8,128)S(1)} %add.6), channel_id=1, source_target_pairs={{0,2},{1,3},{2,0},{3,1},{4,6},{5,7},{6,4},{7,5},{8,10},{9,11},{10,... | collective-permute-start | bytes 12296 | tf_op jit(solution)/shard_map/ppermute | solution.py:394
  51.6 0.7 %fusion = (f32[1,128,128]{2,1,0:T(8,128)}, f32[1,128,128]{2,1,0:T(8,128)}) fusion(f32[2,128,128]{2,1,0:T(8,128)S(1)} %get-tuple-element.132), kind=kLoop, calls=%fused_computation.3 | loop fusion | bytes 262144 | tf_op jit(solution)/shard_map/slice | solution.py:425
  52.3 1.5 %collective-permute-done.12 = f32[8,128]{1,0:T(8,128)S(1)} collective-permute-done((f32[8,128]{1,0:T(8,128)S(1)}, f32[8,128]{1,0:T(8,128)S(1)}, u32[]{:S(2)}, u32[]{:S(2)}) %collective-permute-start.12) | collective-permute-done | bytes 4128 | tf_op jit(solution)/shard_map/ppermute | solution.py:394
  53.7 0.5 slice_bitcast_fusion
  (9 shorter events, 0.2 us)
Async XLA Ops:
  1.5 9.5 %collective-permute-start = (f32[272,128]{1,0:T(8,128)S(1)}, f32[272,128]{1,0:T(8,128)S(1)}, u32[]{:S(2)}, u32[]{:S(2)}) collective-permute-start(f32[272,128]{1,0:T(8,128)S(1)} %get-tuple-element.94), channel_id=1, source_target_pairs={{0,1},{1,0},{2,3},{3,2},{8,24},{9,25},{10,26},{11,27},{16,8},{17,9... | collective-permute-start | bytes 417800 | tf_op jit(solution)/shard_map/ppermute | solution.py:310
  5.1 12.4 %collective-permute-start.1 = (f32[4,128,128]{2,1,0:T(8,128)S(1)}, f32[4,128,128]{2,1,0:T(8,128)S(1)}, u32[]{:S(2)}, u32[]{:S(2)}) collective-permute-start(f32[4,128,128]{2,1,0:T(8,128)S(1)} %shard_map.143), channel_id=1, source_target_pairs={{0,8},{1,9},{2,10},{3,11},{8,0},{9,1},{10,2},{11,3},{16,24},{17,25... | collective-permute-start | bytes 786440 | tf_op jit(solution)/shard_map/ppermute | solution.py:310
  11.1 10.9 %collective-permute-start.5 = (f32[4,128,128]{2,1,0:T(8,128)S(1)}, f32[4,128,128]{2,1,0:T(8,128)S(1)}, u32[]{:S(2)}, u32[]{:S(2)}) collective-permute-start(f32[4,128,128]{2,1,0:T(8,128)S(1)} %get-tuple-element.110), channel_id=1, source_target_pairs={{0,8},{1,9},{2,10},{3,11},{8,0},{9,1},{10,2},{11,3},{16,24},{17,25... | collective-permute-start | bytes 786440 | tf_op jit(solution)/shard_map/ppermute | solution.py:310
  11.2 6.3 %collective-permute-start.2 = (f32[272,128]{1,0:T(8,128)S(1)}, f32[272,128]{1,0:T(8,128)S(1)}, u32[]{:S(2)}, u32[]{:S(2)}) collective-permute-start(f32[272,128]{1,0:T(8,128)S(1)} %get-tuple-element.95.got), channel_id=1, source_target_pairs={{0,1},{1,0},{2,3},{3,2},{8,16},{9,17},{10,18},{11,19},{16,8},{17,9... | collective-permute-start | bytes 417800 | tf_op jit(solution)/shard_map/ppermute | solution.py:310
  17.9 4.5 %collective-permute-start.3 = (f32[4,128,128]{2,1,0:T(8,128)S(1)}, f32[4,128,128]{2,1,0:T(8,128)S(1)}, u32[]{:S(2)}, u32[]{:S(2)}) collective-permute-start(f32[4,128,128]{2,1,0:T(8,128)S(1)} %get-tuple-element.100), channel_id=1, source_target_pairs={{0,1},{1,0},{2,3},{3,2},{8,16},{9,17},{10,18},{11,19},{16,8},{17,9... | collective-permute-start | bytes 786440 | tf_op jit(solution)/shard_map/ppermute | solution.py:310
  22.4 5.4 %collective-permute-start.6 = (f32[4,128,128]{2,1,0:T(8,128)S(1)}, f32[4,128,128]{2,1,0:T(8,128)S(1)}, u32[]{:S(2)}, u32[]{:S(2)}) collective-permute-start(f32[4,128,128]{2,1,0:T(8,128)S(1)} %get-tuple-element.111), channel_id=1, source_target_pairs={{0,1},{1,0},{2,3},{3,2},{8,16},{9,17},{10,18},{11,19},{16,8},{17,9... | collective-permute-start | bytes 786440 | tf_op jit(solution)/shard_map/ppermute | solution.py:310
  22.8 9.7 %collective-permute-start.4 = (f32[4,128,128]{2,1,0:T(8,128)S(1)}, f32[4,128,128]{2,1,0:T(8,128)S(1)}, u32[]{:S(2)}, u32[]{:S(2)}) collective-permute-start(f32[4,128,128]{2,1,0:T(8,128)S(1)} %get-tuple-element.103), channel_id=1, source_target_pairs={{0,8},{1,9},{2,10},{3,11},{8,0},{9,1},{10,2},{11,3},{16,24},{17,25... | collective-permute-start | bytes 786440 | tf_op jit(solution)/shard_map/ppermute | solution.py:310
  28.2 9.6 %collective-permute-start.7 = (f32[4,128,128]{2,1,0:T(8,128)S(1)}, f32[4,128,128]{2,1,0:T(8,128)S(1)}, u32[]{:S(2)}, u32[]{:S(2)}) collective-permute-start(f32[4,128,128]{2,1,0:T(8,128)S(1)} %get-tuple-element.114), channel_id=1, source_target_pairs={{0,8},{1,9},{2,10},{3,11},{8,0},{9,1},{10,2},{11,3},{16,24},{17,25... | collective-permute-start | bytes 786440 | tf_op jit(solution)/shard_map/ppermute | solution.py:310
  39.0 1.2 %collective-permute-start.8 = (f32[8,128]{1,0:T(8,128)S(1)}, f32[8,128]{1,0:T(8,128)S(1)}, u32[]{:S(2)}, u32[]{:S(2)}) collective-permute-start(f32[8,128]{1,0:T(8,128)S(1)} %get-tuple-element.128.refs_0_), channel_id=1, source_target_pairs={{0,1},{1,0},{2,3},{3,2},{4,5},{5,4},{6,7},{7,6},{8,9},{9,8},{10,11... | collective-permute-start | bytes 12296 | tf_op jit(solution)/shard_map/ppermute | solution.py:394
  40.3 6.1 %collective-permute-start.9 = (f32[2,128,128]{2,1,0:T(8,128)S(1)}, f32[2,128,128]{2,1,0:T(8,128)S(1)}, u32[]{:S(2)}, u32[]{:S(2)}) collective-permute-start(f32[2,128,128]{2,1,0:T(8,128)S(1)} %get-tuple-element.131), channel_id=1, source_target_pairs={{0,4},{4,0},{1,5},{5,1},{2,6},{6,2},{3,7},{7,3},{8,12},{12,8},{9,1... | collective-permute-start | bytes 393224 | tf_op jit(solution)/shard_map/ppermute | solution.py:408
  41.9 4.5 %collective-permute-start.10 = (f32[8,128]{1,0:T(8,128)S(1)}, f32[8,128]{1,0:T(8,128)S(1)}, u32[]{:S(2)}, u32[]{:S(2)}) collective-permute-start(f32[8,128]{1,0:T(8,128)S(1)} %get-tuple-element.130.refs_1_), channel_id=1, source_target_pairs={{0,16},{8,24},{16,0},{24,8},{1,17},{9,25},{17,1},{25,9},{2,18},{10... | collective-permute-start | bytes 12296 | tf_op jit(solution)/shard_map/ppermute | solution.py:394
  46.4 3.7 %collective-permute-start.11 = (f32[8,128]{1,0:T(8,128)S(1)}, f32[8,128]{1,0:T(8,128)S(1)}, u32[]{:S(2)}, u32[]{:S(2)}) collective-permute-start(f32[8,128]{1,0:T(8,128)S(1)} %get-tuple-element.134), channel_id=1, source_target_pairs={{0,8},{8,0},{16,24},{24,16},{1,9},{9,1},{17,25},{25,17},{2,10},{10... | collective-permute-start | bytes 12296 | tf_op jit(solution)/shard_map/ppermute | solution.py:394
  50.1 3.6 %collective-permute-start.12 = (f32[8,128]{1,0:T(8,128)S(1)}, f32[8,128]{1,0:T(8,128)S(1)}, u32[]{:S(2)}, u32[]{:S(2)}) collective-permute-start(f32[8,128]{1,0:T(8,128)S(1)} %add.6), channel_id=1, source_target_pairs={{0,2},{1,3},{2,0},{3,1},{4,6},{5,7},{6,4},{7,5},{8,10},{9,11},{10,... | collective-permute-start | bytes 12296 | tf_op jit(solution)/shard_map/ppermute | solution.py:394

commit v6 on v5

--- a/solution.py
+++ b/solution.py
@@ -81,7 +81,7 @@
         copy.wait()
 
 
-def prepare_body(b, c, raw, a_log, skip, dt_bias, cols_out, low_out, low_t_out, b_t_out, c_t_out, sq_out, rows_out, sides_out):
+def prepare_body(b, c, raw, a_log, skip, dt_bias, cols_out, low_out, b_t_out, c_t_out, rows_out, shifted_out):
     size, width = b.shape
     lanes = lax.broadcasted_iota(jnp.int32, (1, width), 1)
     rate = jnp.where(lanes < a_log.shape[1], jnp.exp(head_row(a_log[...], width)), 0.0)
@@ -91,34 +91,50 @@
     cols_out[0] = jnp.exp(logs - mid)
     cols_out[1] = dt * jnp.exp(mid - logs)
     cols_out[2] = dt
+    cols_out[3] = logs
     half = jnp.exp(mid)
     rows_out[...] = jnp.concatenate([half, half * half, rate, head_row(skip[...], width), bias, jnp.zeros((3, width), f32)], axis=0)
-    sigma = 1.0 / (1.0 + jnp.exp(-shifted))
-    cols_out[3] = sigma
-    cols_out[4] = logs
-    lower = jnp.where(triangle(size, True), 1.0, 0.0).astype(f32)
-    cols_out[5] = jnp.dot(lower, rate * sigma, precision=highest, preferred_element_type=f32)
-    sq_out[...] = jnp.exp(2.0 * logs).T
-    sides_out[...] = jnp.concatenate([rate, bias, jnp.zeros((6, width), f32)], axis=0).T
+    shifted_out[...] = shifted
     low_out[...] = jnp.where(triangle(size, True), dot_nt(c[...], b[...]), 0.0).astype(bf16)
-    low_t_out[...] = jnp.where(triangle(size, False), dot_nt(b[...], c[...]), 0.0).astype(bf16)
     b_t_out[...] = b[...].T
     c_t_out[...] = c[...].T
 
 
+def prepare_more_body(b, c, cols, rows, shifted, low_t_out, sq_out, sides_out, sigmas_out):
+    size = b.shape[0]
+    low_t_out[...] = jnp.where(triangle(size, False), dot_nt(b[...], c[...]), 0.0).astype(bf16)
+    sq_out[...] = jnp.exp(2.0 * cols[3]).T
+    rate, bias = rows[2:3, :], rows[4:5, :]
+    sides_out[...] = jnp.concatenate([rate, bias, jnp.zeros((6, rate.shape[1]), f32)], axis=0).T
+    sigma = 1.0 / (1.0 + jnp.exp(-shifted[...]))
+    lower = jnp.where(triangle(size, True), 1.0, 0.0).astype(f32)
+    sigmas_out[0] = sigma
+    sigmas_out[1] = jnp.dot(lower, rate * sigma, precision=highest, preferred_element_type=f32)
+
+
+def side_by_side(parts):
+    return jnp.concatenate(parts, axis=1)
+
+
 def first_body(heads, x, t, cols, low, b_t, c_t, rows, f_out, p_out, xr_out, y_out, err_out):
-    for k, h in enumerate(heads):
-        xs = x[h].astype(f32)
-        g, scale, skip = cols[0, :, h : h + 1], rows[0:1, h : h + 1], rows[3:4, h : h + 1]
-        xr = (xs * cols[1, :, h : h + 1]).astype(bf16)
-        y = dot(low[...], xr)
-        err = g * y + skip * xs - t[h].astype(f32)
-        ew = (err * g).astype(bf16)
-        xr_out[k] = xr
-        y_out[k] = y
+    channels = x.shape[2]
+    spans = [slice(k * channels, (k + 1) * channels) for k in range(len(heads))]
+    for k, h in enumerate(heads):
+        xr_out[k] = (x[h].astype(f32) * cols[1, :, h : h + 1]).astype(bf16)
+    wide = side_by_side([xr_out[k] for k in range(len(heads))])
+    y, contrib = dot(low[...], wide), dot(b_t[...], wide)
+    weighted = []
+    for k, h in enumerate(heads):
+        g, skip = cols[0, :, h : h + 1], rows[3:4, h : h + 1]
+        err = g * y[:, spans[k]] + skip * x[h].astype(f32) - t[h].astype(f32)
+        y_out[k] = y[:, spans[k]]
         err_out[k] = err
-        f_out[k] = scale * dot(b_t[...], xr)
-        p_out[k] = scale * dot(c_t[...], ew)
+        weighted.append((err * g).astype(bf16))
+    pulled = dot(c_t[...], side_by_side(weighted))
+    for k, h in enumerate(heads):
+        scale = rows[0:1, h : h + 1]
+        f_out[k] = scale * contrib[:, spans[k]]
+        p_out[k] = scale * pulled[:, spans[k]]
 
 
 def send_body(f, p, *refs):
@@ -159,7 +175,7 @@
     high = m.astype(bf16)
     low = (m - high.astype(f32)).astype(bf16)
     s_low = s.astype(bf16)
-    return dot(high, s_low) + dot(low, s_low)
+    return dot(side_by_side([high, low]), jnp.concatenate([s_low, s_low], axis=0))
 
 
 def round_body(heads, n, r, f, p, m, mc, rows, got, s_in, d_in, *refs):
@@ -176,12 +192,14 @@
         d_out[k] = d
         total = rows[1:2, h : h + 1]
         after = total * s + f[k]
-        full = p[k] + times(m[h], s) + total * (d + times(mc[h], after))
+        full = p[k] + total * (d + times(mc[h], after))
+        if n - r < r:
+            full = full + times(m[h], s)
         pay_out[k] = jnp.where(place == r - 1, after, full)
 
 
 def last_body(heads, scales, *refs):
-    (x, cols, low, low_t, b, c, rows, xr, y_in, err_in, f, mc, got, s_in, d_in, v_in, sums_in) = refs[:17]
+    (x, cols, sigmas, low_t, b, c, rows, xr, y_in, err_in, f, mc, got, s_in, d_in, v_in, sums_in) = refs[:17]
     gx_out, ew_out, s_low_out, a_low_out, v_out, sums_out = refs[17:]
     n = lax.axis_size("ctx")
     place = lax.axis_index("ctx")
@@ -190,30 +208,36 @@
     lanes = lax.broadcasted_iota(jnp.int32, (1, width), 1)
     v_all, w_all = v_in[0], v_in[1]
     ends, skips = sums_in[0:1, :], sums_in[1:2, :]
-    for k, h in enumerate(heads):
-        g, r = cols[0, :, h : h + 1], cols[1, :, h : h + 1]
-        scale, total, skip = rows[0:1, h : h + 1], rows[1:2, h : h + 1], rows[3:4, h : h + 1]
+    spans = [slice(k * channels, (k + 1) * channels) for k in range(len(heads))]
+    states, adjoints = [], []
+    for k, h in enumerate(heads):
+        scale, total = rows[0:1, h : h + 1], rows[1:2, h : h + 1]
         s = jnp.where(place == n - 1, got[k], s_in[k]) if n > 1 else s_in[k]
         d = jnp.where(place == 0, got[k], d_in[k]) if n > 1 else d_in[k]
         after = total * s + f[k]
         adjoint = d + times(mc[h], after)
-        s_low = (scale * s).astype(bf16)
-        a_low = (scale * adjoint).astype(bf16)
-        carried = dot(c[...], s_low)
-        y = y_in[k] + carried
-        err = err_in[k] + g * carried
-        ew = (err * g).astype(bf16)
-        z = dot(low_t[...], ew) + dot(b[...], a_low)
-        gx_out[k] = (r * z + skip * err).astype(bf16)
-        here = lanes == h
-        v_all = jnp.where(here, jnp.sum(ew.astype(f32) * y, axis=1, keepdims=True), v_all)
-        w_all = jnp.where(here, jnp.sum(xr[k].astype(f32) * z, axis=1, keepdims=True), w_all)
-        ends = jnp.where(here, jnp.sum(jnp.sum(adjoint * after, axis=0, keepdims=True), axis=1, keepdims=True), ends)
+        states.append((scale * s).astype(bf16))
+        adjoints.append((scale * adjoint).astype(bf16))
+        ends = jnp.where(lanes == h, jnp.sum(jnp.sum(adjoint * after, axis=0, keepdims=True), axis=1, keepdims=True), ends)
+    states, adjoints = side_by_side(states), side_by_side(adjoints)
+    carried = dot(c[...], states)
+    errs, weighted = [], []
+    for k, h in enumerate(heads):
+        g = cols[0, :, h : h + 1]
+        errs.append(err_in[k] + g * carried[:, spans[k]])
+        weighted.append((errs[k] * g).astype(bf16))
+    wide = side_by_side(weighted)
+    z = dot(low_t[...], wide) + dot(b[...], adjoints)
+    for k, h in enumerate(heads):
+        here, err, own = lanes == h, errs[k], z[:, spans[k]]
+        y = y_in[k] + carried[:, spans[k]]
+        gx_out[k] = (cols[1, :, h : h + 1] * own + rows[3:4, h : h + 1] * err).astype(bf16)
+        v_all = jnp.where(here, jnp.sum(weighted[k].astype(f32) * y, axis=1, keepdims=True), v_all)
+        w_all = jnp.where(here, jnp.sum(xr[k].astype(f32) * own, axis=1, keepdims=True), w_all)
         skips = jnp.where(here, jnp.sum(jnp.sum(err * x[h].astype(f32), axis=0, keepdims=True), axis=1, keepdims=True), skips)
-        span = slice(k * channels, (k + 1) * channels)
-        ew_out[:, span] = ew
-        s_low_out[:, span] = s_low
-        a_low_out[:, span] = a_low
+    ew_out[...] = wide
+    s_low_out[...] = states
+    a_low_out[...] = adjoints
     if scales is None:
         v_out[0] = v_all
         v_out[1] = w_all
@@ -224,8 +248,8 @@
     by_step = w_all / cols[2]
     v_out[0] = grad_logs
     v_out[1] = by_step
-    alog = jnp.sum(grad_logs * cols[4], axis=0, keepdims=True)
-    bias = jnp.sum(by_step * cols[3] - grad_logs * cols[5], axis=0, keepdims=True)
+    alog = jnp.sum(grad_logs * cols[3], axis=0, keepdims=True)
+    bias = jnp.sum(by_step * sigmas[0] - grad_logs * sigmas[1], axis=0, keepdims=True)
     sums_out[...] = jnp.concatenate(
         [alog * scales[0], skips * scales[1], bias * scales[0], jnp.zeros((5, width), f32)], axis=0
     )
@@ -255,14 +279,14 @@
 
 
 def output_body(chunks, *refs):
-    parts, (cols, rows, v), (gx_out, raw_out, sems) = refs[:chunks], refs[chunks : chunks + 3], refs[chunks + 3 :]
+    parts, (sigmas, rows, v), (gx_out, raw_out, sems) = refs[:chunks], refs[chunks : chunks + 3], refs[chunks + 3 :]
     size, starts = v.shape[1], [0]
     for part in parts:
         starts.append(starts[-1] + part.shape[0])
     copies = fetch([(part, gx_out.at[pl.ds(start, part.shape[0])]) for part, start in zip(parts, starts)], sems)
     later = jnp.where(triangle(size, False), 1.0, 0.0).astype(f32)
     log_rate = jnp.dot(later, v[0], precision=highest, preferred_element_type=f32)
-    raw_out[...] = ((v[1] - rows[2:3, :] * log_rate) * cols[3]).T[: raw_out.shape[0], :]
+    raw_out[...] = ((v[1] - rows[2:3, :] * log_rate) * sigmas[0]).T[: raw_out.shape[0], :]
     for copy in copies:
         copy.wait()
 
@@ -313,10 +337,13 @@
         return exchange(value, [(i + 1, i) for i in range(lowest, n - step)] + [(lowest, n - step)])
 
     later = down(1, own) if n > 1 else own
-    cols, low, low_t, b_t, c_t, sq, rows, sides = call(
-        prepare_body,
-        [shape((6, size, width), f32), square, square, flat, flat, shape((width, size), f32), shape((8, width), f32), shape((width, 8), f32)],
-        b, c, raw, a_log, skip_gain, dt_bias,
+    row, sheet = shape((8, width), f32), shape((size, width), f32)
+    cols, low, b_t, c_t, rows, shifted = call(
+        prepare_body, [shape((4, size, width), f32), square, flat, flat, row, sheet], b, c, raw, a_log, skip_gain, dt_bias
+    )
+    low_t, sq, sides, sigmas = call(
+        prepare_more_body, [square, shape((width, size), f32), shape((width, 8), f32), shape((2, size, width), f32)],
+        b, c, cols, rows, shifted,
     )
     held = []
     for group in groups:
@@ -379,7 +406,7 @@
             functools.partial(last_body, groups[i], scales if final else None),
             like(h["xr"]) + [shape((extent, len(groups[i]) * channels), bf16) for extent in (size, width, width)]
             + [shape(v.shape, f32), shape((8, width), f32)],
-            x, cols, low, low_t, b, c, rows, h["xr"], h["y"], h["err"], h["f"], maps[-1][0],
+            x, cols, sigmas, low_t, b, c, rows, h["xr"], h["y"], h["err"], h["f"], maps[-1][0],
             h.get("got", h["s"]), h["s"], h["d"], v, total, flops=4 * 10**8,
         )
         grad_x.append(gx)
@@ -401,7 +428,7 @@
     keep, send, total = call(cut_body, [halves, halves, sums], grads, *firsts)
     grad_x, grad_raw = call(
         functools.partial(output_body, chunks), [shape((heads, size, channels), bf16), shape(raw.shape, f32)],
-        *grad_x, cols, rows, v, out_specs=[HBM, VMEM], scratch=[pltpu.SemaphoreType.DMA((chunks,))],
+        *grad_x, sigmas, rows, v, out_specs=[HBM, VMEM], scratch=[pltpu.SemaphoreType.DMA((chunks,))],
     )
     step = parts // 2
     while step >= 1:

time: 54.4 us -> 54 us (level)
  Pallas kernels: 13.5 us -> 12.9 us
    pallas_call x20 -> x21, Pallas kernels: 13.5 us -> 12.9 us  [call(): pl.pallas_call(body, out_shape=outs, in_specs=ins or [VMEM] * len(args),...]
  transfers between devices with their start and end apart: 13 -> 13, of which waited for: 7 -> 7; matrix products, arithmetic and copies ran while one was open for 1% -> 1% of each run, Pallas kernels for 21% -> 20%
where the time goes in v6:
time: 54 us; the launch traced here: 53.8 us
  starting transfers between devices  21.8 us (40%)
  waiting for transfers between devices  17.1 us (32%)
  Pallas kernels  12.9 us (24%)
  local copies, waits for them, and re-layouts  1.22 us (2%)
  between operations  0.84 us (2%)
    ppermute x8, starting transfers between devices, exchange(): return lax.ppermute(value, ('ctx', 'seq'), pairs)  15.3 us
    pallas_call x21, Pallas kernels, call(): pl.pallas_call(body, out_shape=outs, in_specs=ins or [VMEM] * len(args),...  12.9 us
    ppermute x8, waiting for transfers between devices, exchange(): return lax.ppermute(value, ('ctx', 'seq'), pairs)  11.8 us
    ppermute x4, waiting for transfers between devices, swapped(): return lax.ppermute(value, axis, [(i, i ^ by) for i in range(spans[axis])])  5.24 us
    ppermute x4, starting transfers between devices, swapped(): return lax.ppermute(value, axis, [(i, i ^ by) for i in range(spans[axis])])  4.87 us
    ppermute x1, starting transfers between devices, on_device(): received = lax.ppermute(send, 'head', [(i, i ^ step) for i in range(parts)])  1.58 us
  transfers between devices with their start and end apart: 13, of which 7 were waited for; matrix products, arithmetic and copies ran while one was open for 1% of the time, Pallas kernels for 20%

profile of v6, /device:TPU:0, one launch (start us, length us, event | category | flops | bytes accessed | tf_op | source)
XLA Modules:
  0.0 53.8 jit_solution(16151623993576070313)
XLA Ops:
  0.6 0.9 %shard_map.136 = (bf16[256,128]{1,0:T(8,128)(2,1)S(1)}, f32[8,256]{1,0:T(8,128)S(1)}, f32[272,128]{1,0:T(8,128)S(1)}) custom-call(bf16[256,128]{1,0:T(8,128)(2,1)} %bitcast.19, f32[8,256]{1,0:T(8,128)} %bitcast.20), custom_call_target="tpu_custom_call" | custom-call | flops 10 | bytes 256 | tf_op jit(solution)/shard_map/pallas_call | solution.py:27
  1.5 0.5 collective-permute-start
  2.0 1.3 %shard_map.135 = (f32[1,8]{1,0:T(1,128)S(1)}, f32[1,8]{1,0:T(1,128)S(1)}, f32[1,8]{1,0:T(1,128)S(1)}, bf16[256,128]{1,0:T(8,128)(2,1)S(1)}, bf16[8,256,128]{2,1,...) custom-call(f32[1,8]{1,0:T(1,128)} %bitcast.21, f32[1,8]{1,0:T(1,128)} %bitcast.22, f32[1,8]{1,0:T(1,128)} %bitcast.23, ...), custom_call_target="tpu_custom_call" | custom-call | flops 10 | bytes 256 | tf_op jit(solution)/shard_map/pallas_call | solution.py:27
  3.4 0.7 %shard_map.137 = (f32[4,256,128]{2,1,0:T(8,128)S(1)}, bf16[256,256]{1,0:T(8,128)(2,1)S(1)}, bf16[128,256]{1,0:T(8,128)(2,1)S(1)}, bf16[128,256]{1,0:T(8,128)(2,1...) custom-call(bf16[256,128]{1,0:T(8,128)(2,1)S(1)} %get-tuple-element.74.b.refs_4_, ...), custom_call_target="tpu_custom_call" | custom-call | flops 1000 | bytes 256 | tf_op jit(solution)/shard_map/pallas_call | solution.py:27
  4.1 0.7 %shard_map.139 = (f32[4,128,128]{2,1,0:T(8,128)S(1)}, f32[4,128,128]{2,1,0:T(8,128)S(1)}, bf16[4,256,128]{2,1,0:T(8,128)(2,1)S(1)}, f32[4,256,128]{2,1,0:T(8,128)S(1)}, f32[4,256,128]{2,1,0:T(8,128)S(1)}) custom-call(bf16[8,256,128]{2,1,0:T(8,128)(2,1)S(1)} %get-tuple-element.73.x.refs_0_, bf16[8,256,128]{2,1,0:T(8,128)(2,1)S(1)} %get-tuple-element.85.t, ...), custom_call_target="tpu_custom_call" | custom-call | flops 4000 | bytes 256 | tf_op jit(solution)/shard_map/pallas_call | solution.py:27
  4.8 5.2 %collective-permute-start.1 = (f32[4,128,128]{2,1,0:T(8,128)S(1)}, f32[4,128,128]{2,1,0:T(8,128)S(1)}, u32[]{:S(2)}, u32[]{:S(2)}) collective-permute-start(f32[4,128,128]{2,1,0:T(8,128)S(1)} %shard_map.144), channel_id=1, source_target_pairs={{0,8},{1,9},{2,10},{3,11},{8,0},{9,1},{10,2},{11,3},{16,24},{17,25... | collective-permute-start | bytes 786440 | tf_op jit(solution)/shard_map/ppermute | solution.py:334
  10.0 0.7 %shard_map.141 = (f32[4,128,128]{2,1,0:T(8,128)S(1)}, f32[4,128,128]{2,1,0:T(8,128)S(1)}, bf16[4,256,128]{2,1,0:T(8,128)(2,1)S(1)}, f32[4,256,128]{2,1,0:T(8,128)S(1)}, f32[4,256,128]{2,1,0:T(8,128)S(1)}) custom-call(bf16[8,256,128]{2,1,0:T(8,128)(2,1)S(1)} %get-tuple-element.73.x.refs_0_, bf16[8,256,128]{2,1,0:T(8,128)(2,1)S(1)} %get-tuple-element.85.t, ...), custom_call_target="tpu_custom_call" | custom-call | flops 4000 | bytes 256 | tf_op jit(solution)/shard_map/pallas_call | solution.py:27
  10.7 0.0 collective-permute-done.refs_0_
  10.8 0.1 collective-permute-start.5
  10.9 0.1 collective-permute-start.2
  10.9 0.4 shard_map.138
  11.4 0.3 shard_map.140.m
  11.7 0.8 %shard_map.143 = (f32[8,128,128]{2,1,0:T(8,128)S(1)}, f32[8,128]{1,0:T(8,128)S(1)}) custom-call(f32[128,8]{1,0:T(8,128)S(1)} %get-tuple-element.93.sides, f32[272,128]{1,0:T(8,128)S(1)} %get-tuple-element.99.got), custom_call_target="tpu_custom_call" | custom-call | flops 1000 | bytes 256 | tf_op jit(solution)/shard_map/pallas_call | solution.py:27
  12.4 4.8 %collective-permute-done.1.got = f32[4,128,128]{2,1,0:T(8,128)S(1)} collective-permute-done((f32[4,128,128]{2,1,0:T(8,128)S(1)}, f32[4,128,128]{2,1,0:T(8,128)S(1)}, u32[]{:S(2)}, u32[]{:S(2)}) %collective-permute-start.1) | collective-permute-done | bytes 262176 | tf_op jit(solution)/shard_map/ppermute | solution.py:334
  17.2 0.0 collective-permute-done.2.refs_0_
  17.2 0.3 shard_map.145
  17.6 0.1 collective-permute-start.3
  17.7 1.1 %shard_map.146 = (f32[8,128,128]{2,1,0:T(8,128)S(1)}, f32[8,128]{1,0:T(8,128)}) custom-call(f32[128,8]{1,0:T(8,128)S(1)} %get-tuple-element.93.sides, f32[272,128]{1,0:T(8,128)S(1)} %get-tuple-element.101.got, f32[8,128,128]{2,1,0:T(8,128)S(1)} %get-tuple-element.100.mc.refs_0_, f32[8,128]{1,0:T(8,128)S(1)} %get-tuple-element.102.refs_1_), custom_call_target="tpu_custom_call" | custom-call | flops 1000 | bytes 256 | tf_op jit(solution)/shard_map/pallas_call | solution.py:27
  18.8 2.9 %collective-permute-done.5.got = f32[4,128,128]{2,1,0:T(8,128)S(1)} collective-permute-done((f32[4,128,128]{2,1,0:T(8,128)S(1)}, f32[4,128,128]{2,1,0:T(8,128)S(1)}, u32[]{:S(2)}, u32[]{:S(2)}) %collective-permute-start.5) | collective-permute-done | bytes 262176 | tf_op jit(solution)/shard_map/ppermute | solution.py:334
  21.7 0.3 shard_map.149
  22.0 0.1 collective-permute-start.6
  22.1 0.0 collective-permute-done.3.got
  22.1 0.4 shard_map.147
  22.5 5.0 %collective-permute-start.4 = (f32[4,128,128]{2,1,0:T(8,128)S(1)}, f32[4,128,128]{2,1,0:T(8,128)S(1)}, u32[]{:S(2)}, u32[]{:S(2)}) collective-permute-start(f32[4,128,128]{2,1,0:T(8,128)S(1)} %get-tuple-element.107), channel_id=1, source_target_pairs={{0,8},{1,9},{2,10},{3,11},{8,0},{9,1},{10,2},{11,3},{16,24},{17,25... | collective-permute-start | bytes 786440 | tf_op jit(solution)/shard_map/ppermute | solution.py:334
  27.5 0.0 collective-permute-done.6.got
  27.5 0.4 shard_map.150
  27.9 4.2 %collective-permute-start.7 = (f32[4,128,128]{2,1,0:T(8,128)S(1)}, f32[4,128,128]{2,1,0:T(8,128)S(1)}, u32[]{:S(2)}, u32[]{:S(2)}) collective-permute-start(f32[4,128,128]{2,1,0:T(8,128)S(1)} %get-tuple-element.118), channel_id=1, source_target_pairs={{0,8},{1,9},{2,10},{3,11},{8,0},{9,1},{10,2},{11,3},{16,24},{17,25... | collective-permute-start | bytes 786440 | tf_op jit(solution)/shard_map/ppermute | solution.py:334
  32.2 0.0 collective-permute-done.4.refs_12_
  32.2 1.1 %shard_map.148 = (bf16[4,256,128]{2,1,0:T(8,128)(2,1)S(1)}, bf16[256,512]{1,0:T(8,128)(2,1)S(1)}, bf16[128,512]{1,0:T(8,128)(2,1)S(1)}, bf16[128,512]{1,0:T(8,12...) custom-call(bf16[8,256,128]{2,1,0:T(8,128)(2,1)S(1)} %get-tuple-element.73.x.refs_0_, ...), custom_call_target="tpu_custom_call" | custom-call | flops 4000 | bytes 256 | tf_op jit(solution)/shard_map/pallas_call | solution.py:27
  33.3 4.2 %collective-permute-done.7.refs_12_ = f32[4,128,128]{2,1,0:T(8,128)S(1)} collective-permute-done((f32[4,128,128]{2,1,0:T(8,128)S(1)}, f32[4,128,128]{2,1,0:T(8,128)S(1)}, u32[]{:S(2)}, u32[]{:S(2)}) %collective-permute-start.7) | collective-permute-done | bytes 262176 | tf_op jit(solution)/shard_map/ppermute | solution.py:334
  37.5 1.1 %shard_map.151 = (bf16[4,256,128]{2,1,0:T(8,128)(2,1)S(1)}, bf16[256,512]{1,0:T(8,128)(2,1)S(1)}, bf16[128,512]{1,0:T(8,128)(2,1)S(1)}, bf16[128,512]{1,0:T(8,12...) custom-call(bf16[8,256,128]{2,1,0:T(8,128)(2,1)S(1)} %get-tuple-element.73.x.refs_0_, ...), custom_call_target="tpu_custom_call" | custom-call | flops 4000 | bytes 256 | tf_op jit(solution)/shard_map/pallas_call | solution.py:27
  38.6 0.1 collective-permute-start.8
  38.7 0.8 %shard_map.153.grads = f32[2,256,128]{2,1,0:T(8,128)S(1)} custom-call(bf16[256,128]{1,0:T(8,128)(2,1)S(1)} %get-tuple-element.74.b.refs_4_, bf16[256,128]{1,0:T(8,128)(2,1)S(1)} %get-tuple-element.75.c.refs_5_, bf16[4,256,128]{2,1,0:T(8,128)(2,1)S(1)} %get-tuple-element.89.refs_7_.refs_0_, bf16[4,256,128]{2,1,0:T(8,128)(2,1)S(1)} %get-tuple-element.111.refs_7_.refs_1_, ...), custom_call_target="tpu_custom_call" | custom-call | flops 4000 | bytes 256 | tf_op jit(solution)/shard_map/pallas_call | solution.py:27
  39.5 0.3 collective-permute-done.8.refs_1_
  39.9 1.6 %collective-permute-start.9 = (f32[2,128,128]{2,1,0:T(8,128)S(1)}, f32[2,128,128]{2,1,0:T(8,128)S(1)}, u32[]{:S(2)}, u32[]{:S(2)}) collective-permute-start(f32[2,128,128]{2,1,0:T(8,128)S(1)} %get-tuple-element.135), channel_id=1, source_target_pairs={{0,4},{4,0},{1,5},{5,1},{2,6},{6,2},{3,7},{7,3},{8,12},{12,8},{9,1... | collective-permute-start | bytes 393224 | tf_op jit(solution)/shard_map/ppermute | solution.py:435
  41.5 1.2 %collective-permute-start.10 = (f32[8,128]{1,0:T(8,128)S(1)}, f32[8,128]{1,0:T(8,128)S(1)}, u32[]{:S(2)}, u32[]{:S(2)}) collective-permute-start(f32[8,128]{1,0:T(8,128)S(1)} %get-tuple-element.134.refs_1_), channel_id=1, source_target_pairs={{0,16},{8,24},{16,0},{24,8},{1,17},{9,25},{17,1},{25,9},{2,18},{10... | collective-permute-start | bytes 12296 | tf_op jit(solution)/shard_map/ppermute | solution.py:421
  42.7 3.3 %collective-permute-done.10.refs_3_ = f32[8,128]{1,0:T(8,128)S(1)} collective-permute-done((f32[8,128]{1,0:T(8,128)S(1)}, f32[8,128]{1,0:T(8,128)S(1)}, u32[]{:S(2)}, u32[]{:S(2)}) %collective-permute-start.10) | collective-permute-done | bytes 4128 | tf_op jit(solution)/shard_map/ppermute | solution.py:421
  46.0 0.0 collective-permute-done.9.refs_2_
  46.0 2.1 %collective-permute-start.11 = (f32[8,128]{1,0:T(8,128)S(1)}, f32[8,128]{1,0:T(8,128)S(1)}, u32[]{:S(2)}, u32[]{:S(2)}) collective-permute-start(f32[8,128]{1,0:T(8,128)S(1)} %get-tuple-element.138), channel_id=1, source_target_pairs={{0,8},{8,0},{16,24},{24,16},{1,9},{9,1},{17,25},{25,17},{2,10},{10... | collective-permute-start | bytes 12296 | tf_op jit(solution)/shard_map/ppermute | solution.py:421
  48.1 1.4 %shard_map.152 = (bf16[8,256,128]{2,1,0:T(8,128)(2,1)}, f32[8,256]{1,0:T(8,128)}) custom-call(bf16[4,256,128]{2,1,0:T(8,128)(2,1)S(1)} %get-tuple-element.110.refs_0_, bf16[4,256,128]{2,1,0:T(8,128)(2,1)S(1)} %get-tuple-element.123.refs_1_, f32[2,256,128]{2,1,0:T(8,128)S(1)} %get-tuple-element.83.refs_2_, ...), custom_call_target="tpu_custom_call" | custom-call | flops 1000 | bytes 256 | tf_op jit(solution)/shard_map/pallas_call | solution.py:27
  49.5 0.2 collective-permute-done.11
  49.7 1.5 %collective-permute-start.12 = (f32[8,128]{1,0:T(8,128)S(1)}, f32[8,128]{1,0:T(8,128)S(1)}, u32[]{:S(2)}, u32[]{:S(2)}) collective-permute-start(f32[8,128]{1,0:T(8,128)S(1)} %add.6), channel_id=1, source_target_pairs={{0,2},{1,3},{2,0},{3,1},{4,6},{5,7},{6,4},{7,5},{8,10},{9,11},{10,... | collective-permute-start | bytes 12296 | tf_op jit(solution)/shard_map/ppermute | solution.py:421
  51.2 0.7 %fusion = (f32[1,128,128]{2,1,0:T(8,128)}, f32[1,128,128]{2,1,0:T(8,128)}) fusion(f32[2,128,128]{2,1,0:T(8,128)S(1)} %get-tuple-element.136), kind=kLoop, calls=%fused_computation.3 | loop fusion | bytes 262144 | tf_op jit(solution)/shard_map/slice | solution.py:452
  51.8 1.5 %collective-permute-done.12 = f32[8,128]{1,0:T(8,128)S(1)} collective-permute-done((f32[8,128]{1,0:T(8,128)S(1)}, f32[8,128]{1,0:T(8,128)S(1)}, u32[]{:S(2)}, u32[]{:S(2)}) %collective-permute-start.12) | collective-permute-done | bytes 4128 | tf_op jit(solution)/shard_map/ppermute | solution.py:421
  53.3 0.5 slice_bitcast_fusion
  (9 shorter events, 0.2 us)
Async XLA Ops:
  1.5 9.2 %collective-permute-start = (f32[272,128]{1,0:T(8,128)S(1)}, f32[272,128]{1,0:T(8,128)S(1)}, u32[]{:S(2)}, u32[]{:S(2)}) collective-permute-start(f32[272,128]{1,0:T(8,128)S(1)} %get-tuple-element.98), channel_id=1, source_target_pairs={{0,1},{1,0},{2,3},{3,2},{8,24},{9,25},{10,26},{11,27},{16,8},{17,9... | collective-permute-start | bytes 417800 | tf_op jit(solution)/shard_map/ppermute | solution.py:334
  4.8 12.4 %collective-permute-start.1 = (f32[4,128,128]{2,1,0:T(8,128)S(1)}, f32[4,128,128]{2,1,0:T(8,128)S(1)}, u32[]{:S(2)}, u32[]{:S(2)}) collective-permute-start(f32[4,128,128]{2,1,0:T(8,128)S(1)} %shard_map.144), channel_id=1, source_target_pairs={{0,8},{1,9},{2,10},{3,11},{8,0},{9,1},{10,2},{11,3},{16,24},{17,25... | collective-permute-start | bytes 786440 | tf_op jit(solution)/shard_map/ppermute | solution.py:334
  10.8 10.9 %collective-permute-start.5 = (f32[4,128,128]{2,1,0:T(8,128)S(1)}, f32[4,128,128]{2,1,0:T(8,128)S(1)}, u32[]{:S(2)}, u32[]{:S(2)}) collective-permute-start(f32[4,128,128]{2,1,0:T(8,128)S(1)} %get-tuple-element.114), channel_id=1, source_target_pairs={{0,8},{1,9},{2,10},{3,11},{8,0},{9,1},{10,2},{11,3},{16,24},{17,25... | collective-permute-start | bytes 786440 | tf_op jit(solution)/shard_map/ppermute | solution.py:334
  10.9 6.3 %collective-permute-start.2 = (f32[272,128]{1,0:T(8,128)S(1)}, f32[272,128]{1,0:T(8,128)S(1)}, u32[]{:S(2)}, u32[]{:S(2)}) collective-permute-start(f32[272,128]{1,0:T(8,128)S(1)} %get-tuple-element.99.got), channel_id=1, source_target_pairs={{0,1},{1,0},{2,3},{3,2},{8,16},{9,17},{10,18},{11,19},{16,8},{17,9... | collective-permute-start | bytes 417800 | tf_op jit(solution)/shard_map/ppermute | solution.py:334
  17.6 4.5 %collective-permute-start.3 = (f32[4,128,128]{2,1,0:T(8,128)S(1)}, f32[4,128,128]{2,1,0:T(8,128)S(1)}, u32[]{:S(2)}, u32[]{:S(2)}) collective-permute-start(f32[4,128,128]{2,1,0:T(8,128)S(1)} %get-tuple-element.104), channel_id=1, source_target_pairs={{0,1},{1,0},{2,3},{3,2},{8,16},{9,17},{10,18},{11,19},{16,8},{17,9... | collective-permute-start | bytes 786440 | tf_op jit(solution)/shard_map/ppermute | solution.py:334
  22.0 5.5 %collective-permute-start.6 = (f32[4,128,128]{2,1,0:T(8,128)S(1)}, f32[4,128,128]{2,1,0:T(8,128)S(1)}, u32[]{:S(2)}, u32[]{:S(2)}) collective-permute-start(f32[4,128,128]{2,1,0:T(8,128)S(1)} %get-tuple-element.115), channel_id=1, source_target_pairs={{0,1},{1,0},{2,3},{3,2},{8,16},{9,17},{10,18},{11,19},{16,8},{17,9... | collective-permute-start | bytes 786440 | tf_op jit(solution)/shard_map/ppermute | solution.py:334
  22.5 9.7 %collective-permute-start.4 = (f32[4,128,128]{2,1,0:T(8,128)S(1)}, f32[4,128,128]{2,1,0:T(8,128)S(1)}, u32[]{:S(2)}, u32[]{:S(2)}) collective-permute-start(f32[4,128,128]{2,1,0:T(8,128)S(1)} %get-tuple-element.107), channel_id=1, source_target_pairs={{0,8},{1,9},{2,10},{3,11},{8,0},{9,1},{10,2},{11,3},{16,24},{17,25... | collective-permute-start | bytes 786440 | tf_op jit(solution)/shard_map/ppermute | solution.py:334
  27.9 9.6 %collective-permute-start.7 = (f32[4,128,128]{2,1,0:T(8,128)S(1)}, f32[4,128,128]{2,1,0:T(8,128)S(1)}, u32[]{:S(2)}, u32[]{:S(2)}) collective-permute-start(f32[4,128,128]{2,1,0:T(8,128)S(1)} %get-tuple-element.118), channel_id=1, source_target_pairs={{0,8},{1,9},{2,10},{3,11},{8,0},{9,1},{10,2},{11,3},{16,24},{17,25... | collective-permute-start | bytes 786440 | tf_op jit(solution)/shard_map/ppermute | solution.py:334
  38.6 1.2 %collective-permute-start.8 = (f32[8,128]{1,0:T(8,128)S(1)}, f32[8,128]{1,0:T(8,128)S(1)}, u32[]{:S(2)}, u32[]{:S(2)}) collective-permute-start(f32[8,128]{1,0:T(8,128)S(1)} %get-tuple-element.132.refs_0_), channel_id=1, source_target_pairs={{0,1},{1,0},{2,3},{3,2},{4,5},{5,4},{6,7},{7,6},{8,9},{9,8},{10,11... | collective-permute-start | bytes 12296 | tf_op jit(solution)/shard_map/ppermute | solution.py:421
  39.9 6.1 %collective-permute-start.9 = (f32[2,128,128]{2,1,0:T(8,128)S(1)}, f32[2,128,128]{2,1,0:T(8,128)S(1)}, u32[]{:S(2)}, u32[]{:S(2)}) collective-permute-start(f32[2,128,128]{2,1,0:T(8,128)S(1)} %get-tuple-element.135), channel_id=1, source_target_pairs={{0,4},{4,0},{1,5},{5,1},{2,6},{6,2},{3,7},{7,3},{8,12},{12,8},{9,1... | collective-permute-start | bytes 393224 | tf_op jit(solution)/shard_map/ppermute | solution.py:435
  41.5 4.5 %collective-permute-start.10 = (f32[8,128]{1,0:T(8,128)S(1)}, f32[8,128]{1,0:T(8,128)S(1)}, u32[]{:S(2)}, u32[]{:S(2)}) collective-permute-start(f32[8,128]{1,0:T(8,128)S(1)} %get-tuple-element.134.refs_1_), channel_id=1, source_target_pairs={{0,16},{8,24},{16,0},{24,8},{1,17},{9,25},{17,1},{25,9},{2,18},{10... | collective-permute-start | bytes 12296 | tf_op jit(solution)/shard_map/ppermute | solution.py:421
  46.0 3.7 %collective-permute-start.11 = (f32[8,128]{1,0:T(8,128)S(1)}, f32[8,128]{1,0:T(8,128)S(1)}, u32[]{:S(2)}, u32[]{:S(2)}) collective-permute-start(f32[8,128]{1,0:T(8,128)S(1)} %get-tuple-element.138), channel_id=1, source_target_pairs={{0,8},{8,0},{16,24},{24,16},{1,9},{9,1},{17,25},{25,17},{2,10},{10... | collective-permute-start | bytes 12296 | tf_op jit(solution)/shard_map/ppermute | solution.py:421
  49.7 3.6 %collective-permute-start.12 = (f32[8,128]{1,0:T(8,128)S(1)}, f32[8,128]{1,0:T(8,128)S(1)}, u32[]{:S(2)}, u32[]{:S(2)}) collective-permute-start(f32[8,128]{1,0:T(8,128)S(1)} %add.6), channel_id=1, source_target_pairs={{0,2},{1,3},{2,0},{3,1},{4,6},{5,7},{6,4},{7,5},{8,10},{9,11},{10,... | collective-permute-start | bytes 12296 | tf_op jit(solution)/shard_map/ppermute | solution.py:421

commit v7 on v6

--- a/solution.py
+++ b/solution.py
@@ -65,19 +65,18 @@
     return copies
 
 
-def own_body(c, raw, cv, rawv, own, sems):
-    for copy in fetch(((c, cv), (raw, rawv)), sems):
+def load_body(*refs):
+    count = len(refs) // 2 - 1
+    copies = fetch(zip(refs[:count], refs[count : 2 * count]), refs[-1])
+    for copy in copies[:2]:
         copy.wait()
+    (c, raw), own = refs[count : count + 2], refs[-2]
     size, state = c.shape
     heads = raw.shape[0]
-    own[:size, :] = cv[...].astype(f32)
+    own[:size, :] = c[...].astype(f32)
     for s in range(size // state):
-        own[size + s * heads : size + (s + 1) * heads, :] = rawv[:, s * state : (s + 1) * state]
-
-
-def load_body(*refs):
-    count = len(refs) // 2
-    for copy in fetch(zip(refs[:count], refs[count : 2 * count]), refs[-1]):
+        own[size + s * heads : size + (s + 1) * heads, :] = raw[:, s * state : (s + 1) * state]
+    for copy in copies[2:]:
         copy.wait()
 
 
@@ -314,14 +313,12 @@
     def like(*arrays):
         return [shape(a.shape, a.dtype) for a in arrays]
 
-    shared = held_in_hbm(c_proj[0], dt_raw[0])
-    c, raw, own = call(
-        own_body, like(*shared) + [shape((size + heads * size // width, width), f32)], *shared,
-        ins=[HBM] * 2, scratch=[pltpu.SemaphoreType.DMA((2,))], flops=10**6,
-    )
-    rest = held_in_hbm(a_log[None], skip_gain[None], dt_bias[None], b_proj[0], x_heads[0], target[0])
-    a_log, skip_gain, dt_bias, b, x, t = call(
-        load_body, like(*rest), *rest, ins=[HBM] * 6, scratch=[pltpu.SemaphoreType.DMA((6,))], flops=10**6
+    arrays = held_in_hbm(
+        c_proj[0], dt_raw[0], a_log[None], skip_gain[None], dt_bias[None], b_proj[0], x_heads[0], target[0]
+    )
+    c, raw, a_log, skip_gain, dt_bias, b, x, t, own = call(
+        load_body, like(*arrays) + [shape((size + heads * size // width, width), f32)], *arrays,
+        ins=[HBM] * len(arrays), scratch=[pltpu.SemaphoreType.DMA((len(arrays),))], flops=10**6,
     )
     lowest = max(n // 2 - 1, 0)
 

time: 54 us -> 53.4 us (0.989)
  starting transfers between devices: 21.8 us -> 23.9 us
  waiting for transfers between devices: 17.1 us -> 15.3 us
  Pallas kernels: 12.9 us -> 12.1 us
    ppermute x4, starting transfers between devices: 4.87 us -> 6.29 us  [swapped(): return lax.ppermute(value, axis, [(i, i ^ by) for i in range(spans[axis])])]
    ppermute x4, waiting for transfers between devices: 5.24 us -> 4.21 us  [swapped(): return lax.ppermute(value, axis, [(i, i ^ by) for i in range(spans[axis])])]
    pallas_call x21 -> x20, Pallas kernels: 12.9 us -> 12.1 us  [call(): pl.pallas_call(body, out_shape=outs, in_specs=ins or [VMEM] * len(args),...]
    ppermute x8, waiting for transfers between devices: 11.8 us -> 11.1 us  [exchange(): return lax.ppermute(value, ('ctx', 'seq'), pairs)]
    ppermute x8, starting transfers between devices: 15.3 us -> 16 us  [exchange(): return lax.ppermute(value, ('ctx', 'seq'), pairs)]
  transfers between devices with their start and end apart: 13 -> 13, of which waited for: 7 -> 7; matrix products, arithmetic and copies ran while one was open for 1% -> 1% of each run, Pallas kernels for 20% -> 18%
where the time goes in v7:
time: 53.4 us; the launch traced here: 53.3 us
  starting transfers between devices  23.9 us (45%)
  waiting for transfers between devices  15.3 us (29%)
  Pallas kernels  12.1 us (23%)
  local copies, waits for them, and re-layouts  1.22 us (2%)
  between operations  0.81 us (2%)
    ppermute x8, starting transfers between devices, exchange(): return lax.ppermute(value, ('ctx', 'seq'), pairs)  16 us
    pallas_call x20, Pallas kernels, call(): pl.pallas_call(body, out_shape=outs, in_specs=ins or [VMEM] * len(args),...  12.1 us
    ppermute x8, waiting for transfers between devices, exchange(): return lax.ppermute(value, ('ctx', 'seq'), pairs)  11.1 us
    ppermute x4, starting transfers between devices, swapped(): return lax.ppermute(value, axis, [(i, i ^ by) for i in range(spans[axis])])  6.29 us
    ppermute x4, waiting for transfers between devices, swapped(): return lax.ppermute(value, axis, [(i, i ^ by) for i in range(spans[axis])])  4.21 us
    ppermute x1, starting transfers between devices, on_device(): received = lax.ppermute(send, 'head', [(i, i ^ step) for i in range(parts)])  1.58 us
  transfers between devices with their start and end apart: 13, of which 7 were waited for; matrix products, arithmetic and copies ran while one was open for 1% of the time, Pallas kernels for 18%

profile of v7, /device:TPU:0, one launch (start us, length us, event | category | flops | bytes accessed | tf_op | source)
XLA Modules:
  0.0 53.3 jit_solution(14684715708672774106)
XLA Ops:
  0.6 1.4 %shard_map.135 = (bf16[256,128]{1,0:T(8,128)(2,1)S(1)}, f32[8,256]{1,0:T(8,128)S(1)}, f32[1,8]{1,0:T(1,128)S(1)}, f32[1,8]{1,0:T(1,128)S(1)}, f32[1,8]{1,0:T(1,1...) custom-call(bf16[256,128]{1,0:T(8,128)(2,1)} %bitcast.18, ...), custom_call_target="tpu_custom_call" | custom-call | flops 10 | bytes 256 | tf_op jit(solution)/shard_map/pallas_call | solution.py:27
  2.1 0.5 collective-permute-start
  2.6 0.7 %shard_map.136 = (f32[4,256,128]{2,1,0:T(8,128)S(1)}, bf16[256,256]{1,0:T(8,128)(2,1)S(1)}, bf16[128,256]{1,0:T(8,128)(2,1)S(1)}, bf16[128,256]{1,0:T(8,128)(2,1...) custom-call(bf16[256,128]{1,0:T(8,128)(2,1)S(1)} %get-tuple-element.74.b.refs_4_, ...), custom_call_target="tpu_custom_call" | custom-call | flops 1000 | bytes 256 | tf_op jit(solution)/shard_map/pallas_call | solution.py:27
  3.3 0.7 %shard_map.138 = (f32[4,128,128]{2,1,0:T(8,128)S(1)}, f32[4,128,128]{2,1,0:T(8,128)S(1)}, bf16[4,256,128]{2,1,0:T(8,128)(2,1)S(1)}, f32[4,256,128]{2,1,0:T(8,128)S(1)}, f32[4,256,128]{2,1,0:T(8,128)S(1)}) custom-call(bf16[8,256,128]{2,1,0:T(8,128)(2,1)S(1)} %get-tuple-element.73.x.refs_0_, bf16[8,256,128]{2,1,0:T(8,128)(2,1)S(1)} %get-tuple-element.85.t, ...), custom_call_target="tpu_custom_call" | custom-call | flops 4000 | bytes 256 | tf_op jit(solution)/shard_map/pallas_call | solution.py:27
  4.0 5.2 %collective-permute-start.1 = (f32[4,128,128]{2,1,0:T(8,128)S(1)}, f32[4,128,128]{2,1,0:T(8,128)S(1)}, u32[]{:S(2)}, u32[]{:S(2)}) collective-permute-start(f32[4,128,128]{2,1,0:T(8,128)S(1)} %shard_map.143), channel_id=1, source_target_pairs={{0,8},{1,9},{2,10},{3,11},{8,0},{9,1},{10,2},{11,3},{16,24},{17,25... | collective-permute-start | bytes 786440 | tf_op jit(solution)/shard_map/ppermute | solution.py:331
  9.2 0.7 %shard_map.140 = (f32[4,128,128]{2,1,0:T(8,128)S(1)}, f32[4,128,128]{2,1,0:T(8,128)S(1)}, bf16[4,256,128]{2,1,0:T(8,128)(2,1)S(1)}, f32[4,256,128]{2,1,0:T(8,128)S(1)}, f32[4,256,128]{2,1,0:T(8,128)S(1)}) custom-call(bf16[8,256,128]{2,1,0:T(8,128)(2,1)S(1)} %get-tuple-element.73.x.refs_0_, bf16[8,256,128]{2,1,0:T(8,128)(2,1)S(1)} %get-tuple-element.85.t, ...), custom_call_target="tpu_custom_call" | custom-call | flops 4000 | bytes 256 | tf_op jit(solution)/shard_map/pallas_call | solution.py:27
  9.9 0.0 collective-permute-done.refs_0_
  10.0 0.8 %collective-permute-start.5 = (f32[4,128,128]{2,1,0:T(8,128)S(1)}, f32[4,128,128]{2,1,0:T(8,128)S(1)}, u32[]{:S(2)}, u32[]{:S(2)}) collective-permute-start(f32[4,128,128]{2,1,0:T(8,128)S(1)} %get-tuple-element.114), channel_id=1, source_target_pairs={{0,8},{1,9},{2,10},{3,11},{8,0},{9,1},{10,2},{11,3},{16,24},{17,25... | collective-permute-start | bytes 786440 | tf_op jit(solution)/shard_map/ppermute | solution.py:331
  10.8 0.0 collective-permute-start.2
  10.8 0.4 shard_map.137
  11.2 0.3 shard_map.139.m
  11.5 0.8 %shard_map.142 = (f32[8,128,128]{2,1,0:T(8,128)S(1)}, f32[8,128]{1,0:T(8,128)S(1)}) custom-call(f32[128,8]{1,0:T(8,128)S(1)} %get-tuple-element.93.sides, f32[272,128]{1,0:T(8,128)S(1)} %get-tuple-element.99.got), custom_call_target="tpu_custom_call" | custom-call | flops 1000 | bytes 256 | tf_op jit(solution)/shard_map/pallas_call | solution.py:27
  12.3 4.1 %collective-permute-done.1.got = f32[4,128,128]{2,1,0:T(8,128)S(1)} collective-permute-done((f32[4,128,128]{2,1,0:T(8,128)S(1)}, f32[4,128,128]{2,1,0:T(8,128)S(1)}, u32[]{:S(2)}, u32[]{:S(2)}) %collective-permute-start.1) | collective-permute-done | bytes 262176 | tf_op jit(solution)/shard_map/ppermute | solution.py:331
  16.4 0.0 collective-permute-done.2.refs_0_
  16.4 0.3 shard_map.144
  16.8 0.1 collective-permute-start.3
  16.9 1.1 %shard_map.145 = (f32[8,128,128]{2,1,0:T(8,128)S(1)}, f32[8,128]{1,0:T(8,128)}) custom-call(f32[128,8]{1,0:T(8,128)S(1)} %get-tuple-element.93.sides, f32[272,128]{1,0:T(8,128)S(1)} %get-tuple-element.101.got, f32[8,128,128]{2,1,0:T(8,128)S(1)} %get-tuple-element.100.mc.refs_0_, f32[8,128]{1,0:T(8,128)S(1)} %get-tuple-element.102.refs_1_), custom_call_target="tpu_custom_call" | custom-call | flops 1000 | bytes 256 | tf_op jit(solution)/shard_map/pallas_call | solution.py:27
  18.0 2.9 %collective-permute-done.5.got = f32[4,128,128]{2,1,0:T(8,128)S(1)} collective-permute-done((f32[4,128,128]{2,1,0:T(8,128)S(1)}, f32[4,128,128]{2,1,0:T(8,128)S(1)}, u32[]{:S(2)}, u32[]{:S(2)}) %collective-permute-start.5) | collective-permute-done | bytes 262176 | tf_op jit(solution)/shard_map/ppermute | solution.py:331
  20.9 0.3 shard_map.148
  21.2 0.1 collective-permute-start.6
  21.3 0.0 collective-permute-done.3.got
  21.3 0.4 shard_map.146
  21.7 4.6 %collective-permute-start.4 = (f32[4,128,128]{2,1,0:T(8,128)S(1)}, f32[4,128,128]{2,1,0:T(8,128)S(1)}, u32[]{:S(2)}, u32[]{:S(2)}) collective-permute-start(f32[4,128,128]{2,1,0:T(8,128)S(1)} %get-tuple-element.107), channel_id=1, source_target_pairs={{0,8},{1,9},{2,10},{3,11},{8,0},{9,1},{10,2},{11,3},{16,24},{17,25... | collective-permute-start | bytes 786440 | tf_op jit(solution)/shard_map/ppermute | solution.py:331
  26.3 0.0 collective-permute-done.6.got
  26.3 0.4 shard_map.149
  26.7 4.7 %collective-permute-start.7 = (f32[4,128,128]{2,1,0:T(8,128)S(1)}, f32[4,128,128]{2,1,0:T(8,128)S(1)}, u32[]{:S(2)}, u32[]{:S(2)}) collective-permute-start(f32[4,128,128]{2,1,0:T(8,128)S(1)} %get-tuple-element.118), channel_id=1, source_target_pairs={{0,8},{1,9},{2,10},{3,11},{8,0},{9,1},{10,2},{11,3},{16,24},{17,25... | collective-permute-start | bytes 786440 | tf_op jit(solution)/shard_map/ppermute | solution.py:331
  31.4 0.0 collective-permute-done.4.refs_12_
  31.4 1.1 %shard_map.147 = (bf16[4,256,128]{2,1,0:T(8,128)(2,1)S(1)}, bf16[256,512]{1,0:T(8,128)(2,1)S(1)}, bf16[128,512]{1,0:T(8,128)(2,1)S(1)}, bf16[128,512]{1,0:T(8,12...) custom-call(bf16[8,256,128]{2,1,0:T(8,128)(2,1)S(1)} %get-tuple-element.73.x.refs_0_, ...), custom_call_target="tpu_custom_call" | custom-call | flops 4000 | bytes 256 | tf_op jit(solution)/shard_map/pallas_call | solution.py:27
  32.5 4.1 %collective-permute-done.7.refs_12_ = f32[4,128,128]{2,1,0:T(8,128)S(1)} collective-permute-done((f32[4,128,128]{2,1,0:T(8,128)S(1)}, f32[4,128,128]{2,1,0:T(8,128)S(1)}, u32[]{:S(2)}, u32[]{:S(2)}) %collective-permute-start.7) | collective-permute-done | bytes 262176 | tf_op jit(solution)/shard_map/ppermute | solution.py:331
  36.6 1.1 %shard_map.150 = (bf16[4,256,128]{2,1,0:T(8,128)(2,1)S(1)}, bf16[256,512]{1,0:T(8,128)(2,1)S(1)}, bf16[128,512]{1,0:T(8,128)(2,1)S(1)}, bf16[128,512]{1,0:T(8,12...) custom-call(bf16[8,256,128]{2,1,0:T(8,128)(2,1)S(1)} %get-tuple-element.73.x.refs_0_, ...), custom_call_target="tpu_custom_call" | custom-call | flops 4000 | bytes 256 | tf_op jit(solution)/shard_map/pallas_call | solution.py:27
  37.7 0.1 collective-permute-start.8
  37.8 0.8 %shard_map.152.grads = f32[2,256,128]{2,1,0:T(8,128)S(1)} custom-call(bf16[256,128]{1,0:T(8,128)(2,1)S(1)} %get-tuple-element.74.b.refs_4_, bf16[256,128]{1,0:T(8,128)(2,1)S(1)} %get-tuple-element.75.c.refs_5_, bf16[4,256,128]{2,1,0:T(8,128)(2,1)S(1)} %get-tuple-element.89.refs_7_.refs_0_, bf16[4,256,128]{2,1,0:T(8,128)(2,1)S(1)} %get-tuple-element.111.refs_7_.refs_1_, ...), custom_call_target="tpu_custom_call" | custom-call | flops 4000 | bytes 256 | tf_op jit(solution)/shard_map/pallas_call | solution.py:27
  38.6 0.3 collective-permute-done.8.refs_1_
  39.0 1.6 %collective-permute-start.9 = (f32[2,128,128]{2,1,0:T(8,128)S(1)}, f32[2,128,128]{2,1,0:T(8,128)S(1)}, u32[]{:S(2)}, u32[]{:S(2)}) collective-permute-start(f32[2,128,128]{2,1,0:T(8,128)S(1)} %get-tuple-element.135), channel_id=1, source_target_pairs={{0,4},{4,0},{1,5},{5,1},{2,6},{6,2},{3,7},{7,3},{8,12},{12,8},{9,1... | collective-permute-start | bytes 393224 | tf_op jit(solution)/shard_map/ppermute | solution.py:432
  40.6 3.3 %collective-permute-start.10 = (f32[8,128]{1,0:T(8,128)S(1)}, f32[8,128]{1,0:T(8,128)S(1)}, u32[]{:S(2)}, u32[]{:S(2)}) collective-permute-start(f32[8,128]{1,0:T(8,128)S(1)} %get-tuple-element.134.refs_1_), channel_id=1, source_target_pairs={{0,16},{8,24},{16,0},{24,8},{1,17},{9,25},{17,1},{25,9},{2,18},{10... | collective-permute-start | bytes 12296 | tf_op jit(solution)/shard_map/ppermute | solution.py:418
  43.9 1.6 %collective-permute-done.10.refs_3_ = f32[8,128]{1,0:T(8,128)S(1)} collective-permute-done((f32[8,128]{1,0:T(8,128)S(1)}, f32[8,128]{1,0:T(8,128)S(1)}, u32[]{:S(2)}, u32[]{:S(2)}) %collective-permute-start.10) | collective-permute-done | bytes 4128 | tf_op jit(solution)/shard_map/ppermute | solution.py:418
  45.5 0.0 collective-permute-done.9.refs_2_
  45.5 1.4 %collective-permute-start.11 = (f32[8,128]{1,0:T(8,128)S(1)}, f32[8,128]{1,0:T(8,128)S(1)}, u32[]{:S(2)}, u32[]{:S(2)}) collective-permute-start(f32[8,128]{1,0:T(8,128)S(1)} %get-tuple-element.138), channel_id=1, source_target_pairs={{0,8},{8,0},{16,24},{24,16},{1,9},{9,1},{17,25},{25,17},{2,10},{10... | collective-permute-start | bytes 12296 | tf_op jit(solution)/shard_map/ppermute | solution.py:418
  46.9 1.4 %shard_map.151 = (bf16[8,256,128]{2,1,0:T(8,128)(2,1)}, f32[8,256]{1,0:T(8,128)}) custom-call(bf16[4,256,128]{2,1,0:T(8,128)(2,1)S(1)} %get-tuple-element.110.refs_0_, bf16[4,256,128]{2,1,0:T(8,128)(2,1)S(1)} %get-tuple-element.123.refs_1_, f32[2,256,128]{2,1,0:T(8,128)S(1)} %get-tuple-element.83.refs_2_, ...), custom_call_target="tpu_custom_call" | custom-call | flops 1000 | bytes 256 | tf_op jit(solution)/shard_map/pallas_call | solution.py:27
  48.3 0.8 %collective-permute-done.11 = f32[8,128]{1,0:T(8,128)S(1)} collective-permute-done((f32[8,128]{1,0:T(8,128)S(1)}, f32[8,128]{1,0:T(8,128)S(1)}, u32[]{:S(2)}, u32[]{:S(2)}) %collective-permute-start.11) | collective-permute-done | bytes 4128 | tf_op jit(solution)/shard_map/ppermute | solution.py:418
  49.2 1.5 %collective-permute-start.12 = (f32[8,128]{1,0:T(8,128)S(1)}, f32[8,128]{1,0:T(8,128)S(1)}, u32[]{:S(2)}, u32[]{:S(2)}) collective-permute-start(f32[8,128]{1,0:T(8,128)S(1)} %add.6), channel_id=1, source_target_pairs={{0,2},{1,3},{2,0},{3,1},{4,6},{5,7},{6,4},{7,5},{8,10},{9,11},{10,... | collective-permute-start | bytes 12296 | tf_op jit(solution)/shard_map/ppermute | solution.py:418
  50.6 0.7 %fusion = (f32[1,128,128]{2,1,0:T(8,128)}, f32[1,128,128]{2,1,0:T(8,128)}) fusion(f32[2,128,128]{2,1,0:T(8,128)S(1)} %get-tuple-element.136), kind=kLoop, calls=%fused_computation.3 | loop fusion | bytes 262144 | tf_op jit(solution)/shard_map/slice | solution.py:449
  51.3 1.5 %collective-permute-done.12 = f32[8,128]{1,0:T(8,128)S(1)} collective-permute-done((f32[8,128]{1,0:T(8,128)S(1)}, f32[8,128]{1,0:T(8,128)S(1)}, u32[]{:S(2)}, u32[]{:S(2)}) %collective-permute-start.12) | collective-permute-done | bytes 4128 | tf_op jit(solution)/shard_map/ppermute | solution.py:418
  52.8 0.5 slice_bitcast_fusion
  (9 shorter events, 0.2 us)
Async XLA Ops:
  2.1 7.9 %collective-permute-start = (f32[272,128]{1,0:T(8,128)S(1)}, f32[272,128]{1,0:T(8,128)S(1)}, u32[]{:S(2)}, u32[]{:S(2)}) collective-permute-start(f32[272,128]{1,0:T(8,128)S(1)} %get-tuple-element.98), channel_id=1, source_target_pairs={{0,1},{1,0},{2,3},{3,2},{8,24},{9,25},{10,26},{11,27},{16,8},{17,9... | collective-permute-start | bytes 417800 | tf_op jit(solution)/shard_map/ppermute | solution.py:331
  4.0 12.4 %collective-permute-start.1 = (f32[4,128,128]{2,1,0:T(8,128)S(1)}, f32[4,128,128]{2,1,0:T(8,128)S(1)}, u32[]{:S(2)}, u32[]{:S(2)}) collective-permute-start(f32[4,128,128]{2,1,0:T(8,128)S(1)} %shard_map.143), channel_id=1, source_target_pairs={{0,8},{1,9},{2,10},{3,11},{8,0},{9,1},{10,2},{11,3},{16,24},{17,25... | collective-permute-start | bytes 786440 | tf_op jit(solution)/shard_map/ppermute | solution.py:331
  10.0 10.9 %collective-permute-start.5 = (f32[4,128,128]{2,1,0:T(8,128)S(1)}, f32[4,128,128]{2,1,0:T(8,128)S(1)}, u32[]{:S(2)}, u32[]{:S(2)}) collective-permute-start(f32[4,128,128]{2,1,0:T(8,128)S(1)} %get-tuple-element.114), channel_id=1, source_target_pairs={{0,8},{1,9},{2,10},{3,11},{8,0},{9,1},{10,2},{11,3},{16,24},{17,25... | collective-permute-start | bytes 786440 | tf_op jit(solution)/shard_map/ppermute | solution.py:331
  10.8 5.6 %collective-permute-start.2 = (f32[272,128]{1,0:T(8,128)S(1)}, f32[272,128]{1,0:T(8,128)S(1)}, u32[]{:S(2)}, u32[]{:S(2)}) collective-permute-start(f32[272,128]{1,0:T(8,128)S(1)} %get-tuple-element.99.got), channel_id=1, source_target_pairs={{0,1},{1,0},{2,3},{3,2},{8,16},{9,17},{10,18},{11,19},{16,8},{17,9... | collective-permute-start | bytes 417800 | tf_op jit(solution)/shard_map/ppermute | solution.py:331
  16.8 4.5 %collective-permute-start.3 = (f32[4,128,128]{2,1,0:T(8,128)S(1)}, f32[4,128,128]{2,1,0:T(8,128)S(1)}, u32[]{:S(2)}, u32[]{:S(2)}) collective-permute-start(f32[4,128,128]{2,1,0:T(8,128)S(1)} %get-tuple-element.104), channel_id=1, source_target_pairs={{0,1},{1,0},{2,3},{3,2},{8,16},{9,17},{10,18},{11,19},{16,8},{17,9... | collective-permute-start | bytes 786440 | tf_op jit(solution)/shard_map/ppermute | solution.py:331
  21.2 5.1 %collective-permute-start.6 = (f32[4,128,128]{2,1,0:T(8,128)S(1)}, f32[4,128,128]{2,1,0:T(8,128)S(1)}, u32[]{:S(2)}, u32[]{:S(2)}) collective-permute-start(f32[4,128,128]{2,1,0:T(8,128)S(1)} %get-tuple-element.115), channel_id=1, source_target_pairs={{0,1},{1,0},{2,3},{3,2},{8,16},{9,17},{10,18},{11,19},{16,8},{17,9... | collective-permute-start | bytes 786440 | tf_op jit(solution)/shard_map/ppermute | solution.py:331
  21.7 9.7 %collective-permute-start.4 = (f32[4,128,128]{2,1,0:T(8,128)S(1)}, f32[4,128,128]{2,1,0:T(8,128)S(1)}, u32[]{:S(2)}, u32[]{:S(2)}) collective-permute-start(f32[4,128,128]{2,1,0:T(8,128)S(1)} %get-tuple-element.107), channel_id=1, source_target_pairs={{0,8},{1,9},{2,10},{3,11},{8,0},{9,1},{10,2},{11,3},{16,24},{17,25... | collective-permute-start | bytes 786440 | tf_op jit(solution)/shard_map/ppermute | solution.py:331
  26.7 9.9 %collective-permute-start.7 = (f32[4,128,128]{2,1,0:T(8,128)S(1)}, f32[4,128,128]{2,1,0:T(8,128)S(1)}, u32[]{:S(2)}, u32[]{:S(2)}) collective-permute-start(f32[4,128,128]{2,1,0:T(8,128)S(1)} %get-tuple-element.118), channel_id=1, source_target_pairs={{0,8},{1,9},{2,10},{3,11},{8,0},{9,1},{10,2},{11,3},{16,24},{17,25... | collective-permute-start | bytes 786440 | tf_op jit(solution)/shard_map/ppermute | solution.py:331
  37.7 1.2 %collective-permute-start.8 = (f32[8,128]{1,0:T(8,128)S(1)}, f32[8,128]{1,0:T(8,128)S(1)}, u32[]{:S(2)}, u32[]{:S(2)}) collective-permute-start(f32[8,128]{1,0:T(8,128)S(1)} %get-tuple-element.132.refs_0_), channel_id=1, source_target_pairs={{0,1},{1,0},{2,3},{3,2},{4,5},{5,4},{6,7},{7,6},{8,9},{9,8},{10,11... | collective-permute-start | bytes 12296 | tf_op jit(solution)/shard_map/ppermute | solution.py:418
  39.0 6.5 %collective-permute-start.9 = (f32[2,128,128]{2,1,0:T(8,128)S(1)}, f32[2,128,128]{2,1,0:T(8,128)S(1)}, u32[]{:S(2)}, u32[]{:S(2)}) collective-permute-start(f32[2,128,128]{2,1,0:T(8,128)S(1)} %get-tuple-element.135), channel_id=1, source_target_pairs={{0,4},{4,0},{1,5},{5,1},{2,6},{6,2},{3,7},{7,3},{8,12},{12,8},{9,1... | collective-permute-start | bytes 393224 | tf_op jit(solution)/shard_map/ppermute | solution.py:432
  40.6 4.9 %collective-permute-start.10 = (f32[8,128]{1,0:T(8,128)S(1)}, f32[8,128]{1,0:T(8,128)S(1)}, u32[]{:S(2)}, u32[]{:S(2)}) collective-permute-start(f32[8,128]{1,0:T(8,128)S(1)} %get-tuple-element.134.refs_1_), channel_id=1, source_target_pairs={{0,16},{8,24},{16,0},{24,8},{1,17},{9,25},{17,1},{25,9},{2,18},{10... | collective-permute-start | bytes 12296 | tf_op jit(solution)/shard_map/ppermute | solution.py:418
  45.5 3.7 %collective-permute-start.11 = (f32[8,128]{1,0:T(8,128)S(1)}, f32[8,128]{1,0:T(8,128)S(1)}, u32[]{:S(2)}, u32[]{:S(2)}) collective-permute-start(f32[8,128]{1,0:T(8,128)S(1)} %get-tuple-element.138), channel_id=1, source_target_pairs={{0,8},{8,0},{16,24},{24,16},{1,9},{9,1},{17,25},{25,17},{2,10},{10... | collective-permute-start | bytes 12296 | tf_op jit(solution)/shard_map/ppermute | solution.py:418
  49.2 3.6 %collective-permute-start.12 = (f32[8,128]{1,0:T(8,128)S(1)}, f32[8,128]{1,0:T(8,128)S(1)}, u32[]{:S(2)}, u32[]{:S(2)}) collective-permute-start(f32[8,128]{1,0:T(8,128)S(1)} %add.6), channel_id=1, source_target_pairs={{0,2},{1,3},{2,0},{3,1},{4,6},{5,7},{6,4},{7,5},{8,10},{9,11},{10,... | collective-permute-start | bytes 12296 | tf_op jit(solution)/shard_map/ppermute | solution.py:418

commit v8 on v7

--- a/solution.py
+++ b/solution.py
@@ -115,7 +115,8 @@
     return jnp.concatenate(parts, axis=1)
 
 
-def first_body(heads, x, t, cols, low, b_t, c_t, rows, f_out, p_out, xr_out, y_out, err_out):
+def first_body(heads, x, t, cols, low, b_t, c_t, rows, f_out, p_out, pay_out, xr_out, y_out, err_out):
+    first = lax.axis_index("ctx") == 0
     channels = x.shape[2]
     spans = [slice(k * channels, (k + 1) * channels) for k in range(len(heads))]
     for k, h in enumerate(heads):
@@ -132,15 +133,10 @@
     pulled = dot(c_t[...], side_by_side(weighted))
     for k, h in enumerate(heads):
         scale = rows[0:1, h : h + 1]
-        f_out[k] = scale * contrib[:, spans[k]]
-        p_out[k] = scale * pulled[:, spans[k]]
-
-
-def send_body(f, p, *refs):
-    count = len(refs) // 2
-    refs[count][...] = jnp.where(lax.axis_index("ctx") == 0, f[...], p[...])
-    for relay, out in zip(refs[:count], refs[count + 1 :]):
-        out[...] = relay[...]
+        f, p = scale * contrib[:, spans[k]], scale * pulled[:, spans[k]]
+        f_out[k] = f
+        p_out[k] = p
+        pay_out[k] = jnp.where(first, f, p)
 
 
 def own_map_body(c, c_t, sq, m_out):
@@ -345,17 +341,14 @@
     held = []
     for group in groups:
         states, panel = shape((len(group), width, channels), f32), (len(group), size, channels)
-        f, p, xr, y, err = call(
+        f, p, pay, xr, y, err = call(
             functools.partial(first_body, group),
-            [states, states, shape(panel, bf16), shape(panel, f32), shape(panel, f32)],
+            [states, states, states, shape(panel, bf16), shape(panel, f32), shape(panel, f32)],
             x, t, cols, low, b_t, c_t, rows, flops=4 * 10**8,
         )
         zero = jnp.zeros(states.shape, f32)
-        held.append(dict(f=f, p=p, xr=xr, y=y, err=err, s=zero, d=zero))
-    held[0]["pay"], = call(send_body, like(held[0]["f"]), held[0]["f"], held[0]["p"])
+        held.append(dict(f=f, p=p, pay=pay, xr=xr, y=y, err=err, s=zero, d=zero))
     (m,) = call(own_map_body, [all_states], c, c_t, sq)
-    for h in held[1:]:
-        h["pay"], later = call(send_body, like(h["f"], later), h["f"], h["p"], later)
     layouts = [later]
     for step in range(2, n - lowest):
         layouts.append(down(step, layouts[-1]))

time: 53.4 us -> 53 us (level)
  starting transfers between devices: 23.9 us -> 23 us
    ppermute x8, waiting for transfers between devices: 11.1 us -> 11.8 us  [exchange(): return lax.ppermute(value, ('ctx', 'seq'), pairs)]
    ppermute x8, starting transfers between devices: 16 us -> 15.3 us  [exchange(): return lax.ppermute(value, ('ctx', 'seq'), pairs)]
    pallas_call x20 -> x18, Pallas kernels: 12.1 us -> 12 us  [call(): pl.pallas_call(body, out_shape=outs, in_specs=ins or [VMEM] * len(args),...]
where the time goes in v8:
time: 53 us; the launch traced here: 52.9 us
  starting transfers between devices  23 us (43%)
  waiting for transfers between devices  15.7 us (30%)
  Pallas kernels  12 us (23%)
  local copies, waits for them, and re-layouts  1.22 us (2%)
  between operations  0.81 us (2%)
    ppermute x8, starting transfers between devices, exchange(): return lax.ppermute(value, ('ctx', 'seq'), pairs)  15.3 us
    pallas_call x18, Pallas kernels, call(): pl.pallas_call(body, out_shape=outs, in_specs=ins or [VMEM] * len(args),...  12 us
    ppermute x8, waiting for transfers between devices, exchange(): return lax.ppermute(value, ('ctx', 'seq'), pairs)  11.8 us
    ppermute x4, starting transfers between devices, swapped(): return lax.ppermute(value, axis, [(i, i ^ by) for i in range(spans[axis])])  6.16 us
    ppermute x4, waiting for transfers between devices, swapped(): return lax.ppermute(value, axis, [(i, i ^ by) for i in range(spans[axis])])  3.94 us
    ppermute x1, starting transfers between devices, on_device(): received = lax.ppermute(send, 'head', [(i, i ^ step) for i in range(parts)])  1.58 us
  transfers between devices with their start and end apart: 13, of which 7 were waited for; matrix products, arithmetic and copies ran while one was open for 1% of the time, Pallas kernels for 18%

profile of v8, /device:TPU:0, one launch (start us, length us, event | category | flops | bytes accessed | tf_op | source)
XLA Modules:
  0.0 52.9 jit_solution(12059564748376270603)
XLA Ops:
  0.6 1.4 %shard_map.135 = (bf16[256,128]{1,0:T(8,128)(2,1)S(1)}, f32[8,256]{1,0:T(8,128)S(1)}, f32[1,8]{1,0:T(1,128)S(1)}, f32[1,8]{1,0:T(1,128)S(1)}, f32[1,8]{1,0:T(1,1...) custom-call(bf16[256,128]{1,0:T(8,128)(2,1)} %bitcast.18, ...), custom_call_target="tpu_custom_call" | custom-call | flops 10 | bytes 256 | tf_op jit(solution)/shard_map/pallas_call | solution.py:27
  2.1 0.5 collective-permute-start
  2.6 0.7 %shard_map.136 = (f32[4,256,128]{2,1,0:T(8,128)S(1)}, bf16[256,256]{1,0:T(8,128)(2,1)S(1)}, bf16[128,256]{1,0:T(8,128)(2,1)S(1)}, bf16[128,256]{1,0:T(8,128)(2,1...) custom-call(bf16[256,128]{1,0:T(8,128)(2,1)S(1)} %get-tuple-element.74.b.refs_4_, ...), custom_call_target="tpu_custom_call" | custom-call | flops 1000 | bytes 256 | tf_op jit(solution)/shard_map/pallas_call | solution.py:27
  3.3 0.7 %shard_map.138 = (f32[4,128,128]{2,1,0:T(8,128)S(1)}, f32[4,128,128]{2,1,0:T(8,128)S(1)}, f32[4,128,128]{2,1,0:T(8,128)S(1)}, bf16[4,256,128]{2,1,0:T(8,128)(2,1...) custom-call(bf16[8,256,128]{2,1,0:T(8,128)(2,1)S(1)} %get-tuple-element.73.x.refs_0_, ...), custom_call_target="tpu_custom_call" | custom-call | flops 4000 | bytes 256 | tf_op jit(solution)/shard_map/pallas_call | solution.py:27
  4.0 5.2 %collective-permute-start.1 = (f32[4,128,128]{2,1,0:T(8,128)S(1)}, f32[4,128,128]{2,1,0:T(8,128)S(1)}, u32[]{:S(2)}, u32[]{:S(2)}) collective-permute-start(f32[4,128,128]{2,1,0:T(8,128)S(1)} %get-tuple-element.98), channel_id=1, source_target_pairs={{0,8},{1,9},{2,10},{3,11},{8,0},{9,1},{10,2},{11,3},{16,24},{17,25... | collective-permute-start | bytes 786440 | tf_op jit(solution)/shard_map/ppermute | solution.py:327
  9.2 0.7 %shard_map.145 = (f32[4,128,128]{2,1,0:T(8,128)S(1)}, f32[4,128,128]{2,1,0:T(8,128)S(1)}, f32[4,128,128]{2,1,0:T(8,128)S(1)}, bf16[4,256,128]{2,1,0:T(8,128)(2,1...) custom-call(bf16[8,256,128]{2,1,0:T(8,128)(2,1)S(1)} %get-tuple-element.73.x.refs_0_, ...), custom_call_target="tpu_custom_call" | custom-call | flops 4000 | bytes 256 | tf_op jit(solution)/shard_map/pallas_call | solution.py:27
  9.9 0.1 collective-permute-start.5
  10.0 0.0 collective-permute-done.got
  10.0 0.1 collective-permute-start.2
  10.0 0.4 shard_map.137
  10.5 0.3 shard_map.139.m
  10.8 0.8 %shard_map.140 = (f32[8,128,128]{2,1,0:T(8,128)S(1)}, f32[8,128]{1,0:T(8,128)S(1)}) custom-call(f32[128,8]{1,0:T(8,128)S(1)} %get-tuple-element.93.sides, f32[272,128]{1,0:T(8,128)S(1)} %collective-permute-done.got), custom_call_target="tpu_custom_call" | custom-call | flops 1000 | bytes 256 | tf_op jit(solution)/shard_map/pallas_call | solution.py:27
  11.5 4.8 %collective-permute-done.1.got = f32[4,128,128]{2,1,0:T(8,128)S(1)} collective-permute-done((f32[4,128,128]{2,1,0:T(8,128)S(1)}, f32[4,128,128]{2,1,0:T(8,128)S(1)}, u32[]{:S(2)}, u32[]{:S(2)}) %collective-permute-start.1) | collective-permute-done | bytes 262176 | tf_op jit(solution)/shard_map/ppermute | solution.py:327
  16.4 0.0 collective-permute-done.2.refs_0_
  16.4 0.3 shard_map.141
  16.7 0.1 collective-permute-start.3
  16.8 1.1 %shard_map.142 = (f32[8,128,128]{2,1,0:T(8,128)S(1)}, f32[8,128]{1,0:T(8,128)}) custom-call(f32[128,8]{1,0:T(8,128)S(1)} %get-tuple-element.93.sides, f32[272,128]{1,0:T(8,128)S(1)} %get-tuple-element.99.got, f32[8,128,128]{2,1,0:T(8,128)S(1)} %get-tuple-element.97.mc.refs_0_, f32[8,128]{1,0:T(8,128)S(1)} %get-tuple-element.100.refs_1_), custom_call_target="tpu_custom_call" | custom-call | flops 1000 | bytes 256 | tf_op jit(solution)/shard_map/pallas_call | solution.py:27
  18.0 2.9 %collective-permute-done.5.got = f32[4,128,128]{2,1,0:T(8,128)S(1)} collective-permute-done((f32[4,128,128]{2,1,0:T(8,128)S(1)}, f32[4,128,128]{2,1,0:T(8,128)S(1)}, u32[]{:S(2)}, u32[]{:S(2)}) %collective-permute-start.5) | collective-permute-done | bytes 262176 | tf_op jit(solution)/shard_map/ppermute | solution.py:327
  20.8 0.3 shard_map.146
  21.2 0.1 collective-permute-start.6
  21.2 0.0 collective-permute-done.3.got
  21.3 0.4 shard_map.143
  21.6 4.6 %collective-permute-start.4 = (f32[4,128,128]{2,1,0:T(8,128)S(1)}, f32[4,128,128]{2,1,0:T(8,128)S(1)}, u32[]{:S(2)}, u32[]{:S(2)}) collective-permute-start(f32[4,128,128]{2,1,0:T(8,128)S(1)} %get-tuple-element.105), channel_id=1, source_target_pairs={{0,8},{1,9},{2,10},{3,11},{8,0},{9,1},{10,2},{11,3},{16,24},{17,25... | collective-permute-start | bytes 786440 | tf_op jit(solution)/shard_map/ppermute | solution.py:327
  26.2 0.0 collective-permute-done.6.got
  26.2 0.4 shard_map.147
  26.6 4.7 %collective-permute-start.7 = (f32[4,128,128]{2,1,0:T(8,128)S(1)}, f32[4,128,128]{2,1,0:T(8,128)S(1)}, u32[]{:S(2)}, u32[]{:S(2)}) collective-permute-start(f32[4,128,128]{2,1,0:T(8,128)S(1)} %get-tuple-element.118), channel_id=1, source_target_pairs={{0,8},{1,9},{2,10},{3,11},{8,0},{9,1},{10,2},{11,3},{16,24},{17,25... | collective-permute-start | bytes 786440 | tf_op jit(solution)/shard_map/ppermute | solution.py:327
  31.3 0.0 collective-permute-done.4.refs_12_
  31.4 1.1 %shard_map.144 = (bf16[4,256,128]{2,1,0:T(8,128)(2,1)S(1)}, bf16[256,512]{1,0:T(8,128)(2,1)S(1)}, bf16[128,512]{1,0:T(8,128)(2,1)S(1)}, bf16[128,512]{1,0:T(8,12...) custom-call(bf16[8,256,128]{2,1,0:T(8,128)(2,1)S(1)} %get-tuple-element.73.x.refs_0_, ...), custom_call_target="tpu_custom_call" | custom-call | flops 4000 | bytes 256 | tf_op jit(solution)/shard_map/pallas_call | solution.py:27
  32.5 4.1 %collective-permute-done.7.refs_12_ = f32[4,128,128]{2,1,0:T(8,128)S(1)} collective-permute-done((f32[4,128,128]{2,1,0:T(8,128)S(1)}, f32[4,128,128]{2,1,0:T(8,128)S(1)}, u32[]{:S(2)}, u32[]{:S(2)}) %collective-permute-start.7) | collective-permute-done | bytes 262176 | tf_op jit(solution)/shard_map/ppermute | solution.py:327
  36.5 1.1 %shard_map.148 = (bf16[4,256,128]{2,1,0:T(8,128)(2,1)S(1)}, bf16[256,512]{1,0:T(8,128)(2,1)S(1)}, bf16[128,512]{1,0:T(8,128)(2,1)S(1)}, bf16[128,512]{1,0:T(8,12...) custom-call(bf16[8,256,128]{2,1,0:T(8,128)(2,1)S(1)} %get-tuple-element.73.x.refs_0_, ...), custom_call_target="tpu_custom_call" | custom-call | flops 4000 | bytes 256 | tf_op jit(solution)/shard_map/pallas_call | solution.py:27
  37.7 0.1 collective-permute-start.8
  37.7 0.8 %shard_map.150.grads = f32[2,256,128]{2,1,0:T(8,128)S(1)} custom-call(bf16[256,128]{1,0:T(8,128)(2,1)S(1)} %get-tuple-element.74.b.refs_4_, bf16[256,128]{1,0:T(8,128)(2,1)S(1)} %get-tuple-element.75.c.refs_5_, bf16[4,256,128]{2,1,0:T(8,128)(2,1)S(1)} %get-tuple-element.89.refs_7_.refs_0_, bf16[4,256,128]{2,1,0:T(8,128)(2,1)S(1)} %get-tuple-element.109.refs_7_.refs_1_, ...), custom_call_target="tpu_custom_call" | custom-call | flops 4000 | bytes 256 | tf_op jit(solution)/shard_map/pallas_call | solution.py:27
  38.6 0.3 collective-permute-done.8.refs_1_
  38.9 1.6 %collective-permute-start.9 = (f32[2,128,128]{2,1,0:T(8,128)S(1)}, f32[2,128,128]{2,1,0:T(8,128)S(1)}, u32[]{:S(2)}, u32[]{:S(2)}) collective-permute-start(f32[2,128,128]{2,1,0:T(8,128)S(1)} %get-tuple-element.135), channel_id=1, source_target_pairs={{0,4},{4,0},{1,5},{5,1},{2,6},{6,2},{3,7},{7,3},{8,12},{12,8},{9,1... | collective-permute-start | bytes 393224 | tf_op jit(solution)/shard_map/ppermute | solution.py:425
  40.5 2.8 %collective-permute-start.10 = (f32[8,128]{1,0:T(8,128)S(1)}, f32[8,128]{1,0:T(8,128)S(1)}, u32[]{:S(2)}, u32[]{:S(2)}) collective-permute-start(f32[8,128]{1,0:T(8,128)S(1)} %get-tuple-element.134.refs_1_), channel_id=1, source_target_pairs={{0,16},{8,24},{16,0},{24,8},{1,17},{9,25},{17,1},{25,9},{2,18},{10... | collective-permute-start | bytes 12296 | tf_op jit(solution)/shard_map/ppermute | solution.py:411
  43.3 1.7 %collective-permute-done.10.refs_3_ = f32[8,128]{1,0:T(8,128)S(1)} collective-permute-done((f32[8,128]{1,0:T(8,128)S(1)}, f32[8,128]{1,0:T(8,128)S(1)}, u32[]{:S(2)}, u32[]{:S(2)}) %collective-permute-start.10) | collective-permute-done | bytes 4128 | tf_op jit(solution)/shard_map/ppermute | solution.py:411
  45.0 0.0 collective-permute-done.9.refs_2_
  45.0 1.8 %collective-permute-start.11 = (f32[8,128]{1,0:T(8,128)S(1)}, f32[8,128]{1,0:T(8,128)S(1)}, u32[]{:S(2)}, u32[]{:S(2)}) collective-permute-start(f32[8,128]{1,0:T(8,128)S(1)} %get-tuple-element.138), channel_id=1, source_target_pairs={{0,8},{8,0},{16,24},{24,16},{1,9},{9,1},{17,25},{25,17},{2,10},{10... | collective-permute-start | bytes 12296 | tf_op jit(solution)/shard_map/ppermute | solution.py:411
  46.8 1.4 %shard_map.149 = (bf16[8,256,128]{2,1,0:T(8,128)(2,1)}, f32[8,256]{1,0:T(8,128)}) custom-call(bf16[4,256,128]{2,1,0:T(8,128)(2,1)S(1)} %get-tuple-element.108.refs_0_, bf16[4,256,128]{2,1,0:T(8,128)(2,1)S(1)} %get-tuple-element.123.refs_1_, f32[2,256,128]{2,1,0:T(8,128)S(1)} %get-tuple-element.83.refs_2_, ...), custom_call_target="tpu_custom_call" | custom-call | flops 1000 | bytes 256 | tf_op jit(solution)/shard_map/pallas_call | solution.py:27
  48.3 0.4 collective-permute-done.11
  48.7 1.5 %collective-permute-start.12 = (f32[8,128]{1,0:T(8,128)S(1)}, f32[8,128]{1,0:T(8,128)S(1)}, u32[]{:S(2)}, u32[]{:S(2)}) collective-permute-start(f32[8,128]{1,0:T(8,128)S(1)} %add.6), channel_id=1, source_target_pairs={{0,2},{1,3},{2,0},{3,1},{4,6},{5,7},{6,4},{7,5},{8,10},{9,11},{10,... | collective-permute-start | bytes 12296 | tf_op jit(solution)/shard_map/ppermute | solution.py:411
  50.2 0.7 %fusion = (f32[1,128,128]{2,1,0:T(8,128)}, f32[1,128,128]{2,1,0:T(8,128)}) fusion(f32[2,128,128]{2,1,0:T(8,128)S(1)} %get-tuple-element.136), kind=kLoop, calls=%fused_computation.3 | loop fusion | bytes 262144 | tf_op jit(solution)/shard_map/slice | solution.py:442
  50.9 1.5 %collective-permute-done.12 = f32[8,128]{1,0:T(8,128)S(1)} collective-permute-done((f32[8,128]{1,0:T(8,128)S(1)}, f32[8,128]{1,0:T(8,128)S(1)}, u32[]{:S(2)}, u32[]{:S(2)}) %collective-permute-start.12) | collective-permute-done | bytes 4128 | tf_op jit(solution)/shard_map/ppermute | solution.py:411
  52.3 0.5 slice_bitcast_fusion
  (7 shorter events, 0.1 us)
Async XLA Ops:
  2.1 7.9 %collective-permute-start = (f32[272,128]{1,0:T(8,128)S(1)}, f32[272,128]{1,0:T(8,128)S(1)}, u32[]{:S(2)}, u32[]{:S(2)}) collective-permute-start(f32[272,128]{1,0:T(8,128)S(1)} %get-tuple-element.96), channel_id=1, source_target_pairs={{0,1},{1,0},{2,3},{3,2},{8,24},{9,25},{10,26},{11,27},{16,8},{17,9... | collective-permute-start | bytes 417800 | tf_op jit(solution)/shard_map/ppermute | solution.py:327
  4.0 12.4 %collective-permute-start.1 = (f32[4,128,128]{2,1,0:T(8,128)S(1)}, f32[4,128,128]{2,1,0:T(8,128)S(1)}, u32[]{:S(2)}, u32[]{:S(2)}) collective-permute-start(f32[4,128,128]{2,1,0:T(8,128)S(1)} %get-tuple-element.98), channel_id=1, source_target_pairs={{0,8},{1,9},{2,10},{3,11},{8,0},{9,1},{10,2},{11,3},{16,24},{17,25... | collective-permute-start | bytes 786440 | tf_op jit(solution)/shard_map/ppermute | solution.py:327
  9.9 11.0 %collective-permute-start.5 = (f32[4,128,128]{2,1,0:T(8,128)S(1)}, f32[4,128,128]{2,1,0:T(8,128)S(1)}, u32[]{:S(2)}, u32[]{:S(2)}) collective-permute-start(f32[4,128,128]{2,1,0:T(8,128)S(1)} %get-tuple-element.114), channel_id=1, source_target_pairs={{0,8},{1,9},{2,10},{3,11},{8,0},{9,1},{10,2},{11,3},{16,24},{17,25... | collective-permute-start | bytes 786440 | tf_op jit(solution)/shard_map/ppermute | solution.py:327
  10.0 6.4 %collective-permute-start.2 = (f32[272,128]{1,0:T(8,128)S(1)}, f32[272,128]{1,0:T(8,128)S(1)}, u32[]{:S(2)}, u32[]{:S(2)}) collective-permute-start(f32[272,128]{1,0:T(8,128)S(1)} %collective-permute-done.got), channel_id=1, source_target_pairs={{0,1},{1,0},{2,3},{3,2},{8,16},{9,17},{10,18},{11,19},{16,8},{17,9... | collective-permute-start | bytes 417800 | tf_op jit(solution)/shard_map/ppermute | solution.py:327
  16.7 4.5 %collective-permute-start.3 = (f32[4,128,128]{2,1,0:T(8,128)S(1)}, f32[4,128,128]{2,1,0:T(8,128)S(1)}, u32[]{:S(2)}, u32[]{:S(2)}) collective-permute-start(f32[4,128,128]{2,1,0:T(8,128)S(1)} %get-tuple-element.102), channel_id=1, source_target_pairs={{0,1},{1,0},{2,3},{3,2},{8,16},{9,17},{10,18},{11,19},{16,8},{17,9... | collective-permute-start | bytes 786440 | tf_op jit(solution)/shard_map/ppermute | solution.py:327
  21.2 5.0 %collective-permute-start.6 = (f32[4,128,128]{2,1,0:T(8,128)S(1)}, f32[4,128,128]{2,1,0:T(8,128)S(1)}, u32[]{:S(2)}, u32[]{:S(2)}) collective-permute-start(f32[4,128,128]{2,1,0:T(8,128)S(1)} %get-tuple-element.115), channel_id=1, source_target_pairs={{0,1},{1,0},{2,3},{3,2},{8,16},{9,17},{10,18},{11,19},{16,8},{17,9... | collective-permute-start | bytes 786440 | tf_op jit(solution)/shard_map/ppermute | solution.py:327
  21.6 9.7 %collective-permute-start.4 = (f32[4,128,128]{2,1,0:T(8,128)S(1)}, f32[4,128,128]{2,1,0:T(8,128)S(1)}, u32[]{:S(2)}, u32[]{:S(2)}) collective-permute-start(f32[4,128,128]{2,1,0:T(8,128)S(1)} %get-tuple-element.105), channel_id=1, source_target_pairs={{0,8},{1,9},{2,10},{3,11},{8,0},{9,1},{10,2},{11,3},{16,24},{17,25... | collective-permute-start | bytes 786440 | tf_op jit(solution)/shard_map/ppermute | solution.py:327
  26.6 9.9 %collective-permute-start.7 = (f32[4,128,128]{2,1,0:T(8,128)S(1)}, f32[4,128,128]{2,1,0:T(8,128)S(1)}, u32[]{:S(2)}, u32[]{:S(2)}) collective-permute-start(f32[4,128,128]{2,1,0:T(8,128)S(1)} %get-tuple-element.118), channel_id=1, source_target_pairs={{0,8},{1,9},{2,10},{3,11},{8,0},{9,1},{10,2},{11,3},{16,24},{17,25... | collective-permute-start | bytes 786440 | tf_op jit(solution)/shard_map/ppermute | solution.py:327
  37.7 1.2 %collective-permute-start.8 = (f32[8,128]{1,0:T(8,128)S(1)}, f32[8,128]{1,0:T(8,128)S(1)}, u32[]{:S(2)}, u32[]{:S(2)}) collective-permute-start(f32[8,128]{1,0:T(8,128)S(1)} %get-tuple-element.132.refs_0_), channel_id=1, source_target_pairs={{0,1},{1,0},{2,3},{3,2},{4,5},{5,4},{6,7},{7,6},{8,9},{9,8},{10,11... | collective-permute-start | bytes 12296 | tf_op jit(solution)/shard_map/ppermute | solution.py:411
  38.9 6.1 %collective-permute-start.9 = (f32[2,128,128]{2,1,0:T(8,128)S(1)}, f32[2,128,128]{2,1,0:T(8,128)S(1)}, u32[]{:S(2)}, u32[]{:S(2)}) collective-permute-start(f32[2,128,128]{2,1,0:T(8,128)S(1)} %get-tuple-element.135), channel_id=1, source_target_pairs={{0,4},{4,0},{1,5},{5,1},{2,6},{6,2},{3,7},{7,3},{8,12},{12,8},{9,1... | collective-permute-start | bytes 393224 | tf_op jit(solution)/shard_map/ppermute | solution.py:425
  40.5 4.5 %collective-permute-start.10 = (f32[8,128]{1,0:T(8,128)S(1)}, f32[8,128]{1,0:T(8,128)S(1)}, u32[]{:S(2)}, u32[]{:S(2)}) collective-permute-start(f32[8,128]{1,0:T(8,128)S(1)} %get-tuple-element.134.refs_1_), channel_id=1, source_target_pairs={{0,16},{8,24},{16,0},{24,8},{1,17},{9,25},{17,1},{25,9},{2,18},{10... | collective-permute-start | bytes 12296 | tf_op jit(solution)/shard_map/ppermute | solution.py:411
  45.0 3.7 %collective-permute-start.11 = (f32[8,128]{1,0:T(8,128)S(1)}, f32[8,128]{1,0:T(8,128)S(1)}, u32[]{:S(2)}, u32[]{:S(2)}) collective-permute-start(f32[8,128]{1,0:T(8,128)S(1)} %get-tuple-element.138), channel_id=1, source_target_pairs={{0,8},{8,0},{16,24},{24,16},{1,9},{9,1},{17,25},{25,17},{2,10},{10... | collective-permute-start | bytes 12296 | tf_op jit(solution)/shard_map/ppermute | solution.py:411
  48.7 3.6 %collective-permute-start.12 = (f32[8,128]{1,0:T(8,128)S(1)}, f32[8,128]{1,0:T(8,128)S(1)}, u32[]{:S(2)}, u32[]{:S(2)}) collective-permute-start(f32[8,128]{1,0:T(8,128)S(1)} %add.6), channel_id=1, source_target_pairs={{0,2},{1,3},{2,0},{3,1},{4,6},{5,7},{6,4},{7,5},{8,10},{9,11},{10,... | collective-permute-start | bytes 12296 | tf_op jit(solution)/shard_map/ppermute | solution.py:411

commit v9 on v8

--- a/solution.py
+++ b/solution.py
@@ -383,7 +383,13 @@
                 )
                 for relay in relays:
                     maps = with_map(maps, relay)
-            h["got"] = exchange(h["pay"], swap(r))
+            if r == 1 and i and len(groups[i]) > 1:
+                half = len(groups[i]) // 2
+                one_way = sorted({(r - 1, r), (n - r, n - 1 - r)})
+                parts_of = (h["pay"][:half], h["pay"][half:])
+                h["got"] = jnp.concatenate([lax.ppermute(part, "ctx", one_way) for part in parts_of], axis=0)
+            else:
+                h["got"] = exchange(h["pay"], swap(r))
 
     tokens = size * n * x_heads.shape[0] * lax.axis_size("seq")
     scales = (1.0 / tokens, 1.0 / (tokens * channels))

time: 53 us -> 53 us (level)
  waiting for transfers between devices: 15.7 us -> 10.5 us
  starting transfers between devices: 23 us -> 28.1 us
    ppermute x8 -> x7, waiting for transfers between devices: 11.8 us -> 3.99 us  [exchange(): return lax.ppermute(value, ('ctx', 'seq'), pairs)]
    ppermute x0 -> x2, starting transfers between devices: none -> 6.5 us  [on_device(): lax.ppermute(part, 'ctx', one_way)]
    ppermute x0 -> x2, waiting for transfers between devices: none -> 1.63 us  [on_device(): lax.ppermute(part, 'ctx', one_way)]
    ppermute x4, starting transfers between devices: 6.16 us -> 5.19 us  [swapped(): return lax.ppermute(value, axis, [(i, i ^ by) for i in range(spans[axis])])]
    ppermute x4, waiting for transfers between devices: 3.94 us -> 4.91 us  [swapped(): return lax.ppermute(value, axis, [(i, i ^ by) for i in range(spans[axis])])]
    ppermute x8 -> x7, starting transfers between devices: 15.3 us -> 14.8 us  [exchange(): return lax.ppermute(value, ('ctx', 'seq'), pairs)]
  transfers between devices with their start and end apart: 13 -> 14, of which waited for: 7 -> 8; matrix products, arithmetic and copies ran while one was open for 1% -> 1% of each run, Pallas kernels for 18% -> 18%
where the time goes in v9:
time: 53 us; the launch traced here: 52.8 us
  starting transfers between devices  28.1 us (53%)
  Pallas kernels  12 us (23%)
  waiting for transfers between devices  10.5 us (20%)
  local copies, waits for them, and re-layouts  1.24 us (2%)
  between operations  0.86 us (2%)
    ppermute x7, starting transfers between devices, exchange(): return lax.ppermute(value, ('ctx', 'seq'), pairs)  14.8 us
    pallas_call x18, Pallas kernels, call(): pl.pallas_call(body, out_shape=outs, in_specs=ins or [VMEM] * len(args),...  12 us
    ppermute x2, starting transfers between devices, on_device(): lax.ppermute(part, 'ctx', one_way)  6.5 us
    ppermute x4, starting transfers between devices, swapped(): return lax.ppermute(value, axis, [(i, i ^ by) for i in range(spans[axis])])  5.19 us
    ppermute x4, waiting for transfers between devices, swapped(): return lax.ppermute(value, axis, [(i, i ^ by) for i in range(spans[axis])])  4.91 us
    ppermute x7, waiting for transfers between devices, exchange(): return lax.ppermute(value, ('ctx', 'seq'), pairs)  3.99 us
    ppermute x2, waiting for transfers between devices, on_device(): lax.ppermute(part, 'ctx', one_way)  1.63 us
    ppermute x1, starting transfers between devices, on_device(): received = lax.ppermute(send, 'head', [(i, i ^ step) for i in range(parts)])  1.59 us
  transfers between devices with their start and end apart: 14, of which 8 were waited for; matrix products, arithmetic and copies ran while one was open for 1% of the time, Pallas kernels for 18%

profile of v9, /device:TPU:0, one launch (start us, length us, event | category | flops | bytes accessed | tf_op | source)
XLA Modules:
  0.0 52.8 jit_solution(5721769559631289398)
XLA Ops:
  0.6 1.4 %shard_map.135 = (bf16[256,128]{1,0:T(8,128)(2,1)S(1)}, f32[8,256]{1,0:T(8,128)S(1)}, f32[1,8]{1,0:T(1,128)S(1)}, f32[1,8]{1,0:T(1,128)S(1)}, f32[1,8]{1,0:T(1,1...) custom-call(bf16[256,128]{1,0:T(8,128)(2,1)} %bitcast.18, ...), custom_call_target="tpu_custom_call" | custom-call | flops 10 | bytes 256 | tf_op jit(solution)/shard_map/pallas_call | solution.py:27
  2.1 0.5 collective-permute-start
  2.6 0.7 %shard_map.136 = (f32[4,256,128]{2,1,0:T(8,128)S(1)}, bf16[256,256]{1,0:T(8,128)(2,1)S(1)}, bf16[128,256]{1,0:T(8,128)(2,1)S(1)}, bf16[128,256]{1,0:T(8,128)(2,1...) custom-call(bf16[256,128]{1,0:T(8,128)(2,1)S(1)} %get-tuple-element.74.b.refs_4_, ...), custom_call_target="tpu_custom_call" | custom-call | flops 1000 | bytes 256 | tf_op jit(solution)/shard_map/pallas_call | solution.py:27
  3.3 0.7 %shard_map.138 = (f32[4,128,128]{2,1,0:T(8,128)S(1)}, f32[4,128,128]{2,1,0:T(8,128)S(1)}, f32[4,128,128]{2,1,0:T(8,128)S(1)}, bf16[4,256,128]{2,1,0:T(8,128)(2,1...) custom-call(bf16[8,256,128]{2,1,0:T(8,128)(2,1)S(1)} %get-tuple-element.73.x.refs_0_, ...), custom_call_target="tpu_custom_call" | custom-call | flops 4000 | bytes 256 | tf_op jit(solution)/shard_map/pallas_call | solution.py:27
  4.0 5.2 %collective-permute-start.1 = (f32[4,128,128]{2,1,0:T(8,128)S(1)}, f32[4,128,128]{2,1,0:T(8,128)S(1)}, u32[]{:S(2)}, u32[]{:S(2)}) collective-permute-start(f32[4,128,128]{2,1,0:T(8,128)S(1)} %get-tuple-element.98), channel_id=1, source_target_pairs={{0,8},{1,9},{2,10},{3,11},{8,0},{9,1},{10,2},{11,3},{16,24},{17,25... | collective-permute-start | bytes 786440 | tf_op jit(solution)/shard_map/ppermute | solution.py:327
  9.2 0.7 %shard_map.145 = (f32[4,128,128]{2,1,0:T(8,128)S(1)}, f32[4,128,128]{2,1,0:T(8,128)S(1)}, f32[4,128,128]{2,1,0:T(8,128)S(1)}, bf16[4,256,128]{2,1,0:T(8,128)(2,1...) custom-call(bf16[8,256,128]{2,1,0:T(8,128)(2,1)S(1)} %get-tuple-element.73.x.refs_0_, ...), custom_call_target="tpu_custom_call" | custom-call | flops 4000 | bytes 256 | tf_op jit(solution)/shard_map/pallas_call | solution.py:27
  9.9 0.0 collective-permute-done.got
  9.9 0.1 collective-permute-start.2
  10.0 5.2 %collective-permute-start.6 = (f32[2,128,128]{2,1,0:T(8,128)S(1)}, f32[2,128,128]{2,1,0:T(8,128)S(1)}, u32[]{:S(2)}, u32[]{:S(2)}) collective-permute-start(f32[2,128,128]{2,1,0:T(8,128)S(1)} %get-tuple-element.140), channel_id=1, source_target_pairs={{0,8},{24,16},{1,9},{25,17},{2,10},{26,18},{3,11},{27,19},{4,12},{... | collective-permute-start | bytes 393224 | tf_op jit(solution)/shard_map/ppermute | solution.py:390
  15.2 1.3 %collective-permute-start.5 = (f32[2,128,128]{2,1,0:T(8,128)S(1)}, f32[2,128,128]{2,1,0:T(8,128)S(1)}, u32[]{:S(2)}, u32[]{:S(2)}) collective-permute-start(f32[2,128,128]{2,1,0:T(8,128)S(1)} %get-tuple-element.139), channel_id=1, source_target_pairs={{0,8},{24,16},{1,9},{25,17},{2,10},{26,18},{3,11},{27,19},{4,12},{... | collective-permute-start | bytes 393224 | tf_op jit(solution)/shard_map/ppermute | solution.py:390
  16.5 0.4 shard_map.137
  16.9 0.3 shard_map.139.m
  17.2 0.8 %shard_map.140 = (f32[8,128,128]{2,1,0:T(8,128)S(1)}, f32[8,128]{1,0:T(8,128)S(1)}) custom-call(f32[128,8]{1,0:T(8,128)S(1)} %get-tuple-element.93.sides, f32[272,128]{1,0:T(8,128)S(1)} %collective-permute-done.got), custom_call_target="tpu_custom_call" | custom-call | flops 1000 | bytes 256 | tf_op jit(solution)/shard_map/pallas_call | solution.py:27
  18.0 0.0 collective-permute-done.1.got
  18.0 0.0 collective-permute-done.2.refs_0_
  18.0 0.3 shard_map.141
  18.4 0.1 collective-permute-start.3
  18.5 0.2 collective-permute-done.6
  18.7 1.4 %collective-permute-done.5 = f32[2,128,128]{2,1,0:T(8,128)S(1)} collective-permute-done((f32[2,128,128]{2,1,0:T(8,128)S(1)}, f32[2,128,128]{2,1,0:T(8,128)S(1)}, u32[]{:S(2)}, u32[]{:S(2)}) %collective-permute-start.5) | collective-permute-done | bytes 131104 | tf_op jit(solution)/shard_map/ppermute | solution.py:390
  20.1 1.1 %shard_map.142 = (f32[8,128,128]{2,1,0:T(8,128)S(1)}, f32[8,128]{1,0:T(8,128)}) custom-call(f32[128,8]{1,0:T(8,128)S(1)} %get-tuple-element.93.sides, f32[272,128]{1,0:T(8,128)S(1)} %get-tuple-element.99.got, f32[8,128,128]{2,1,0:T(8,128)S(1)} %get-tuple-element.97.mc.refs_0_, f32[8,128]{1,0:T(8,128)S(1)} %get-tuple-element.100.refs_1_), custom_call_target="tpu_custom_call" | custom-call | flops 1000 | bytes 256 | tf_op jit(solution)/shard_map/pallas_call | solution.py:27
  21.2 0.3 shard_map.146
  21.6 0.1 collective-permute-start.7
  21.7 0.0 collective-permute-done.3.got
  21.7 0.4 shard_map.143
  22.1 3.8 %collective-permute-start.4 = (f32[4,128,128]{2,1,0:T(8,128)S(1)}, f32[4,128,128]{2,1,0:T(8,128)S(1)}, u32[]{:S(2)}, u32[]{:S(2)}) collective-permute-start(f32[4,128,128]{2,1,0:T(8,128)S(1)} %get-tuple-element.105), channel_id=1, source_target_pairs={{0,8},{1,9},{2,10},{3,11},{8,0},{9,1},{10,2},{11,3},{16,24},{17,25... | collective-permute-start | bytes 786440 | tf_op jit(solution)/shard_map/ppermute | solution.py:327
  25.8 0.0 collective-permute-done.7.got
  25.9 0.4 shard_map.147
  26.3 5.1 %collective-permute-start.8 = (f32[4,128,128]{2,1,0:T(8,128)S(1)}, f32[4,128,128]{2,1,0:T(8,128)S(1)}, u32[]{:S(2)}, u32[]{:S(2)}) collective-permute-start(f32[4,128,128]{2,1,0:T(8,128)S(1)} %get-tuple-element.118), channel_id=1, source_target_pairs={{0,8},{1,9},{2,10},{3,11},{8,0},{9,1},{10,2},{11,3},{16,24},{17,25... | collective-permute-start | bytes 786440 | tf_op jit(solution)/shard_map/ppermute | solution.py:327
  31.3 0.5 collective-permute-done.4.refs_12_
  31.9 1.1 %shard_map.144 = (bf16[4,256,128]{2,1,0:T(8,128)(2,1)S(1)}, bf16[256,512]{1,0:T(8,128)(2,1)S(1)}, bf16[128,512]{1,0:T(8,128)(2,1)S(1)}, bf16[128,512]{1,0:T(8,12...) custom-call(bf16[8,256,128]{2,1,0:T(8,128)(2,1)S(1)} %get-tuple-element.73.x.refs_0_, ...), custom_call_target="tpu_custom_call" | custom-call | flops 4000 | bytes 256 | tf_op jit(solution)/shard_map/pallas_call | solution.py:27
  33.0 3.5 %collective-permute-done.8.refs_12_ = f32[4,128,128]{2,1,0:T(8,128)S(1)} collective-permute-done((f32[4,128,128]{2,1,0:T(8,128)S(1)}, f32[4,128,128]{2,1,0:T(8,128)S(1)}, u32[]{:S(2)}, u32[]{:S(2)}) %collective-permute-start.8) | collective-permute-done | bytes 262176 | tf_op jit(solution)/shard_map/ppermute | solution.py:327
  36.4 1.1 %shard_map.148 = (bf16[4,256,128]{2,1,0:T(8,128)(2,1)S(1)}, bf16[256,512]{1,0:T(8,128)(2,1)S(1)}, bf16[128,512]{1,0:T(8,128)(2,1)S(1)}, bf16[128,512]{1,0:T(8,12...) custom-call(bf16[8,256,128]{2,1,0:T(8,128)(2,1)S(1)} %get-tuple-element.73.x.refs_0_, ...), custom_call_target="tpu_custom_call" | custom-call | flops 4000 | bytes 256 | tf_op jit(solution)/shard_map/pallas_call | solution.py:27
  37.6 0.1 collective-permute-start.9
  37.6 0.8 %shard_map.150.grads = f32[2,256,128]{2,1,0:T(8,128)S(1)} custom-call(bf16[256,128]{1,0:T(8,128)(2,1)S(1)} %get-tuple-element.74.b.refs_4_, bf16[256,128]{1,0:T(8,128)(2,1)S(1)} %get-tuple-element.75.c.refs_5_, bf16[4,256,128]{2,1,0:T(8,128)(2,1)S(1)} %get-tuple-element.89.refs_7_.refs_0_, bf16[4,256,128]{2,1,0:T(8,128)(2,1)S(1)} %get-tuple-element.109.refs_7_.refs_1_, ...), custom_call_target="tpu_custom_call" | custom-call | flops 4000 | bytes 256 | tf_op jit(solution)/shard_map/pallas_call | solution.py:27
  38.5 0.3 collective-permute-done.9.refs_1_
  38.8 1.6 %collective-permute-start.10 = (f32[2,128,128]{2,1,0:T(8,128)S(1)}, f32[2,128,128]{2,1,0:T(8,128)S(1)}, u32[]{:S(2)}, u32[]{:S(2)}) collective-permute-start(f32[2,128,128]{2,1,0:T(8,128)S(1)} %get-tuple-element.135), channel_id=1, source_target_pairs={{0,4},{4,0},{1,5},{5,1},{2,6},{6,2},{3,7},{7,3},{8,12},{12,8},{9,1... | collective-permute-start | bytes 393224 | tf_op jit(solution)/shard_map/ppermute | solution.py:431
  40.4 2.1 %collective-permute-start.11 = (f32[8,128]{1,0:T(8,128)S(1)}, f32[8,128]{1,0:T(8,128)S(1)}, u32[]{:S(2)}, u32[]{:S(2)}) collective-permute-start(f32[8,128]{1,0:T(8,128)S(1)} %get-tuple-element.134.refs_1_), channel_id=1, source_target_pairs={{0,16},{8,24},{16,0},{24,8},{1,17},{9,25},{17,1},{25,9},{2,18},{10... | collective-permute-start | bytes 12296 | tf_op jit(solution)/shard_map/ppermute | solution.py:417
  42.5 2.5 %collective-permute-done.11.refs_3_ = f32[8,128]{1,0:T(8,128)S(1)} collective-permute-done((f32[8,128]{1,0:T(8,128)S(1)}, f32[8,128]{1,0:T(8,128)S(1)}, u32[]{:S(2)}, u32[]{:S(2)}) %collective-permute-start.11) | collective-permute-done | bytes 4128 | tf_op jit(solution)/shard_map/ppermute | solution.py:417
  44.9 0.0 collective-permute-done.10.refs_2_
  45.0 1.6 %collective-permute-start.12 = (f32[8,128]{1,0:T(8,128)S(1)}, f32[8,128]{1,0:T(8,128)S(1)}, u32[]{:S(2)}, u32[]{:S(2)}) collective-permute-start(f32[8,128]{1,0:T(8,128)S(1)} %get-tuple-element.138), channel_id=1, source_target_pairs={{0,8},{8,0},{16,24},{24,16},{1,9},{9,1},{17,25},{25,17},{2,10},{10... | collective-permute-start | bytes 12296 | tf_op jit(solution)/shard_map/ppermute | solution.py:417
  46.5 1.4 %shard_map.149 = (bf16[8,256,128]{2,1,0:T(8,128)(2,1)}, f32[8,256]{1,0:T(8,128)}) custom-call(bf16[4,256,128]{2,1,0:T(8,128)(2,1)S(1)} %get-tuple-element.108.refs_0_, bf16[4,256,128]{2,1,0:T(8,128)(2,1)S(1)} %get-tuple-element.123.refs_1_, f32[2,256,128]{2,1,0:T(8,128)S(1)} %get-tuple-element.83.refs_2_, ...), custom_call_target="tpu_custom_call" | custom-call | flops 1000 | bytes 256 | tf_op jit(solution)/shard_map/pallas_call | solution.py:27
  48.0 0.7 %collective-permute-done.12 = f32[8,128]{1,0:T(8,128)S(1)} collective-permute-done((f32[8,128]{1,0:T(8,128)S(1)}, f32[8,128]{1,0:T(8,128)S(1)}, u32[]{:S(2)}, u32[]{:S(2)}) %collective-permute-start.12) | collective-permute-done | bytes 4128 | tf_op jit(solution)/shard_map/ppermute | solution.py:417
  48.6 1.5 %collective-permute-start.13 = (f32[8,128]{1,0:T(8,128)S(1)}, f32[8,128]{1,0:T(8,128)S(1)}, u32[]{:S(2)}, u32[]{:S(2)}) collective-permute-start(f32[8,128]{1,0:T(8,128)S(1)} %add.6), channel_id=1, source_target_pairs={{0,2},{1,3},{2,0},{3,1},{4,6},{5,7},{6,4},{7,5},{8,10},{9,11},{10,... | collective-permute-start | bytes 12296 | tf_op jit(solution)/shard_map/ppermute | solution.py:417
  50.1 0.7 %fusion.1 = (f32[1,128,128]{2,1,0:T(8,128)}, f32[1,128,128]{2,1,0:T(8,128)}) fusion(f32[2,128,128]{2,1,0:T(8,128)S(1)} %get-tuple-element.136), kind=kLoop, calls=%fused_computation.5 | loop fusion | bytes 262144 | tf_op jit(solution)/shard_map/slice | solution.py:448
  50.8 1.5 %collective-permute-done.13 = f32[8,128]{1,0:T(8,128)S(1)} collective-permute-done((f32[8,128]{1,0:T(8,128)S(1)}, f32[8,128]{1,0:T(8,128)S(1)}, u32[]{:S(2)}, u32[]{:S(2)}) %collective-permute-start.13) | collective-permute-done | bytes 4128 | tf_op jit(solution)/shard_map/ppermute | solution.py:417
  52.2 0.5 slice_bitcast_fusion
  (9 shorter events, 0.1 us)
Async XLA Ops:
  2.1 7.8 %collective-permute-start = (f32[272,128]{1,0:T(8,128)S(1)}, f32[272,128]{1,0:T(8,128)S(1)}, u32[]{:S(2)}, u32[]{:S(2)}) collective-permute-start(f32[272,128]{1,0:T(8,128)S(1)} %get-tuple-element.96), channel_id=1, source_target_pairs={{0,1},{1,0},{2,3},{3,2},{8,24},{9,25},{10,26},{11,27},{16,8},{17,9... | collective-permute-start | bytes 417800 | tf_op jit(solution)/shard_map/ppermute | solution.py:327
  4.0 14.0 %collective-permute-start.1 = (f32[4,128,128]{2,1,0:T(8,128)S(1)}, f32[4,128,128]{2,1,0:T(8,128)S(1)}, u32[]{:S(2)}, u32[]{:S(2)}) collective-permute-start(f32[4,128,128]{2,1,0:T(8,128)S(1)} %get-tuple-element.98), channel_id=1, source_target_pairs={{0,8},{1,9},{2,10},{3,11},{8,0},{9,1},{10,2},{11,3},{16,24},{17,25... | collective-permute-start | bytes 786440 | tf_op jit(solution)/shard_map/ppermute | solution.py:327
  9.9 8.1 %collective-permute-start.2 = (f32[272,128]{1,0:T(8,128)S(1)}, f32[272,128]{1,0:T(8,128)S(1)}, u32[]{:S(2)}, u32[]{:S(2)}) collective-permute-start(f32[272,128]{1,0:T(8,128)S(1)} %collective-permute-done.got), channel_id=1, source_target_pairs={{0,1},{1,0},{2,3},{3,2},{8,16},{9,17},{10,18},{11,19},{16,8},{17,9... | collective-permute-start | bytes 417800 | tf_op jit(solution)/shard_map/ppermute | solution.py:327
  10.0 8.7 %collective-permute-start.6 = (f32[2,128,128]{2,1,0:T(8,128)S(1)}, f32[2,128,128]{2,1,0:T(8,128)S(1)}, u32[]{:S(2)}, u32[]{:S(2)}) collective-permute-start(f32[2,128,128]{2,1,0:T(8,128)S(1)} %get-tuple-element.140), channel_id=1, source_target_pairs={{0,8},{24,16},{1,9},{25,17},{2,10},{26,18},{3,11},{27,19},{4,12},{... | collective-permute-start | bytes 393224 | tf_op jit(solution)/shard_map/ppermute | solution.py:390
  15.2 4.9 %collective-permute-start.5 = (f32[2,128,128]{2,1,0:T(8,128)S(1)}, f32[2,128,128]{2,1,0:T(8,128)S(1)}, u32[]{:S(2)}, u32[]{:S(2)}) collective-permute-start(f32[2,128,128]{2,1,0:T(8,128)S(1)} %get-tuple-element.139), channel_id=1, source_target_pairs={{0,8},{24,16},{1,9},{25,17},{2,10},{26,18},{3,11},{27,19},{4,12},{... | collective-permute-start | bytes 393224 | tf_op jit(solution)/shard_map/ppermute | solution.py:390
  18.4 3.3 %collective-permute-start.3 = (f32[4,128,128]{2,1,0:T(8,128)S(1)}, f32[4,128,128]{2,1,0:T(8,128)S(1)}, u32[]{:S(2)}, u32[]{:S(2)}) collective-permute-start(f32[4,128,128]{2,1,0:T(8,128)S(1)} %get-tuple-element.102), channel_id=1, source_target_pairs={{0,1},{1,0},{2,3},{3,2},{8,16},{9,17},{10,18},{11,19},{16,8},{17,9... | collective-permute-start | bytes 786440 | tf_op jit(solution)/shard_map/ppermute | solution.py:327
  21.6 4.3 %collective-permute-start.7 = (f32[4,128,128]{2,1,0:T(8,128)S(1)}, f32[4,128,128]{2,1,0:T(8,128)S(1)}, u32[]{:S(2)}, u32[]{:S(2)}) collective-permute-start(f32[4,128,128]{2,1,0:T(8,128)S(1)} %get-tuple-element.115), channel_id=1, source_target_pairs={{0,1},{1,0},{2,3},{3,2},{8,16},{9,17},{10,18},{11,19},{16,8},{17,9... | collective-permute-start | bytes 786440 | tf_op jit(solution)/shard_map/ppermute | solution.py:327
  22.1 9.8 %collective-permute-start.4 = (f32[4,128,128]{2,1,0:T(8,128)S(1)}, f32[4,128,128]{2,1,0:T(8,128)S(1)}, u32[]{:S(2)}, u32[]{:S(2)}) collective-permute-start(f32[4,128,128]{2,1,0:T(8,128)S(1)} %get-tuple-element.105), channel_id=1, source_target_pairs={{0,8},{1,9},{2,10},{3,11},{8,0},{9,1},{10,2},{11,3},{16,24},{17,25... | collective-permute-start | bytes 786440 | tf_op jit(solution)/shard_map/ppermute | solution.py:327
  26.3 10.2 %collective-permute-start.8 = (f32[4,128,128]{2,1,0:T(8,128)S(1)}, f32[4,128,128]{2,1,0:T(8,128)S(1)}, u32[]{:S(2)}, u32[]{:S(2)}) collective-permute-start(f32[4,128,128]{2,1,0:T(8,128)S(1)} %get-tuple-element.118), channel_id=1, source_target_pairs={{0,8},{1,9},{2,10},{3,11},{8,0},{9,1},{10,2},{11,3},{16,24},{17,25... | collective-permute-start | bytes 786440 | tf_op jit(solution)/shard_map/ppermute | solution.py:327
  37.6 1.2 %collective-permute-start.9 = (f32[8,128]{1,0:T(8,128)S(1)}, f32[8,128]{1,0:T(8,128)S(1)}, u32[]{:S(2)}, u32[]{:S(2)}) collective-permute-start(f32[8,128]{1,0:T(8,128)S(1)} %get-tuple-element.132.refs_0_), channel_id=1, source_target_pairs={{0,1},{1,0},{2,3},{3,2},{4,5},{5,4},{6,7},{7,6},{8,9},{9,8},{10,11... | collective-permute-start | bytes 12296 | tf_op jit(solution)/shard_map/ppermute | solution.py:417
  38.8 6.1 %collective-permute-start.10 = (f32[2,128,128]{2,1,0:T(8,128)S(1)}, f32[2,128,128]{2,1,0:T(8,128)S(1)}, u32[]{:S(2)}, u32[]{:S(2)}) collective-permute-start(f32[2,128,128]{2,1,0:T(8,128)S(1)} %get-tuple-element.135), channel_id=1, source_target_pairs={{0,4},{4,0},{1,5},{5,1},{2,6},{6,2},{3,7},{7,3},{8,12},{12,8},{9,1... | collective-permute-start | bytes 393224 | tf_op jit(solution)/shard_map/ppermute | solution.py:431
  40.4 4.5 %collective-permute-start.11 = (f32[8,128]{1,0:T(8,128)S(1)}, f32[8,128]{1,0:T(8,128)S(1)}, u32[]{:S(2)}, u32[]{:S(2)}) collective-permute-start(f32[8,128]{1,0:T(8,128)S(1)} %get-tuple-element.134.refs_1_), channel_id=1, source_target_pairs={{0,16},{8,24},{16,0},{24,8},{1,17},{9,25},{17,1},{25,9},{2,18},{10... | collective-permute-start | bytes 12296 | tf_op jit(solution)/shard_map/ppermute | solution.py:417
  45.0 3.7 %collective-permute-start.12 = (f32[8,128]{1,0:T(8,128)S(1)}, f32[8,128]{1,0:T(8,128)S(1)}, u32[]{:S(2)}, u32[]{:S(2)}) collective-permute-start(f32[8,128]{1,0:T(8,128)S(1)} %get-tuple-element.138), channel_id=1, source_target_pairs={{0,8},{8,0},{16,24},{24,16},{1,9},{9,1},{17,25},{25,17},{2,10},{10... | collective-permute-start | bytes 12296 | tf_op jit(solution)/shard_map/ppermute | solution.py:417
  48.6 3.6 %collective-permute-start.13 = (f32[8,128]{1,0:T(8,128)S(1)}, f32[8,128]{1,0:T(8,128)S(1)}, u32[]{:S(2)}, u32[]{:S(2)}) collective-permute-start(f32[8,128]{1,0:T(8,128)S(1)} %add.6), channel_id=1, source_target_pairs={{0,2},{1,3},{2,0},{3,1},{4,6},{5,7},{6,4},{7,5},{8,10},{9,11},{10,... | collective-permute-start | bytes 12296 | tf_op jit(solution)/shard_map/ppermute | solution.py:417
